TPU v7x, 32 devices: a whole 2x2x4 slice. The times are simulated.
32 devices in a mesh: section: 2 (over x), dp: 4 (over y, core), seq: 4 (over z).
Axes of the slice: x: 2, y: 2, z: 4, core: 2. Of those that a mesh axis runs over, the one named last changes fastest.
Arguments:
- tokens: bfloat16 [16, 1024, 1536], P('dp', 'seq'), may hold values from -6 to 6
- cotangent: bfloat16 [16, 1024, 1536], P('dp', 'seq'), may hold values from -6 to 6
- in_proj: bfloat16 [2, 1536, 6448], P('section', ('dp', 'seq')), may hold values from -0.15625 to 0.15625
- out_proj: bfloat16 [2, 3072, 1536], P('section', ('dp', 'seq')), may hold values from -0.109375 to 0.109375
- conv_weight: bfloat16 [2, 4, 3328], P('section', None, ('dp', 'seq')), may hold values from -3 to 3
- conv_bias: bfloat16 [2, 3328], P('section', ('dp', 'seq')), may hold values from -3 to 3
- norm_gain: bfloat16 [2, 1536], P('section', ('dp', 'seq')), may hold values from 0.5 to 1.5
- gate_gain: bfloat16 [2, 3072], P('section', ('dp', 'seq')), may hold values from 0.5 to 1.5
- step_bias: float32 [2, 48], P('section'), may hold values from -7 to -2
- log_decay: float32 [2, 48], P('section'), may hold values from -1 to 2
- skip_gain: float32 [2, 48], P('section'), may hold values from 0.5 to 1.5
Outputs:
- activations: bfloat16 [2, 16, 1024, 1536], P('section', 'dp', 'seq')
- input_grads: float32 [2, 16, 1024, 1536], P('section', 'dp', 'seq')
- grad_in_proj: float32 [2, 1536, 6448], P('section', ('dp', 'seq'))
- grad_out_proj: float32 [2, 3072, 1536], P('section', ('dp', 'seq'))
- grad_conv_weight: float32 [2, 4, 3328], P('section', None, ('dp', 'seq'))
- grad_conv_bias: float32 [2, 3328], P('section', ('dp', 'seq'))
- grad_norm_gain: float32 [2, 1536], P('section', ('dp', 'seq'))
- grad_gate_gain: float32 [2, 3072], P('section', ('dp', 'seq'))
- grad_step_bias: float32 [2, 48], P('section')
- grad_log_decay: float32 [2, 48], P('section')
- grad_skip_gain: float32 [2, 48], P('section')
All inputs are finite; a program needn't handle non-finite values.
Results may differ from a plain program's by a relative error of at most 0.012.
The roundings to bfloat16 on the way count: a program that leaves them out, or rounds other values in their place, can miss the bound.
Values may be sent and summed in bfloat16 or wider, within the bound.
No kernel may reach another device: no remote copies, remote signals or barrier semaphores. Data moves between devices by JAX's collectives and lax.ppermute only.
A program may use at most 448 MiB of HBM per device.

v0:
```python
import jax
import jax.numpy as jnp
from jax import lax
from jax.sharding import PartitionSpec as P

HEADS = 48
HEAD_DIM = 64
STATE = 128
CONV = 4
MICRO = 4
DI = 3072


eps_norm = 1e-05
highest = lax.Precision.HIGHEST


def from_behind(block, axis, distance):
    devices = range(lax.axis_size(axis))
    route = [(i - distance, i) for i in devices if i - distance in devices]
    return lax.ppermute(block, axis, route)


def prefix(value, axis, combine, identity, reverse):
    peers, position = (lax.axis_size(axis), lax.axis_index(axis))
    everything = jax.tree.map(lambda part: lax.all_gather(part, axis), value)
    start = jax.tree.map(
        lambda part, zero: jnp.broadcast_to(jnp.asarray(zero, part.dtype), part.shape),
        value,
        identity,
    )

    def hop(k, before):
        at = peers - 1 - k if reverse else k
        reached = at > position if reverse else at < position
        new = combine(before, jax.tree.map(lambda part: part[at], everything))
        return jax.tree.map(lambda a, b: jnp.where(reached, a, b), new, before)

    return lax.fori_loop(0, peers, hop, start)


def rms_scale(hidden, gains):
    return hidden * lax.rsqrt(jnp.mean(hidden * hidden, axis=-1, keepdims=True) + eps_norm) * gains


def conv_act(padded, conv_taps, conv_shift):
    length = padded.shape[1] - conv_taps.shape[0] + 1
    summed = conv_shift
    for offset in range(conv_taps.shape[0]):
        summed = summed + padded[:, offset : offset + length] * conv_taps[offset]
    return jax.nn.silu(summed)


def ssd_inputs(activated, step_raw, step_bias, log_decay):
    values = activated[..., :DI].reshape(activated.shape[:2] + (HEADS, HEAD_DIM))
    b_rows = activated[..., DI : DI + STATE]
    c_rows = activated[..., DI + STATE :]
    step_size = jax.nn.softplus(step_raw + step_bias)
    cumulative = jnp.cumsum(step_size * -jnp.exp(log_decay), axis=1)
    return (values, b_rows, c_rows, step_size, cumulative)


def block_states(activated, step_raw, step_bias, log_decay):
    values, b_rows, c_rows, step_size, cumulative = ssd_inputs(
        activated, step_raw, step_bias, log_decay
    )
    totals = cumulative[:, -1]
    weights_in = jnp.exp(totals[:, None] - cumulative) * step_size
    fresh_state = jnp.einsum("sqh,sqhp,sqn->shpn", weights_in, values, b_rows, precision=highest)
    return (jnp.exp(totals), fresh_state)


def block_output(
    activated,
    step_raw,
    gate_part,
    step_bias,
    log_decay,
    skip_gain,
    gain_gate,
    carry_state,
    narrow=False,
):
    values, b_rows, c_rows, step_size, cumulative = ssd_inputs(
        activated, step_raw, step_bias, log_decay
    )
    length = cumulative.shape[1]
    causal = jnp.arange(length)[:, None] >= jnp.arange(length)[None, :]
    cum_heads = jnp.swapaxes(cumulative, 1, 2)
    segment = jnp.where(causal, cum_heads[..., :, None] - cum_heads[..., None, :], -1e30)
    if narrow:
        scores = jnp.einsum(
            "sqn,skn->sqk",
            c_rows.astype(jnp.bfloat16),
            b_rows.astype(jnp.bfloat16),
            preferred_element_type=jnp.float32,
        )
    else:
        scores = jnp.einsum("sqn,skn->sqk", c_rows, b_rows, precision=highest)
    mixing = jnp.exp(segment) * scores[:, None] * jnp.swapaxes(step_size, 1, 2)[:, :, None, :]
    within = jnp.einsum("shqk,skhp->sqhp", mixing, values, precision=highest)
    carried = (
        jnp.einsum("sqn,shpn->sqhp", c_rows, carry_state, precision=highest)
        * jnp.exp(cumulative)[..., None]
    )
    ssm_out = (within + carried + skip_gain[:, None] * values).reshape(gate_part.shape)
    return rms_scale(ssm_out * jax.nn.silu(gate_part), gain_gate)


def chain_combine(earlier, later):
    return (earlier[0] * later[0], later[0][..., None, None] * earlier[1] + later[1])


def forward_layer(hidden, matrices, head_params):
    in_w, out_w, conv_taps, conv_shift, gain_in, gain_gate = matrices
    step_bias, log_decay, skip_gain = head_params
    normed = rms_scale(hidden, gain_in.astype(jnp.float32)).astype(jnp.bfloat16)
    projected = jnp.einsum("sqd,de->sqe", normed, in_w, preferred_element_type=jnp.float32)
    gate_part = projected[..., :DI]
    conv_in = projected[..., DI : 2 * DI + 2 * STATE].astype(jnp.bfloat16)
    step_raw = projected[..., 2 * DI + 2 * STATE :]
    rim_rows = from_behind(conv_in[:, conv_in.shape[1] - CONV + 1 :], "seq", 1)
    padded = jnp.concatenate([rim_rows, conv_in], axis=1).astype(jnp.float32)
    activated = conv_act(padded, conv_taps.astype(jnp.float32), conv_shift.astype(jnp.float32))
    activated = lax.optimization_barrier(activated.astype(jnp.bfloat16)).astype(jnp.float32)
    decay_total, fresh_state = block_states(activated, step_raw, step_bias, log_decay)
    carry_state = prefix(
        (decay_total, fresh_state),
        "seq",
        chain_combine,
        (jnp.ones_like(decay_total), jnp.zeros_like(fresh_state)),
        False,
    )[1]
    gate_out = block_output(
        activated,
        step_raw,
        gate_part,
        step_bias,
        log_decay,
        skip_gain,
        gain_gate.astype(jnp.float32),
        carry_state,
        True,
    ).astype(jnp.bfloat16)
    branch = jnp.einsum("sqe,ed->sqd", gate_out, out_w, preferred_element_type=jnp.float32)
    kept_values = (
        normed,
        gate_part,
        step_raw,
        padded,
        activated,
        decay_total,
        carry_state,
        gate_out,
    )
    return (hidden + branch, (rim_rows, carry_state), kept_values)


def backward_layer(hidden, grad_out, matrices, head_params):
    unused_out, context_now, kept_values = forward_layer(hidden, matrices, head_params)
    normed, gate_part, step_raw, padded, activated, decay_total, carry_state, gate_out = kept_values
    in_w, out_w, conv_taps, conv_shift, gain_in, gain_gate = matrices
    step_bias, log_decay, skip_gain = head_params
    grad_low = grad_out.astype(jnp.bfloat16)
    grad_out_w = jnp.einsum("sqe,sqd->ed", gate_out, grad_low, preferred_element_type=jnp.float32)
    grad_gate_out = jnp.einsum("sqd,ed->sqe", grad_low, out_w, preferred_element_type=jnp.float32)
    unused_mix, pull_output = jax.vjp(
        block_output,
        activated,
        step_raw,
        gate_part,
        step_bias,
        log_decay,
        skip_gain,
        gain_gate.astype(jnp.float32),
        carry_state,
    )
    (
        grad_act_out,
        grad_step_out,
        grad_gate,
        grad_bias_out,
        grad_decay_out,
        grad_skip,
        grad_gain_gate,
        grad_carry,
    ) = pull_output(grad_gate_out)
    chain_grad = prefix(
        (decay_total, grad_carry),
        "seq",
        chain_combine,
        (jnp.ones_like(decay_total), jnp.zeros_like(grad_carry)),
        True,
    )[1]
    grad_total = jnp.sum(carry_state * chain_grad, axis=(2, 3))
    unused_states, pull_states = jax.vjp(block_states, activated, step_raw, step_bias, log_decay)
    grad_act_state, grad_step_state, grad_bias_state, grad_decay_state = pull_states(
        (grad_total, chain_grad)
    )
    unused_conv, pull_conv = jax.vjp(
        conv_act, padded, conv_taps.astype(jnp.float32), conv_shift.astype(jnp.float32)
    )
    grad_padded, grad_taps, grad_shift = pull_conv(grad_act_out + grad_act_state)
    edge_rows = CONV - 1
    returned = from_behind(grad_padded[:, :edge_rows], "seq", -1)
    grad_conv = grad_padded[:, edge_rows:]
    split_at = grad_conv.shape[1] - edge_rows
    grad_conv = jnp.concatenate(
        [grad_conv[:, :split_at], grad_conv[:, split_at:] + returned], axis=1
    )
    grad_proj = jnp.concatenate(
        [grad_gate, grad_conv, grad_step_out + grad_step_state], axis=-1
    ).astype(jnp.bfloat16)
    grad_normed = jnp.einsum("sqe,de->sqd", grad_proj, in_w, preferred_element_type=jnp.float32)
    unused_norm, pull_norm = jax.vjp(rms_scale, hidden, gain_in.astype(jnp.float32))
    grad_hidden, grad_gain_in = pull_norm(grad_normed)
    matrix_grads = (grad_out_w, grad_taps, grad_shift, grad_gain_in, grad_gain_gate)
    head_grads = (grad_bias_out + grad_bias_state, grad_decay_out + grad_decay_state, grad_skip)
    return (grad_out + grad_hidden, normed, grad_proj, matrix_grads, head_grads)


def make_term(normed_rows, proj_rows):
    return jnp.einsum("td,te->de", normed_rows, proj_rows, preferred_element_type=jnp.float32)


def shards(
    tokens,
    cotangent,
    in_proj,
    out_proj,
    conv_weight,
    conv_bias,
    norm_gain,
    gate_gain,
    step_bias,
    log_decay,
    skip_gain,
):
    first_section = lax.axis_index("section") == 0
    gathered = (
        lax.all_gather(in_proj, ("dp", "seq"), axis=1, tiled=True),
        lax.all_gather(out_proj, ("dp", "seq"), axis=1, tiled=True),
        lax.all_gather(conv_weight, ("dp", "seq"), axis=2, tiled=True),
        lax.all_gather(conv_bias, ("dp", "seq"), axis=1, tiled=True),
        lax.all_gather(norm_gain, ("dp", "seq"), axis=1, tiled=True),
        lax.all_gather(gate_gain, ("dp", "seq"), axis=1, tiled=True),
    )
    matrices = tuple((piece[0] for piece in gathered))
    head_params = (step_bias[0], log_decay[0], skip_gain[0])
    group_rows = tokens.shape[0] // MICRO
    received = jnp.zeros((group_rows,) + tokens.shape[1:], jnp.bfloat16)
    layer_inputs, contexts, layer_outputs = ([], [], [])
    for tick_index in range(MICRO + 1):
        row_start = min(tick_index, MICRO - 1) * group_rows
        layer_in = jnp.where(
            first_section, tokens[row_start : row_start + group_rows], received
        ).astype(jnp.float32)
        new_hidden, context_now, kept_values = forward_layer(layer_in, matrices, head_params)
        layer_out = new_hidden.astype(jnp.bfloat16)
        layer_inputs.append(layer_in)
        contexts.append(context_now)
        layer_outputs.append(layer_out)
        if tick_index < MICRO:
            received = from_behind(layer_out, "section", 1)
    activations = jnp.concatenate(
        [
            jnp.where(first_section, layer_outputs[micro_index], layer_outputs[micro_index + 1])
            for micro_index in range(MICRO)
        ],
        axis=0,
    )[None]
    regathered = (
        lax.all_gather(in_proj, ("dp", "seq"), axis=1, tiled=True),
        lax.all_gather(out_proj, ("dp", "seq"), axis=1, tiled=True),
        lax.all_gather(conv_weight, ("dp", "seq"), axis=2, tiled=True),
        lax.all_gather(conv_bias, ("dp", "seq"), axis=1, tiled=True),
        lax.all_gather(norm_gain, ("dp", "seq"), axis=1, tiled=True),
        lax.all_gather(gate_gain, ("dp", "seq"), axis=1, tiled=True),
    )
    back_matrices = tuple((piece[0] for piece in regathered))
    grad_received = jnp.zeros((group_rows,) + tokens.shape[1:], jnp.bfloat16)
    normed_list, proj_list, grad_inputs = ([], [], [])
    matrix_totals = None
    head_totals = None
    for tick_index in range(MICRO + 1):
        forward_tick = MICRO - tick_index
        cot_start = max(MICRO - 1 - tick_index, 0) * group_rows
        valid = jnp.where(first_section, float(tick_index >= 1), float(tick_index <= MICRO - 1))
        grad_out = (
            jnp.where(
                first_section, grad_received, cotangent[cot_start : cot_start + group_rows]
            ).astype(jnp.float32)
            * valid
        )
        grad_in, normed, grad_proj, matrix_grads, head_grads = backward_layer(
            layer_inputs[forward_tick], grad_out, back_matrices, head_params
        )
        if tick_index == 0:
            matrix_totals, head_totals = (matrix_grads, head_grads)
        else:
            matrix_totals = jax.tree.map(jnp.add, matrix_totals, matrix_grads)
            head_totals = jax.tree.map(jnp.add, head_totals, head_grads)
        normed_list.append(normed)
        proj_list.append(grad_proj)
        grad_inputs.append(grad_in)
        if tick_index < MICRO:
            grad_received = from_behind(grad_in.astype(jnp.bfloat16), "section", -1)
    input_grads = jnp.concatenate(
        [
            jnp.where(
                first_section,
                grad_inputs[MICRO - micro_index],
                grad_inputs[MICRO - 1 - micro_index],
            )
            for micro_index in range(MICRO)
        ],
        axis=0,
    )[None]
    normed_all = jnp.concatenate(normed_list, axis=0).reshape(-1, normed_list[0].shape[-1])
    proj_all = jnp.concatenate(proj_list, axis=0).reshape(-1, proj_list[0].shape[-1])
    grad_in_proj = lax.psum_scatter(
        make_term(normed_all, proj_all), ("dp", "seq"), scatter_dimension=0, tiled=True
    )[None]
    grad_out_proj, grad_conv_weight, grad_conv_bias, grad_norm_gain, grad_gate_gain = (
        lax.psum_scatter(matrix_totals[0][None], ("dp", "seq"), scatter_dimension=1, tiled=True),
        lax.psum_scatter(matrix_totals[1][None], ("dp", "seq"), scatter_dimension=2, tiled=True),
        lax.psum_scatter(matrix_totals[2][None], ("dp", "seq"), scatter_dimension=1, tiled=True),
        lax.psum_scatter(matrix_totals[3][None], ("dp", "seq"), scatter_dimension=1, tiled=True),
        lax.psum_scatter(matrix_totals[4][None], ("dp", "seq"), scatter_dimension=1, tiled=True),
    )
    grad_step_bias, grad_log_decay, grad_skip_gain = lax.psum(
        (head_totals[0], head_totals[1], head_totals[2]), ("dp", "seq")
    )
    return (
        activations,
        input_grads,
        grad_in_proj,
        grad_out_proj,
        grad_conv_weight,
        grad_conv_bias,
        grad_norm_gain,
        grad_gate_gain,
        grad_step_bias[None],
        grad_log_decay[None],
        grad_skip_gain[None],
    )


def solution(mesh):
    placed = (
        P("dp", "seq", None),
        P("dp", "seq", None),
        P("section", ("dp", "seq"), None),
        P("section", ("dp", "seq"), None),
        P("section", None, ("dp", "seq")),
        P("section", ("dp", "seq")),
        P("section", ("dp", "seq")),
        P("section", ("dp", "seq")),
        P("section", None),
        P("section", None),
        P("section", None),
    )
    return jax.shard_map(
        shards,
        mesh=mesh,
        in_specs=placed,
        out_specs=(
            P("section", "dp", "seq", None),
            P("section", "dp", "seq", None),
            P("section", ("dp", "seq"), None),
            P("section", ("dp", "seq"), None),
            P("section", None, ("dp", "seq")),
            P("section", ("dp", "seq")),
            P("section", ("dp", "seq")),
            P("section", ("dp", "seq")),
            P("section", None),
            P("section", None),
            P("section", None),
        ),
        check_vma=False,
    )
```

profile of v0, /device:TPU:0, one launch (start us, length us, event | category | flops | bytes accessed | tf_op | source)
XLA Modules:
  0.0 3330.2 jit_solution(9807195000599721390)
XLA Ops:
  13.9 64.9 %all-reduce.74 = (bf16[1536]{0:T(1024)(128)(2,1)S(1)}, bf16[3328]{0:T(1024)(128)(2,1)S(1)}, bf16[3072]{0:T(1024)(128)(2,1)S(1)}) all-reduce(bf16[1536]{0:T(1024)(128)(2,1)S(1)} %dynamic-update-slice.1, bf16[3328]{0:T(1024)(128)(2,1)S(1)} %dynamic-update-slice, ...), channel_id=1, replica_groups=mesh['section'=2,'dp'=4,'seq'=4] {'dp','seq'}, use_global_device_ids=true, to_apply=%add.71 | all-reduce | flops 7936 | bytes 31744
  80.2 63.0 %all_gather.65 = bf16[1,4,3328]{1,0,2:T(2,128)(2,1)S(1)} all-gather(bf16[1,4,208]{1,0,2:T(2,128)(2,1)S(1)} %copy.1167), channel_id=1, replica_groups=mesh['section'=2,'dp'=4,'seq'=4] {'dp','seq'}, dimensions={2}, use_global_device_ids=true | all-gather | bytes 28288 | tf_op jit(solution)/shard_map/all_gather | solution.py:243
  147.0 69.0 %slice_reduce_fusion.3 = (f32[3328]{0:T(1024)S(1)}, f32[3328]{0:T(1024)S(1)}, f32[3328]{0:T(1024)S(1)}, f32[3328]{0:T(1024)S(1)}) fusion(f32[1,4,3328]{1,0,2:T(1,128)S(1)} %convert_element_type.373), kind=kLoop, calls=%fused_computation.518 | loop fusion | bytes 106496 | tf_op jit(solution)/shard_map/slice | solution.py:50
  269.1 93.6 %all-gather.27.cloned.1.call-done = f32[192,64,128]{2,1,0:T(8,128)} async-done(((f32[48,64,128]{2,1,0:T(8,128)}), f32[192,64,128]{2,1,0:T(8,128)}) %all-gather.27.cloned.1.call-update) | async-done | bytes 6291472 | tf_op jit(solution)/shard_map/all_gather | solution.py:26
  412.6 32.1 all-gather.25.cloned.1.call-done
  527.5 95.1 %all-gather.29.cloned.1.call-done = f32[192,64,128]{2,1,0:T(8,128)} async-done(((f32[48,64,128]{2,1,0:T(8,128)}), f32[192,64,128]{2,1,0:T(8,128)}) %all-gather.29.cloned.1.call-update) | async-done | bytes 6291472 | tf_op jit(solution)/shard_map/all_gather | solution.py:26
  751.2 95.7 %all-gather.31.cloned.1.call-done = f32[192,64,128]{2,1,0:T(8,128)} async-done(((f32[48,64,128]{2,1,0:T(8,128)}), f32[192,64,128]{2,1,0:T(8,128)}) %all-gather.31.cloned.1.call-update) | async-done | bytes 6291472 | tf_op jit(solution)/shard_map/all_gather | solution.py:26
  976.0 95.4 %all-gather.33.cloned.1.call-done = f32[192,64,128]{2,1,0:T(8,128)} async-done(((f32[48,64,128]{2,1,0:T(8,128)}), f32[192,64,128]{2,1,0:T(8,128)}) %all-gather.33.cloned.1.call-update) | async-done | bytes 6291472 | tf_op jit(solution)/shard_map/all_gather | solution.py:26
  1224.4 82.9 %all-gather.35.cloned.1.call-done = f32[192,64,128]{2,1,0:T(8,128)} async-done(((f32[48,64,128]{2,1,0:T(8,128)}), f32[192,64,128]{2,1,0:T(8,128)}) %all-gather.35.cloned.1.call-update) | async-done | bytes 6291472 | tf_op jit(solution)/shard_map/all_gather | solution.py:26
  1307.3 17.2 while.179
  1448.3 54.2 %all-gather.37.cloned.1.call-done = f32[192,64,128]{2,1,0:T(8,128)} async-done(((f32[48,64,128]{2,1,0:T(8,128)}), f32[192,64,128]{2,1,0:T(8,128)}) %all-gather.37.cloned.1.call-update) | async-done | bytes 6291472 | tf_op jit(solution)/shard_map/all_gather | solution.py:26
  1502.5 17.5 while.180
  1597.0 17.7 collective-permute-done.10
  1697.5 57.3 %all-gather.39.cloned.1.call-done = f32[192,64,128]{2,1,0:T(8,128)} async-done(((f32[48,64,128]{2,1,0:T(8,128)}), f32[192,64,128]{2,1,0:T(8,128)}) %all-gather.39.cloned.1.call-update) | async-done | bytes 6291472 | tf_op jit(solution)/shard_map/all_gather | solution.py:26
  1840.5 17.8 collective-permute-done.12
  1940.7 57.7 %all-gather.41.cloned.1.call-done = f32[192,64,128]{2,1,0:T(8,128)} async-done(((f32[48,64,128]{2,1,0:T(8,128)}), f32[192,64,128]{2,1,0:T(8,128)}) %all-gather.41.cloned.1.call-update) | async-done | bytes 6291472 | tf_op jit(solution)/shard_map/all_gather | solution.py:26
  2084.0 17.8 collective-permute-done.14
  2184.5 57.4 %all-gather.43.cloned.1.call-done = f32[192,64,128]{2,1,0:T(8,128)} async-done(((f32[48,64,128]{2,1,0:T(8,128)}), f32[192,64,128]{2,1,0:T(8,128)}) %all-gather.43.cloned.1.call-update) | async-done | bytes 6291472 | tf_op jit(solution)/shard_map/all_gather | solution.py:26
  2328.0 17.4 collective-permute-done.16
  2572.9 31.8 add_bitcast_fusion
  2625.4 35.0 %convolution_bitcast_fusion = f32[1536,6448]{1,0:T(8,128)} fusion(bf16[5,256,1536]{2,1,0:T(8,128)(2,1)S(1)} %fusion.527, bf16[5,256,6448]{2,1,0:T(8,128)(2,1)} %maximum_dynamic-update-slice_fusion), kind=kOutput, calls=%fused_computation.30 | convolution fusion | flops 25354567680 | bytes 60055552 | tf_op jit(solution)/shard_map/td,te->de/dot_general | solution.py:223
  2684.7 33.6 %all-reduce.73 = (f32[1,48]{1,0:T(1,128)}, f32[1,48]{1,0:T(1,128)}, f32[1,48]{1,0:T(1,128)}) all-reduce(f32[1,48]{1,0:T(1,128)S(1)} %add_bitcast_fusion.3, f32[1,48]{1,0:T(1,128)S(1)} %fusion.702, f32[1,48]{1,0:T(1,128)S(1)} %add_bitcast_fusion.2), channel_id=1, replica_groups=mesh['section'=2,'dp'=4,'seq'=4] {'dp','seq'}, use_global_device_ids=true, to_apply=%region_171.173 | all-reduce | flops 144 | bytes 1152 | tf_op jit(solution)/shard_map/psum | solution.py:331
  2735.7 196.9 %reduce-scatter.17.cloned.1.call-done = f32[1,192,1536]{2,1,0:T(8,128)} async-done(((f32[1,3072,1536]{2,1,0:T(8,128)}), f32[1,192,1536]{2,1,0:T(8,128)}) %reduce-scatter.17.cloned.1.call-update) | async-done | bytes 1179664 | tf_op jit(solution)/shard_map/reduce_scatter | solution.py:325
  2932.6 390.5 %reduce-scatter.15.cloned.1.call-done = f32[96,6448]{1,0:T(8,128)} async-done(((f32[1536,6448]{1,0:T(8,128)}), f32[96,6448]{1,0:T(8,128)}) %reduce-scatter.15.cloned.1.call-update) | async-done | bytes 2476048 | tf_op jit(solution)/shard_map/reduce_scatter | solution.py:321
  (1523 shorter events, 1704.1 us)
Async XLA Ops:
  7.2 209.0 %all-gather.23.cloned.1.call-start = ((), (), s32[]{:S(2)}) async-start(), calls=%async_computation.6 | async-start | bytes 21307392 | tf_op jit(solution)/shard_map/all_gather | solution.py:241
  7.9 354.8 %all-gather.27.cloned.1.call-start = ((), (), s32[]{:S(2)}) async-start(), calls=%async_computation.10 | async-start | bytes 7864320 | tf_op jit(solution)/shard_map/all_gather | solution.py:26
  248.8 195.9 %all-gather.25.cloned.1.call-start = ((), (), s32[]{:S(2)}) async-start(), calls=%async_computation.7 | async-start | bytes 10027008 | tf_op jit(solution)/shard_map/all_gather | solution.py:242
  249.5 373.1 %all-gather.29.cloned.1.call-start = ((), (), s32[]{:S(2)}) async-start(), calls=%async_computation.11 | async-start | bytes 7864320 | tf_op jit(solution)/shard_map/all_gather | solution.py:26
  452.1 20.6 collective-permute-start.1
  508.0 338.9 %all-gather.31.cloned.1.call-start = ((), (), s32[]{:S(2)}) async-start(), calls=%async_computation.12 | async-start | bytes 7864320 | tf_op jit(solution)/shard_map/all_gather | solution.py:26
  676.6 20.4 collective-permute-start.3
  731.1 340.2 %all-gather.33.cloned.1.call-start = ((), (), s32[]{:S(2)}) async-start(), calls=%async_computation.13 | async-start | bytes 7864320 | tf_op jit(solution)/shard_map/all_gather | solution.py:26
  955.5 351.8 %all-gather.35.cloned.1.call-start = ((), (), s32[]{:S(2)}) async-start(), calls=%async_computation.14 | async-start | bytes 7864320 | tf_op jit(solution)/shard_map/all_gather | solution.py:26
  1192.0 310.5 %all-gather.37.cloned.1.call-start = ((), (), s32[]{:S(2)}) async-start(), calls=%async_computation.15 | async-start | bytes 7864320 | tf_op jit(solution)/shard_map/all_gather | solution.py:26
  1388.8 366.0 %all-gather.39.cloned.1.call-start = ((), (), s32[]{:S(2)}) async-start(), calls=%async_computation.16 | async-start | bytes 7864320 | tf_op jit(solution)/shard_map/all_gather | solution.py:26
  1593.0 21.7 collective-permute-start.10
  1639.8 358.6 %all-gather.41.cloned.1.call-start = ((), (), s32[]{:S(2)}) async-start(), calls=%async_computation.17 | async-start | bytes 7864320 | tf_op jit(solution)/shard_map/all_gather | solution.py:26
  1836.6 21.7 collective-permute-start.12
  1883.4 358.5 %all-gather.43.cloned.1.call-start = ((), (), s32[]{:S(2)}) async-start(), calls=%async_computation.18 | async-start | bytes 7864320 | tf_op jit(solution)/shard_map/all_gather | solution.py:26
  2080.1 21.7 collective-permute-start.14
  2127.0 358.6 %all-gather.45.cloned.1.call-start = ((), (), s32[]{:S(2)}) async-start(), calls=%async_computation.19 | async-start | bytes 7864320 | tf_op jit(solution)/shard_map/all_gather | solution.py:26
  2323.6 21.7 collective-permute-start.16
  2370.6 311.1 %reduce-scatter.25.cloned.1.call-start = ((), (), s32[]{:S(2)}) async-start(), calls=%async_computation.23 | async-start | bytes 1671168
  2477.2 241.2 %reduce-scatter.21.cloned.1.call-start = ((), (), s32[]{:S(2)}) async-start(), calls=%async_computation.21 | async-start | bytes 1810432
  2550.8 176.9 %reduce-scatter.23.cloned.1.call-start = ((), (), s32[]{:S(2)}) async-start(), calls=%async_computation.22 | async-start | bytes 835584
  2568.6 165.6 %reduce-scatter.19.cloned.1.call-start = ((), (), s32[]{:S(2)}) async-start(), calls=%async_computation.20 | async-start | bytes 1810432
  2572.8 359.8 %reduce-scatter.17.cloned.1.call-start = ((), (), s32[]{:S(2)}) async-start(), calls=%async_computation.9 | async-start | bytes 20054016 | tf_op jit(solution)/shard_map/reduce_scatter | solution.py:325
  2604.8 718.3 %reduce-scatter.15.cloned.1.call-start = ((), (), s32[]{:S(2)}) async-start(), calls=%async_computation.8 | async-start | bytes 42614784 | tf_op jit(solution)/shard_map/reduce_scatter | solution.py:321
  (412 other events, 6486.3 us)
Sparse Core Ops, SparseCore 0:
  9.6 149.6 all-gather.22
  248.9 113.7 all-gather.26
  365.0 79.6 all-gather.24
  508.1 114.4 all-gather.28
  731.2 115.6 all-gather.30
  955.7 115.6 all-gather.32
  1192.2 115.0 all-gather.34
  1388.9 113.5 all-gather.36
  1639.9 114.7 all-gather.38
  1883.5 114.8 all-gather.40
  2127.1 114.8 all-gather.42
  2370.7 114.7 all-gather.44
  2489.2 57.9 reduce-scatter.24
  2551.2 60.8 reduce-scatter.20
  2615.8 55.5 reduce-scatter.22
  2674.9 59.1 reduce-scatter.18
  2738.7 193.9 reduce-scatter.16
  2937.4 385.7 reduce-scatter.14
where the time goes:
time: 3350 us; the launch traced here: 3330 us
  waiting for transfers between devices  1460 us (44%)
  matrix products  738 us (22%)
  local copies, waits for them, and re-layouts  433 us (13%)
  other arithmetic  432 us (13%)
  blocking collectives  207 us (6%)
  starting transfers between devices  34.2 us (1%)
    all_gather x10, waiting for transfers between devices, prefix(): everything = jax.tree.map(lambda part: lax.all_gather(part, axis), value)  698 us
    reduce_scatter x1, waiting for transfers between devices, shards(): lax.psum_scatter(make_term(normed_all, proj_all), ('dp', 'seq'), scatter_...  391 us
    dot_general x20, matrix products, block_output(): within = jnp.einsum('shqk,skhp->sqhp', mixing, values, precision=highest)  268 us
    reduce_scatter x1, waiting for transfers between devices, shards(): lax.psum_scatter(matrix_totals[0][None], ('dp', 'seq'), scatter_dimension...  197 us
    ppermute x18, waiting for transfers between devices, from_behind(): return lax.ppermute(block, axis, route)  139 us
    select_n x40, other arithmetic, hop(): return jax.tree.map(lambda a, b: jnp.where(reached, a, b), new, before)  82.3 us
    dot_general x15, matrix products, block_states(): jnp.einsum('sqh,sqhp,sqn->shpn', weights_in, values, b_rows, precision=hi...  72.4 us
    unnamed x816, local copies, waits for them, and re-layouts  70.4 us
  transfers between devices with their start and end apart: 36, of which 22 were waited for; matrix products, arithmetic and copies ran while one was open for 23% of the time, Pallas kernels for 0%

commit v1 on v0

v1 whole, which is shorter than its diff:
```python
import jax
import jax.numpy as jnp
import numpy as np
from jax import lax
from jax.experimental import pallas as pl
from jax.experimental.pallas import tpu as pltpu
from jax.sharding import PartitionSpec as P

D = 1536
HEADS = 48
HEAD_DIM = 64
STATE = 128
CONV = 4
DI = 3072
BC = 2 * STATE
TAIL = BC + 128
GROUP = 8
WIDTH = GROUP * HEAD_DIM
GROUPS = HEADS // GROUP
OUT_TILE = 256
LANES = 128
EPS = 1e-05
f32 = jnp.float32
bf16 = jnp.bfloat16
VMEM_LIMIT = 56 * 2**20
NN = ((1,), (0,))
NT = ((1,), (1,))
TN = ((0,), (0,))


def dot(a, b, dims, precision=None):
    return lax.dot_general(a, b, (dims, ((), ())), preferred_element_type=f32, precision=precision)


def halves(value):
    top = value.astype(bf16)
    rest = (value - top.astype(f32)).astype(bf16)
    return jnp.concatenate([top, rest], axis=1)


def lower_mask(rows, cols):
    return lax.broadcasted_iota(jnp.int32, (rows, cols), 0) >= lax.broadcasted_iota(
        jnp.int32, (rows, cols), 1
    )


def sigmoid(v):
    return 1.0 / (1.0 + jnp.exp(-v))


def head_steps(step_raw, head_rows):
    biased = step_raw + head_rows[0:1]
    return jnp.maximum(biased, 0.0) + jnp.log1p(jnp.exp(-jnp.abs(biased)))


def running_sum(value):
    length = value.shape[0]
    ones = jnp.where(lower_mask(length, length), 1.0, 0.0).astype(f32)
    return dot(ones, value, NN, lax.Precision.HIGHEST)


def conv_pre(ext_ref, taps, length, width):
    summed = taps[CONV : CONV + 1]
    for j in range(CONV):
        summed = summed + ext_ref[5 + j : 5 + j + length, 0:width] * taps[j : j + 1]
    return summed


def fill_ext(ext_ref, tail, rows, length, width):
    ext_ref[0:8, 0:width] = tail[8:16].astype(f32)
    ext_ref[8 : 8 + length, 0:width] = rows


def fwd_body(
    h_ref, h_tile, ngain, wg, wc, wbc, wo, taps, taps_bc, head_rows, skip, gate_gain, spread, tail_in,
    tail_bc_in, state_in,
    normed_o, gate_o, cin_o, cin_bc_o, step_o, ssm_o, state_o, gout_o, r_o, branch_o, out_o,
    tail_o, tail_bc_o,
    u_s, ssq_s, k_s, c_s, bt_s, dt_s, ec_s, w_s, cum_s, cumt_s, ext_s,
):
    step = pl.program_id(0)
    length = h_ref.shape[0]
    half = length // 2

    @pl.when(step == 0)
    def _():
        h = h_ref[...].astype(f32)
        scale = lax.rsqrt(jnp.mean(h * h, axis=1, keepdims=True) + EPS)
        normed = (h * scale * ngain[...]).astype(bf16)
        normed_o[...] = normed
        projected = dot(normed, wbc[...], NN)
        step_raw = projected[:, BC:]
        step_o[...] = step_raw
        conv_in = projected[:, :BC].astype(bf16)
        cin_bc_o[...] = conv_in
        tail_bc_o[...] = conv_in[length - 16 :]
        fill_ext(ext_s, tail_bc_in[...], conv_in.astype(f32), length, BC)
        pre = conv_pre(ext_s, taps_bc[...], length, BC)
        act = (pre * sigmoid(pre)).astype(bf16)
        b_rows, c_rows = act[:, :STATE], act[:, STATE:]
        c_s[...] = c_rows
        bt_s[...] = b_rows.astype(f32).T.astype(bf16)
        k_s[...] = dot(c_rows, b_rows, NT)
        dt = head_steps(step_raw, head_rows[...])
        cum = running_sum(dt * head_rows[1:2])
        total = cum[length - 1 : length]
        dt_s[...] = halves(dt)
        ec_s[...] = halves(jnp.exp(cum))
        w_s[...] = halves(dt * jnp.exp(total - cum))
        for g in range(GROUPS):
            cum_s[g] = cum[:, g * GROUP : (g + 1) * GROUP]
        cumt_s[...] = cum.T
        ssq_s[...] = jnp.zeros_like(ssq_s)

    @pl.when(step < GROUPS)
    def _():
        normed = normed_o[...]
        gate = dot(normed, wg[...], NN)
        gate_o[...] = gate
        conv_in = dot(normed, wc[...], NN).astype(bf16)
        cin_o[...] = conv_in
        tail_o[...] = conv_in[length - 16 :]
        fill_ext(ext_s, tail_in[...], conv_in.astype(f32), length, WIDTH)
        pre = conv_pre(ext_s, taps[...], length, WIDTH)
        act = (pre * sigmoid(pre)).astype(bf16).astype(f32)
        where = spread[...]
        x_dt = (act * dot(dt_s[...], where, NN)).astype(bf16)
        x_w = (act * dot(w_s[...], where, NN)).astype(bf16)
        ec = dot(ec_s[...], where, NN)
        state = state_in[...]
        state_o[...] = ec[length - 1 : length] * state + dot(bt_s[...], x_w, NN)
        carried = dot(c_s[...], state.astype(bf16), NN) * ec
        cum = cum_s[step]
        cumt = cumt_s[pl.ds(pl.multiple_of(step * GROUP, GROUP), GROUP), :]
        k = k_s[...]
        mask = lower_mask(half, half)
        left_lane = lax.broadcasted_iota(jnp.int32, (length, LANES), 1) < HEAD_DIM
        pieces = []
        for pair in range(GROUP // 2):
            x_pair = x_dt[:, pair * LANES : (pair + 1) * LANES]
            results = []
            for i in (2 * pair, 2 * pair + 1):
                col, row = cum[:, i : i + 1], cumt[i : i + 1, :]
                top = jnp.exp(jnp.where(mask, col[:half] - row[:, :half], -1e30))
                low_left = jnp.exp(col[half:] - row[:, :half])
                low_right = jnp.exp(jnp.where(mask, col[half:] - row[:, half:], -1e30))
                top = (top * k[:half, :half]).astype(bf16)
                low = jnp.concatenate(
                    [
                        (low_left * k[half:, :half]).astype(bf16),
                        (low_right * k[half:, half:]).astype(bf16),
                    ],
                    axis=1,
                )
                results.append(
                    jnp.concatenate([dot(top, x_pair[:half], NN), dot(low, x_pair, NN)], axis=0)
                )
            pieces.append(jnp.where(left_lane, results[0], results[1]))
        within = jnp.concatenate(pieces, axis=1)
        ssm = within + carried + skip[...] * act
        ssm_o[...] = ssm
        u = ssm * (gate * sigmoid(gate))
        u_s[:, pl.ds(pl.multiple_of(step * WIDTH, WIDTH), WIDTH)] = u
        ssq_s[...] += jnp.sum(u * u, axis=1, keepdims=True)

    @pl.when(step == GROUPS)
    def _():
        r = lax.rsqrt(ssq_s[...] * (1.0 / DI) + EPS)
        r_o[...] = r
        for g in range(GROUPS):
            cols = slice(g * WIDTH, (g + 1) * WIDTH)
            gout_o[:, cols] = (u_s[:, cols] * r[:, 0:1] * gate_gain[:, cols]).astype(bf16)

    @pl.when(step >= GROUPS)
    def _():
        branch = dot(gout_o[...], wo[...], NN)
        branch_o[...] = branch
        out_o[...] = (h_tile[...].astype(f32) + branch).astype(bf16)


def bwd_body(
    h_ref, gout_ref, ngain, branch, r_ref, wo, wg, wc, wbc, taps, taps_bc, head_rows, skip,
    gate_gain, spread, gather, gate_ref, ssm_ref, cin, cin_bc, step_ref, tail_in, tail_bc_in,
    state_in, adj_in, next_in, next_bc_in,
    gg_o, gc_o, gbc_o, gin_o, gin_low_o, adj_o, next_o, next_bc_o, chan_o, chan_bc_o, ngrad_o,
    head_o,
    acc_s, kt_s, wt_s, b_s, c_s, ct_s, dt_s, ec_s, w_s, cum_s, cumt_s, db_s, dc_s, rows_s, cols_s,
    direct_s, fresh_s, carry_s, edge_s, dsilu_s, q_s, ext_s, ext2_s,
):
    step = pl.program_id(0)
    length = h_ref.shape[0]
    half = length // 2

    @pl.when(step == 0)
    def _():
        fill_ext(ext_s, tail_bc_in[...], cin_bc[...].astype(f32), length, BC)
        pre = conv_pre(ext_s, taps_bc[...], length, BC)
        sig = sigmoid(pre)
        dsilu_s[...] = sig * (1.0 + pre * (1.0 - sig))
        act = (pre * sig).astype(bf16)
        b_rows, c_rows = act[:, :STATE], act[:, STATE:]
        b_s[...] = b_rows
        c_s[...] = c_rows
        ct_s[...] = c_rows.astype(f32).T.astype(bf16)
        kt_s[...] = dot(b_rows, c_rows, NT)
        dt = head_steps(step_ref[...], head_rows[...])
        cum = running_sum(dt * head_rows[1:2])
        total = cum[length - 1 : length]
        dt_s[...] = halves(dt)
        ec_s[...] = halves(jnp.exp(cum))
        w_s[...] = halves(jnp.exp(total - cum))
        for g in range(GROUPS):
            cum_s[g] = cum[:, g * GROUP : (g + 1) * GROUP]
        cumt_s[...] = cum.T
        for ref in (acc_s, wt_s, db_s, dc_s, rows_s, cols_s, direct_s, fresh_s, carry_s, edge_s):
            ref[...] = jnp.zeros_like(ref)
        rowdot = jnp.sum(branch[...] * gout_ref[...].astype(f32), axis=1, keepdims=True)
        q_s[...] = jnp.broadcast_to(rowdot * (1.0 / DI), q_s.shape) * r_ref[...] * r_ref[...]

    @pl.when(step < GROUPS)
    def _():
        grad_gated = dot(gout_ref[...], wo[...], NT)
        gate, ssm = gate_ref[...], ssm_ref[...]
        sig = sigmoid(gate)
        silu = gate * sig
        u = ssm * silu
        scaled = r_ref[:, 0:1] * grad_gated
        gain_grad = jnp.sum(scaled * u, axis=0, keepdims=True)
        grad_u = scaled * gate_gain[...] - u * q_s[:, 0:1]
        grad_ssm = grad_u * silu
        grad_gate = (grad_u * ssm * (sig * (1.0 + gate * (1.0 - sig)))).astype(bf16)
        gg_o[...] = grad_gate
        conv_in = cin[...].astype(f32)
        fill_ext(ext_s, tail_in[...], conv_in, length, WIDTH)
        pre = conv_pre(ext_s, taps[...], length, WIDTH)
        sig = sigmoid(pre)
        act = (pre * sig).astype(bf16).astype(f32)
        dsilu = sig * (1.0 + pre * (1.0 - sig))
        where, pick = spread[...], gather[...]
        dt, ec, w = (dot(ref[...], where, NN) for ref in (dt_s, ec_s, w_s))
        skip_grad = jnp.sum(act * grad_ssm, axis=0, keepdims=True)
        x_dt = act * dt
        x_low, g_low = x_dt.astype(bf16), grad_ssm.astype(bf16)
        g_ec = (grad_ssm * ec).astype(bf16)
        state, adj = state_in[...], adj_in[...]
        state_low, adj_low = state.astype(bf16), adj.astype(bf16)
        from_adj = w * dot(b_s[...], adj_low, NN)
        carried = ec * dot(c_s[...], state_low, NN)
        db_s[...] += dot((x_dt * w).astype(bf16), adj_low, NT)
        dc_s[...] += dot(g_ec, state_low, NT)
        last = ec[length - 1 : length]
        adj_o[...] = last * adj + dot(ct_s[...], g_ec, NN)
        edge = last * jnp.sum(state * adj, axis=0, keepdims=True)
        edge_s[...] += dot(halves(edge), pick, NN)
        cum = cum_s[step]
        start = pl.multiple_of(step * GROUP, GROUP)
        cumt = cumt_s[pl.ds(start, GROUP), :]
        kt = kt_s[...]
        mask = lax.broadcasted_iota(jnp.int32, (half, half), 0) <= lax.broadcasted_iota(
            jnp.int32, (half, half), 1
        )
        left_lane = lax.broadcasted_iota(jnp.int32, (length, LANES), 1) < HEAD_DIM
        lane_id = lax.broadcasted_iota(jnp.int32, (1, LANES), 1)
        pieces, col_sums = [], []
        row_sums = rows_s[...]
        w_tl, w_tr, w_br = wt_s[:half, :half], wt_s[:half, half:], wt_s[half:, half:]
        for pair in range(GROUP // 2):
            lanes = slice(pair * LANES, (pair + 1) * LANES)
            x_pair, g_pair = x_low[:, lanes], g_low[:, lanes]
            results = []
            for i in (2 * pair, 2 * pair + 1):
                col, row = cum[:, i : i + 1], cumt[i : i + 1, :]
                mine = left_lane if i % 2 == 0 else jnp.logical_not(left_lane)
                x_head = jnp.where(mine, x_pair, jnp.zeros_like(x_pair))
                l_tl = jnp.exp(jnp.where(mask, row[:, :half] - col[:half], -1e30))
                l_tr = jnp.exp(row[:, half:] - col[:half])
                l_br = jnp.exp(jnp.where(mask, row[:, half:] - col[half:], -1e30))
                lk_tl, lk_tr, lk_br = (
                    l_tl * kt[:half, :half],
                    l_tr * kt[:half, half:],
                    l_br * kt[half:, half:],
                )
                mixed = jnp.concatenate([lk_tl.astype(bf16), lk_tr.astype(bf16)], axis=1)
                results.append(
                    jnp.concatenate(
                        [dot(mixed, g_pair, NN), dot(lk_br.astype(bf16), g_pair[half:], NN)], axis=0
                    )
                )
                p_top = dot(x_head[:half], g_pair, NT)
                p_br = dot(x_head[half:], g_pair[half:], NT)
                p_tl, p_tr = p_top[:, :half], p_top[:, half:]
                w_tl, w_tr, w_br = w_tl + l_tl * p_tl, w_tr + l_tr * p_tr, w_br + l_br * p_br
                z_tl, z_tr, z_br = lk_tl * p_tl, lk_tr * p_tr, lk_br * p_br
                sums = jnp.concatenate(
                    [
                        jnp.sum(z_tl + z_tr, axis=1, keepdims=True),
                        jnp.sum(z_br, axis=1, keepdims=True),
                    ],
                    axis=0,
                )
                row_sums = row_sums + jnp.where(lane_id == start + i, sums, 0.0)
                col_sums.append(
                    jnp.concatenate(
                        [
                            jnp.sum(z_tl, axis=0, keepdims=True),
                            jnp.sum(z_tr, axis=0, keepdims=True)
                            + jnp.sum(z_br, axis=0, keepdims=True),
                        ],
                        axis=1,
                    )
                )
            pieces.append(jnp.where(left_lane, results[0], results[1]))
        wt_s[:half, :half] = w_tl
        wt_s[:half, half:] = w_tr
        wt_s[half:, half:] = w_br
        rows_s[...] = row_sums
        cols_s[pl.ds(start, GROUP), :] = jnp.concatenate(col_sums, axis=0)
        mixed_grad = jnp.concatenate(pieces, axis=1) + from_adj
        direct_s[...] += dot(halves(act * mixed_grad), pick, NN)
        fresh_s[...] += dot(halves(x_dt * from_adj), pick, NN)
        carry_s[...] += dot(halves(grad_ssm * carried), pick, NN)
        grad_pre = (dt * mixed_grad + skip[...] * grad_ssm) * dsilu
        next_o[...] = grad_pre[0:8]
        ext2_s[0:length] = grad_pre
        ext2_s[length : length + 8] = next_in[...]
        tap_rows = taps[...]
        grad_conv = grad_pre * tap_rows[CONV - 1 : CONV]
        for j in range(CONV - 1):
            shift = CONV - 1 - j
            grad_conv = grad_conv + ext2_s[shift : shift + length] * tap_rows[j : j + 1]
        grad_conv = grad_conv.astype(bf16)
        gc_o[...] = grad_conv
        sums = [
            jnp.sum(grad_pre * ext_s[5 + j : 5 + j + length], axis=0, keepdims=True)
            for j in range(CONV)
        ]
        sums += [jnp.sum(grad_pre, axis=0, keepdims=True), gain_grad, skip_grad]
        chan_o[...] = jnp.concatenate(sums + [jnp.zeros_like(skip_grad)], axis=0)
        acc_s[...] += dot(grad_gate, wg[...], NT) + dot(grad_conv, wc[...], NT)

    @pl.when(step == GROUPS)
    def _():
        wt = wt_s[...].astype(bf16)
        grad_b = db_s[...] + dot(wt, c_s[...], NN)
        grad_c = dc_s[...] + dot(wt, b_s[...], TN)
        grad_pre = jnp.concatenate([grad_b, grad_c], axis=1) * dsilu_s[...]
        next_bc_o[...] = grad_pre[0:8]
        ext2_s[0:length, 0:BC] = grad_pre
        ext2_s[length : length + 8, 0:BC] = next_bc_in[...]
        fill_ext(ext_s, tail_bc_in[...], cin_bc[...].astype(f32), length, BC)
        tap_rows = taps_bc[...]
        grad_conv = grad_pre * tap_rows[CONV - 1 : CONV]
        for j in range(CONV - 1):
            shift = CONV - 1 - j
            grad_conv = grad_conv + ext2_s[shift : shift + length, 0:BC] * tap_rows[j : j + 1]
        sums = [
            jnp.sum(grad_pre * ext_s[5 + j : 5 + j + length, 0:BC], axis=0, keepdims=True)
            for j in range(CONV)
        ]
        sums += [jnp.sum(grad_pre, axis=0, keepdims=True)]
        chan_bc_o[...] = jnp.concatenate(sums + [jnp.zeros((3, BC), f32)], axis=0)
        dt = head_steps(step_ref[...], head_rows[...])
        rate = head_rows[1:2]
        ones = jnp.where(lower_mask(length, length), 1.0, 0.0).astype(f32)
        fresh = fresh_s[...]
        from_here = cols_s[...].T - rows_s[...] + carry_s[...]
        suffix = (
            dot(ones, from_here, TN, lax.Precision.HIGHEST)
            + dot(ones, fresh, NN, lax.Precision.HIGHEST)
            - fresh
            + edge_s[0:1]
        )
        decayed = rate * suffix
        grad_step = (direct_s[...] + decayed) * sigmoid(step_ref[...] + head_rows[0:1])
        head_o[...] = jnp.concatenate(
            [
                jnp.sum(grad_step, axis=0, keepdims=True),
                jnp.sum(dt * decayed, axis=0, keepdims=True),
                jnp.zeros((6, LANES), f32),
            ],
            axis=0,
        )
        low = jnp.concatenate([grad_conv.astype(bf16), grad_step.astype(bf16)], axis=1)
        gbc_o[...] = low
        grad_normed = acc_s[...] + dot(low, wbc[...], NT)
        h = h_ref[...].astype(f32)
        scale = lax.rsqrt(jnp.mean(h * h, axis=1, keepdims=True) + EPS)
        ngrad_o[...] = jnp.sum(grad_normed * h * scale, axis=0, keepdims=True)
        weighted = grad_normed * ngain[...]
        mean = jnp.mean(h * weighted, axis=1, keepdims=True)
        grad_in = gout_ref[...].astype(f32) + scale * weighted - h * (scale * scale * scale * mean)
        gin_o[...] = grad_in
        gin_low_o[...] = grad_in.astype(bf16)


def spread_table():
    table = np.zeros((2 * LANES, DI), np.float32)
    for head in range(HEADS):
        table[head, head * HEAD_DIM : (head + 1) * HEAD_DIM] = 1.0
        table[LANES + head, head * HEAD_DIM : (head + 1) * HEAD_DIM] = 1.0
    return table


def whole(shape):
    return pl.BlockSpec(shape, lambda i: (0,) * len(shape))


def by_group(rows, width=WIDTH):
    return pl.BlockSpec((rows, width), lambda i: (0, jnp.minimum(i, GROUPS - 1)))


def tail_of(rows, width):
    return pl.BlockSpec((rows, width), lambda i: (0, DI // width))


def gather_table():
    table = np.zeros((GROUPS, 2, WIDTH, LANES), np.float32)
    for group in range(GROUPS):
        for column in range(WIDTH):
            table[group, :, column, group * GROUP + column // HEAD_DIM] = 1.0
    return table.reshape(-1, LANES)


def fwd_call(h, params, weights, state, tail, tail_bc):
    length = h.shape[0]
    wg, wc, wo = weights
    out_tiles = D // OUT_TILE
    by_out = pl.BlockSpec((length, OUT_TILE), lambda i: (0, jnp.maximum(i - GROUPS, 0)))
    in_specs = [
        whole((length, D)), by_out, whole((1, D)), by_group(D), by_group(D), tail_of(D, TAIL),
        pl.BlockSpec((DI, OUT_TILE), lambda i: (0, jnp.maximum(i - GROUPS, 0))),
        by_group(8), tail_of(8, BC), whole((8, LANES)), by_group(1), whole((1, DI)),
        by_group(2 * LANES), by_group(16), whole((16, BC)), by_group(STATE),
    ]
    out = [
        ((length, D), bf16, whole((length, D))),
        ((length, DI), f32, by_group(length)),
        ((length, DI), bf16, by_group(length)),
        ((length, BC), bf16, whole((length, BC))),
        ((length, LANES), f32, whole((length, LANES))),
        ((length, DI), f32, by_group(length)),
        ((STATE, DI), f32, by_group(STATE)),
        ((length, DI), bf16, whole((length, DI))),
        ((length, LANES), f32, whole((length, LANES))),
        ((length, D), f32, by_out),
        ((length, D), bf16, by_out),
        ((16, DI), bf16, by_group(16)),
        ((16, BC), bf16, whole((16, BC))),
    ]
    scratch = [
        ((length, DI), f32), ((length, LANES), f32), ((length, length), f32),
        ((length, STATE), bf16), ((STATE, length), bf16), ((length, 2 * LANES), bf16),
        ((length, 2 * LANES), bf16), ((length, 2 * LANES), bf16), ((GROUPS, length, GROUP), f32),
        ((LANES, length), f32), ((length + 8, WIDTH), f32),
    ]
    return pl.pallas_call(
        fwd_body,
        grid=(GROUPS + out_tiles,),
        in_specs=in_specs,
        out_specs=[spec for _, _, spec in out],
        out_shape=[jax.ShapeDtypeStruct(shape, dtype) for shape, dtype, _ in out],
        scratch_shapes=[pltpu.VMEM(shape, dtype) for shape, dtype in scratch],
        compiler_params=pltpu.CompilerParams(
            dimension_semantics=("arbitrary",), vmem_limit_bytes=VMEM_LIMIT
        ),
        cost_estimate=pl.CostEstimate(flops=12 * 10**9, bytes_accessed=45 * 10**6, transcendentals=5 * 10**6),
        name="layer_forward",
    )(
        h, h, params["norm_gain"], wg, wc, wc, wo, params["taps"], params["taps"],
        params["heads"], params["skip"], params["gate_gain"], params["spread"], tail, tail_bc, state,
    )


def bwd_call(h, grad_out, kept, params, weights, adj, ahead, ahead_bc):
    length = h.shape[0]
    wg, wc, wo = weights
    rows_of_wo = pl.BlockSpec((WIDTH, D), lambda i: (jnp.minimum(i, GROUPS - 1), 0))
    pick = pl.BlockSpec((2 * WIDTH, LANES), lambda i: (jnp.minimum(i, GROUPS - 1), 0))
    in_specs = [
        whole((length, D)), whole((length, D)), whole((1, D)), whole((length, D)),
        whole((length, LANES)), rows_of_wo, by_group(D), by_group(D), tail_of(D, TAIL),
        by_group(8), tail_of(8, BC), whole((8, LANES)), by_group(1), by_group(1),
        by_group(2 * LANES), pick, by_group(length), by_group(length), by_group(length),
        whole((length, BC)), whole((length, LANES)), by_group(16), whole((16, BC)),
        by_group(STATE), by_group(STATE), by_group(8), whole((8, BC)),
    ]
    out = [
        ((length, DI), bf16, by_group(length)),
        ((length, DI), bf16, by_group(length)),
        ((length, TAIL), bf16, whole((length, TAIL))),
        ((length, D), f32, whole((length, D))),
        ((length, D), bf16, whole((length, D))),
        ((STATE, DI), f32, by_group(STATE)),
        ((8, DI), f32, by_group(8)),
        ((8, BC), f32, whole((8, BC))),
        ((8, DI), f32, by_group(8)),
        ((8, BC), f32, whole((8, BC))),
        ((1, D), f32, whole((1, D))),
        ((8, LANES), f32, whole((8, LANES))),
    ]
    scratch = [
        ((length, D), f32), ((length, length), f32), ((length, length), f32),
        ((length, STATE), bf16), ((length, STATE), bf16), ((STATE, length), bf16),
        ((length, 2 * LANES), bf16), ((length, 2 * LANES), bf16), ((length, 2 * LANES), bf16),
        ((GROUPS, length, GROUP), f32), ((LANES, length), f32), ((length, STATE), f32),
        ((length, STATE), f32), ((length, LANES), f32), ((LANES, length), f32),
        ((length, LANES), f32), ((length, LANES), f32), ((length, LANES), f32), ((1, LANES), f32),
        ((length, BC), f32), ((length, LANES), f32), ((length + 8, WIDTH), f32),
        ((length + 8, WIDTH), f32),
    ]
    return pl.pallas_call(
        bwd_body,
        grid=(GROUPS + 1,),
        in_specs=in_specs,
        out_specs=[spec for _, _, spec in out],
        out_shape=[jax.ShapeDtypeStruct(shape, dtype) for shape, dtype, _ in out],
        scratch_shapes=[pltpu.VMEM(shape, dtype) for shape, dtype in scratch],
        compiler_params=pltpu.CompilerParams(
            dimension_semantics=("arbitrary",), vmem_limit_bytes=VMEM_LIMIT
        ),
        cost_estimate=pl.CostEstimate(flops=25 * 10**9, bytes_accessed=55 * 10**6, transcendentals=8 * 10**6),
        name="layer_backward",
    )(
        h, grad_out, params["norm_gain"], kept["branch"], kept["r"], wo, wg, wc, wc,
        params["taps"], params["taps"], params["heads"], params["skip"], params["gate_gain"],
        params["spread"], params["gather"], kept["gate"], kept["ssm"], kept["cin"], kept["cin_bc"],
        kept["step"], kept["tail"], kept["tail_bc"], kept["state"], adj, ahead, ahead_bc,
    )


def xor_route(size, bit):
    return [(i, i ^ bit) for i in range(size)]


def bits_of(size):
    return [1 << b for b in range(size.bit_length() - 1)]


def gather_small(row):
    for axis in ("seq", "dp"):
        size, position = lax.axis_size(axis), lax.axis_index(axis)
        for bit in bits_of(size):
            other = lax.ppermute(row, axis, xor_route(size, bit))
            row = jnp.where(
                (position & bit) == 0,
                jnp.concatenate([row, other], axis=0),
                jnp.concatenate([other, row], axis=0),
            )
    return row


def sum_small(value):
    for axis in ("dp", "seq"):
        size = lax.axis_size(axis)
        for bit in bits_of(size):
            value = value + lax.ppermute(value, axis, xor_route(size, bit))
    return value


def direct_paths():
    return lax.axis_size("dp") == 4 and lax.axis_size("seq") == 4


def pair_route(allowed):
    return [(d * 4 + z, (d ^ 2) * 4 + z) for d in range(4) for z in range(4) if allowed(z)]


def gather_rows(shard):
    if not direct_paths():
        return lax.all_gather(shard, ("dp", "seq"), axis=0, tiled=True)
    rows, cols = shard.shape
    dp, z = lax.axis_index("dp"), lax.axis_index("seq")
    y, core = dp // 2, dp % 2
    held = jnp.zeros((2, 4, rows, cols), shard.dtype)

    def place(held, piece, at_y, at_z):
        return lax.dynamic_update_slice(held, piece[None, None], (at_y, at_z, 0, 0))

    up, down = shard, shard
    beside = lax.ppermute(shard, "dp", xor_route(4, 2))
    arrivals = []
    for hop in range(1, 4):
        up = lax.ppermute(up, "seq", [(i, i + 1) for i in range(hop - 1, 3)])
        down = lax.ppermute(down, "seq", [(i, i - 1) for i in range(1, 5 - hop)])
        up_beside = lax.ppermute(up, ("dp", "seq"), pair_route(lambda i: i >= hop))
        down_beside = lax.ppermute(down, ("dp", "seq"), pair_route(lambda i: i <= 3 - hop))
        arrivals.append((up, up_beside, jnp.where(z >= hop, z - hop, z)))
        arrivals.append((down, down_beside, jnp.where(z + hop <= 3, z + hop, z)))
    for piece, piece_beside, at in arrivals:
        held = place(held, piece, y, at)
        held = place(held, piece_beside, 1 - y, at)
    held = place(place(held, beside, 1 - y, z), shard, y, z)
    other = lax.ppermute(held, "dp", xor_route(4, 1))
    full = jnp.where(
        core == 0, jnp.stack([held, other], axis=1), jnp.stack([other, held], axis=1)
    )
    return full.reshape(16 * rows, cols)


def reduce_rows(mine, rest):
    dp, z = lax.axis_index("dp"), lax.axis_index("seq")
    y = dp // 2
    from_core = lax.ppermute(rest(), "dp", xor_route(4, 1))
    chip = mine(from_core)
    order = jnp.array([[3, 2, 1, 0], [3, 2, 0, 1], [0, 1, 3, 2], [0, 1, 2, 3]], jnp.int32)[z]
    sums = []
    for j in range(4):
        at = order[j]

        def pick(at_y):
            return lax.dynamic_slice(chip, (at_y, at, 0, 0), (1, 1) + chip.shape[2:])[0, 0]

        arrived = lax.ppermute(pick(1 - y), "dp", xor_route(4, 2))
        sums.append(pick(y).astype(f32) + arrived.astype(f32))

    def up(value, hop):
        return lax.ppermute(value.astype(bf16), "seq", [(i, i + 1) for i in range(hop)]).astype(f32)

    def down(value, hop):
        return lax.ppermute(
            value.astype(bf16), "seq", [(i, i - 1) for i in range(4 - hop, 4)]
        ).astype(f32)

    up_1, down_1 = up(sums[0], 1), down(sums[0], 1)
    up_2 = up(jnp.where(z == 0, sums[1], sums[0]) + up_1, 2)
    down_2 = down(jnp.where(z == 3, sums[1], sums[0]) + down_1, 2)
    up_3 = up(jnp.where(z == 1, sums[1], sums[2]) + up_2, 3)
    down_3 = down(jnp.where(z == 2, sums[1], sums[2]) + down_2, 3)
    return sums[3] + up_3 + down_3


def weight_grad(left, right):
    def term(columns):
        return jnp.einsum("td,te->de", columns, right, preferred_element_type=f32)

    dp, seq = lax.axis_size("dp"), lax.axis_size("seq")
    if not direct_paths():
        return lax.optimization_barrier(
            lax.psum_scatter(term(left), ("dp", "seq"), scatter_dimension=0, tiled=True)
        )
    rows = left.shape[1] // (dp * seq)
    core = lax.axis_index("dp") % 2
    by_core = left.reshape(left.shape[0], 2, 2, 4 * rows)
    shape = (2, 4, rows, right.shape[1])

    def owned(which):
        chosen = jnp.where(which == 0, by_core[:, :, 0], by_core[:, :, 1])
        return term(chosen.reshape(left.shape[0], 8 * rows))

    return reduce_rows(
        lambda arrived: (owned(core).reshape(shape) + arrived.astype(f32)).astype(bf16),
        lambda: owned(1 - core).astype(bf16).reshape(shape),
    )


def turn(value, shift, parts):
    size = lax.axis_size("seq")
    route = [(i, i - i % parts + (i % parts + shift) % parts) for i in range(size)]
    return lax.ppermute(value, "seq", route)


def to_sequences(rows):
    parts = rows.shape[0]
    rank = lax.axis_index("seq") % parts
    arrived = []
    for shift in range(parts):
        piece = lax.dynamic_index_in_dim(rows, (rank + shift) % parts, 0, keepdims=False)
        arrived.append(piece if shift == 0 else turn(piece, shift, parts))
    arrived = jnp.stack(arrived)
    return [
        lax.dynamic_index_in_dim(arrived, (rank - k) % parts, 0, keepdims=False)
        for k in range(parts)
    ]


def to_pieces(blocks, sent_type):
    parts = len(blocks)
    rank = lax.axis_index("seq") % parts
    stacked = jnp.stack(blocks)
    held = stacked
    for shift in range(parts):
        piece = lax.dynamic_index_in_dim(stacked, (rank + shift) % parts, 0, keepdims=False)
        if shift:
            piece = turn(piece.astype(sent_type), shift, parts).astype(piece.dtype)
        held = lax.dynamic_update_slice(held, piece[None], ((rank - shift) % parts, 0, 0))
    return held


KEPT = (
    "normed", "gate", "cin", "cin_bc", "step", "ssm", "state_out", "gout", "r", "branch", "out",
    "tail_out", "tail_bc_out",
)
SKEW = 2


def shards(
    tokens, cotangent, in_proj, out_proj, conv_weight, conv_bias, norm_gain, gate_gain, step_bias,
    log_decay, skip_gain,
):
    first = lax.axis_index("section") == 0
    seq = lax.axis_size("seq")
    parts, length = tokens.shape[0], tokens.shape[1]
    owned = in_proj.shape[1]
    blocks_in = to_sequences(jnp.where(first, tokens, cotangent))

    shard = in_proj[0]
    shard_conv = jnp.pad(shard[:, DI:], ((0, 0), (0, TAIL - BC - HEADS)))
    w_conv = gather_rows(shard_conv)
    w_gate = gather_rows(shard[:, :DI])
    w_out = gather_rows(out_proj[0])
    weights = (w_gate, w_conv, w_out)

    sizes = [CONV * conv_bias.shape[1], conv_bias.shape[1], norm_gain.shape[1], gate_gain.shape[1]]
    packed = jnp.concatenate([conv_weight[0].reshape(-1), conv_bias[0], norm_gain[0], gate_gain[0]])
    packed = gather_small(packed[None]).astype(f32)
    ends = np.cumsum(sizes)
    taps, shift, gain_in, gain_gate = (
        packed[:, end - size : end] for end, size in zip(ends, sizes)
    )
    taps = jnp.swapaxes(taps.reshape(-1, CONV, conv_bias.shape[1]), 0, 1).reshape(CONV, -1)
    taps = jnp.concatenate([taps, shift.reshape(1, -1), jnp.zeros((3, taps.shape[1]), f32)], axis=0)
    lanes = ((0, 0), (0, LANES - HEADS))
    params = {
        "norm_gain": gain_in.reshape(1, -1),
        "gate_gain": gain_gate.reshape(1, -1),
        "taps": taps,
        "heads": jnp.pad(
            jnp.concatenate([step_bias, -jnp.exp(log_decay), jnp.zeros((6, HEADS), f32)], axis=0),
            lanes,
        ),
        "skip": jnp.repeat(skip_gain, HEAD_DIM, axis=1),
        "spread": jnp.asarray(spread_table(), bf16),
        "gather": jnp.asarray(gather_table(), bf16),
    }

    ticks = parts + SKEW
    hops = seq // parts

    def forward(start):
        kept, received = [], [jnp.zeros((length, D), bf16)] * SKEW
        carry = start
        for tick in range(ticks):
            if tick == SKEW:
                carry = tuple(jnp.where(first, now, at) for now, at in zip(carry, start))
            h = jnp.where(first, blocks_in[min(tick, parts - 1)], received[tick])
            values = dict(zip(KEPT, fwd_call(h, params, weights, *carry)))
            values.update(h=h, state=carry[0], tail=carry[1], tail_bc=carry[2])
            carry = (values["state_out"], values["tail_out"], values["tail_bc_out"])
            kept.append(values)
            if tick < parts:
                received.append(lax.ppermute(values["out"], "section", [(0, 1)]))
        return kept

    def backward(kept, start):
        zeros = tuple(jnp.zeros_like(part) for part in start)
        carry = tuple(jnp.where(first, zero, at) for zero, at in zip(zeros, start))
        grads, received = [None] * ticks, [jnp.zeros((length, D), bf16)] * SKEW
        for tick in range(ticks):
            if tick == SKEW and hops > 1:
                carry = tuple(jnp.where(first, at, now) for now, at in zip(carry, start))
            if tick == parts:
                carry = tuple(jnp.where(first, now, zero) for now, zero in zip(carry, zeros))
            from_loss = blocks_in[parts - 1 - tick] if tick < parts else zeros_low
            grad_out = jnp.where(first, received[tick], from_loss)
            at = ticks - 1 - tick
            names = (
                "gate", "conv", "tail", "in", "in_low", "adj", "next", "next_bc", "chan", "chan_bc",
                "norm", "head",
            )
            values = dict(
                zip(names, bwd_call(kept[at]["h"], grad_out, kept[at], params, weights, *carry))
            )
            values["out"] = grad_out
            carry = (values["adj"], values["next"], values["next_bc"])
            grads[at] = values
            if tick < parts:
                received.append(lax.ppermute(values["in_low"], "section", [(1, 0)]))
        return grads

    zeros_low = jnp.zeros((length, D), bf16)
    start = (jnp.zeros((STATE, DI), f32), jnp.zeros((16, DI), bf16), jnp.zeros((16, BC), bf16))
    if hops > 1:

        def onward(_, start):
            kept = forward(start)
            ends = (
                tuple(kept[parts - 1][name] for name in ("state_out", "tail_out", "tail_bc_out")),
                tuple(kept[ticks - 1][name] for name in ("state_out", "tail_out", "tail_bc_out")),
            )
            route = [(i, i + parts) for i in range(seq - parts)]
            return tuple(
                lax.ppermute(jnp.where(first, a, b), "seq", route) for a, b in zip(*ends)
            )

        start = lax.fori_loop(0, hops - 1, onward, start)
    kept = forward(start)
    activations = to_pieces(
        [jnp.where(first, kept[k]["out"], kept[k + SKEW]["out"]) for k in range(parts)], bf16
    )[None]

    start = (jnp.zeros((STATE, DI), f32), jnp.zeros((8, DI), f32), jnp.zeros((8, BC), f32))
    if hops > 1:

        def back(_, start):
            grads = backward(kept, start)
            ends = (
                tuple(grads[0][name] for name in ("adj", "next", "next_bc")),
                tuple(grads[SKEW][name] for name in ("adj", "next", "next_bc")),
            )
            route = [(i, i - parts) for i in range(parts, seq)]
            return tuple(
                lax.ppermute(jnp.where(first, a, b), "seq", route) for a, b in zip(*ends)
            )

        start = lax.fori_loop(0, hops - 1, back, start)
    grads = backward(kept, start)

    def select(values, name):
        return jnp.concatenate(
            [jnp.where(first, values[k][name], values[k + SKEW][name]) for k in range(parts)], axis=0
        )

    normed, gate_out = select(kept, "normed"), select(kept, "gout")
    grad_out_proj = weight_grad(gate_out, select(grads, "out"))[None]
    grad_gate = weight_grad(normed, select(grads, "gate"))
    grad_conv = weight_grad(
        normed, jnp.concatenate([select(grads, "conv"), select(grads, "tail")], axis=1)
    )
    grad_in_proj = jnp.concatenate([grad_gate, grad_conv[:, : DI + BC + HEADS]], axis=1)[None]
    input_grads = to_pieces(
        [jnp.where(first, grads[k]["in"], grads[k + SKEW]["in"]) for k in range(parts)], bf16
    )[None]

    def total(name):
        return sum(values[name] for values in grads)

    channels = jnp.concatenate([total("chan"), total("chan_bc")], axis=1)
    norm = total("norm")
    head = total("head")
    skip = channels[6, :DI].reshape(HEADS, HEAD_DIM).sum(axis=1)
    small = jnp.concatenate(
        [
            channels[: CONV + 1].reshape(-1), channels[5, :DI], norm[0], head[0], head[1],
            jnp.pad(skip, (0, LANES - HEADS)),
        ]
    )
    small = sum_small(small.reshape(-1, LANES)).reshape(-1)
    place = lax.axis_index("dp") * seq + lax.axis_index("seq")

    def mine(flat, width):
        return lax.dynamic_slice_in_dim(flat, place * width, width, axis=flat.ndim - 1)

    width = conv_bias.shape[1]
    full = CONV * (DI + BC)
    grad_taps = small[:full].reshape(CONV, -1)
    grad_shift = small[full : full + DI + BC]
    rest = small[full + DI + BC :]
    return (
        activations,
        input_grads,
        grad_in_proj,
        grad_out_proj,
        mine(grad_taps, width)[None],
        mine(grad_shift, width)[None],
        mine(rest[DI : DI + D], owned)[None],
        mine(rest[:DI], gate_gain.shape[1])[None],
        rest[DI + D : DI + D + HEADS][None],
        rest[DI + D + LANES : DI + D + LANES + HEADS][None],
        rest[DI + D + 2 * LANES : DI + D + 2 * LANES + HEADS][None],
    )


def solution(mesh):
    placed = (
        P("dp", "seq", None),
        P("dp", "seq", None),
        P("section", ("dp", "seq"), None),
        P("section", ("dp", "seq"), None),
        P("section", None, ("dp", "seq")),
        P("section", ("dp", "seq")),
        P("section", ("dp", "seq")),
        P("section", ("dp", "seq")),
        P("section", None),
        P("section", None),
        P("section", None),
    )
    return jax.shard_map(
        shards,
        mesh=mesh,
        in_specs=placed,
        out_specs=(
            P("section", "dp", "seq", None),
            P("section", "dp", "seq", None),
        )
        + placed[2:],
        check_vma=False,
    )
```

time: 3350 us -> 1440 us (0.43)
  waiting for transfers between devices: 1460 us -> 398 us
  matrix products: 738 us -> 69.9 us
  Pallas kernels: 0 us -> 424 us
  other arithmetic: 432 us -> 107 us
  local copies, waits for them, and re-layouts: 433 us -> 181 us
  blocking collectives: 207 us -> 0 us
  starting transfers between devices: 34.2 us -> 236 us
    all_gather x12 -> x0, waiting for transfers between devices: 730 us -> none  [the longest x10 698 us: prefix(): everything = jax.tree.map(lambda part: lax.all_gather(part, axis), value)]
    dot_general x96 -> x6, matrix products: 738 us -> 69.9 us  [term(): return jnp.einsum('td,te->de', columns, right, preferred_element_type=f32)]
    reduce_scatter x2 -> x0, waiting for transfers between devices: 587 us -> none  [the longest x1 391 us: shards(): lax.psum_scatter(make_term(normed_all, proj_all), ('dp', 'seq'), scatter_...]
    pallas_call x0 -> x12, Pallas kernels: none -> 424 us  [the longest x6 249 us: bwd_call(): pl.pallas_call(bwd_body, grid=(GROUPS + 1,), in_specs=in_specs, out_specs...]
    ppermute x18 -> x100, waiting for transfers between devices: 139 us -> 398 us  [the longest x9 82 us: gather_rows(): down = lax.ppermute(down, 'seq', [(i, i - 1) for i in range(1, 5 - hop)])]
    ppermute x18 -> x100, starting transfers between devices: 33.5 us -> 236 us  [the longest x9 64.5 us: up(): lax.ppermute(value.astype(bf16), 'seq', [(i, i + 1) for i in range(hop)])]
    reduce_sum x46 -> x1, other arithmetic: 152 us -> 0.11 us  [shards(): skip = channels[6, :DI].reshape(HEADS, HEAD_DIM).sum(axis=1)]
    all_gather x6 -> x0, blocking collectives: 109 us -> none  [the longest x1 63 us: shards(): lax.all_gather(conv_weight, ('dp', 'seq'), axis=2, tiled=True)]
  transfers between devices with their start and end apart: 36 -> 100, of which waited for: 22 -> 38; matrix products, arithmetic and copies ran while one was open for 23% -> 18% of each run, Pallas kernels for 0% -> 19%
where the time goes in v1:
time: 1440 us; the launch traced here: 1430 us
  Pallas kernels  424 us (29%)
  waiting for transfers between devices  398 us (28%)
  starting transfers between devices  236 us (16%)
  local copies, waits for them, and re-layouts  181 us (13%)
  other arithmetic  107 us (7%)
  matrix products  69.9 us (5%)
    pallas_call x6, Pallas kernels, bwd_call(): pl.pallas_call(bwd_body, grid=(GROUPS + 1,), in_specs=in_specs, out_specs...  249 us
    pallas_call x6, Pallas kernels, fwd_call(): pl.pallas_call(fwd_body, grid=(GROUPS + out_tiles,), in_specs=in_specs, o...  175 us
    ppermute x9, waiting for transfers between devices, gather_rows(): down = lax.ppermute(down, 'seq', [(i, i - 1) for i in range(1, 5 - hop)])  82 us
    ppermute x9, waiting for transfers between devices, turn(): return lax.ppermute(value, 'seq', route)  75.6 us
    ppermute x9, waiting for transfers between devices, gather_rows(): lax.ppermute(down, ('dp', 'seq'), pair_route(lambda i: i <= 3 - hop))  74.9 us
    dot_general x6, matrix products, term(): return jnp.einsum('td,te->de', columns, right, preferred_element_type=f32)  69.9 us
    ppermute x9, starting transfers between devices, up(): lax.ppermute(value.astype(bf16), 'seq', [(i, i + 1) for i in range(hop)])  64.5 us
    unnamed x243, local copies, waits for them, and re-layouts  62.5 us
  transfers between devices with their start and end apart: 100, of which 38 were waited for; matrix products, arithmetic and copies ran while one was open for 18% of the time, Pallas kernels for 19%

profile of v1, /device:TPU:0, one launch (start us, length us, event | category | flops | bytes accessed | tf_op | source)
XLA Modules:
  0.0 1426.2 jit_solution(11861558741904345393)
XLA Ops:
  71.0 20.1 %collective-permute-done.10 = bf16[96,3072]{1,0:T(8,128)(2,1)S(1)} collective-permute-done((bf16[96,3072]{1,0:T(8,128)(2,1)}, bf16[96,3072]{1,0:T(8,128)(2,1)S(1)}, u32[]{:S(2)}, u32[]{:S(2)}) %collective-permute-start.10) | collective-permute-done | bytes 589856 | tf_op jit(solution)/shard_map/ppermute | solution.py:586
  112.4 34.8 %collective-permute-done.23 = bf16[96,3456]{1,0:T(8,128)(2,1)S(1)} collective-permute-done((bf16[96,3456]{1,0:T(8,128)(2,1)S(1)}, bf16[96,3456]{1,0:T(8,128)(2,1)S(1)}, u32[]{:S(2)}, u32[]{:S(2)}) %collective-permute-start.23) | collective-permute-done | bytes 663584 | tf_op jit(solution)/shard_map/ppermute | solution.py:584
  211.3 21.4 %collective-permute-done.27 = bf16[96,3456]{1,0:T(8,128)(2,1)S(1)} collective-permute-done((bf16[96,3456]{1,0:T(8,128)(2,1)S(1)}, bf16[96,3456]{1,0:T(8,128)(2,1)S(1)}, u32[]{:S(2)}, u32[]{:S(2)}) %collective-permute-start.27) | collective-permute-done | bytes 663584 | tf_op jit(solution)/shard_map/ppermute | solution.py:584
  333.0 36.8 %collective-permute-start = (bf16[256,1536]{1,0:T(8,128)(2,1)}, bf16[256,1536]{1,0:T(8,128)(2,1)S(1)}, u32[]{:S(2)}, u32[]{:S(2)}) collective-permute-start(bf16[256,1536]{1,0:T(8,128)(2,1)} %get-tuple-element.353), channel_id=1, source_target_pairs={{0,1},{1,2},{2,3},{3,0},{4,5},{5,6},{6,7},{7,4},{8,9},{9,10},{10,1... | collective-permute-start | bytes 2359304 | tf_op jit(solution)/shard_map/ppermute | solution.py:659
  427.0 29.0 %layer_forward.6 = (bf16[256,1536]{1,0:T(8,128)(2,1)}, f32[256,3072]{1,0:T(8,128)}, bf16[256,3072]{1,0:T(8,128)(2,1)}, bf16[256,256]{1,0:T(8,128)(2,1)}, f32[256...) custom-call(bf16[256,1536]{1,0:T(8,128)(2,1)} %bitcast_select_fusion, ...), custom_call_target="tpu_custom_call" | custom-call | flops 12000000000 | bytes 45000000 | tf_op jit(solution)/shard_map/layer_forward/pallas_call | solution.py:456
  459.8 15.2 %collective-permute-done.49 = bf16[256,1536]{1,0:T(8,128)(2,1)} collective-permute-done((bf16[256,1536]{1,0:T(8,128)(2,1)}, bf16[256,1536]{1,0:T(8,128)(2,1)}, u32[]{:S(2)}, u32[]{:S(2)}) %collective-permute-start.49) | collective-permute-done | bytes 786464 | tf_op jit(solution)/shard_map/ppermute | solution.py:751
  476.7 29.0 %layer_forward.7 = (bf16[256,1536]{1,0:T(8,128)(2,1)}, f32[256,3072]{1,0:T(8,128)}, bf16[256,3072]{1,0:T(8,128)(2,1)}, bf16[256,256]{1,0:T(8,128)(2,1)}, f32[256...) custom-call(bf16[256,1536]{1,0:T(8,128)(2,1)} %get-tuple-element.341, ...), custom_call_target="tpu_custom_call" | custom-call | flops 12000000000 | bytes 45000000 | tf_op jit(solution)/shard_map/layer_forward/pallas_call | solution.py:456
  516.3 29.0 %layer_forward.8 = (bf16[256,1536]{1,0:T(8,128)(2,1)}, f32[256,3072]{1,0:T(8,128)}, bf16[256,3072]{1,0:T(8,128)(2,1)}, bf16[256,256]{1,0:T(8,128)(2,1)}, f32[256...) custom-call(bf16[256,1536]{1,0:T(8,128)(2,1)} %get-tuple-element.340, ...), custom_call_target="tpu_custom_call" | custom-call | flops 12000000000 | bytes 45000000 | tf_op jit(solution)/shard_map/layer_forward/pallas_call | solution.py:456
  563.1 29.2 %layer_forward.9 = (bf16[256,1536]{1,0:T(8,128)(2,1)}, f32[256,3072]{1,0:T(8,128)}, bf16[256,3072]{1,0:T(8,128)(2,1)}, bf16[256,256]{1,0:T(8,128)(2,1)}, f32[256...) custom-call(bf16[256,1536]{1,0:T(8,128)(2,1)} %get-tuple-element.349, ...), custom_call_target="tpu_custom_call" | custom-call | flops 12000000000 | bytes 45000000 | tf_op jit(solution)/shard_map/layer_forward/pallas_call | solution.py:456
  599.3 29.2 %layer_forward.10 = (bf16[256,1536]{1,0:T(8,128)(2,1)}, f32[256,3072]{1,0:T(8,128)}, bf16[256,3072]{1,0:T(8,128)(2,1)}, bf16[256,256]{1,0:T(8,128)(2,1)}, f32[25...) custom-call(bf16[256,1536]{1,0:T(8,128)(2,1)} %get-tuple-element.348, ...), custom_call_target="tpu_custom_call" | custom-call | flops 12000000000 | bytes 45000000 | tf_op jit(solution)/shard_map/layer_forward/pallas_call | solution.py:456
  635.1 29.1 %layer_forward.11 = (bf16[256,1536]{1,0:T(8,128)(2,1)}, f32[256,3072]{1,0:T(8,128)}, bf16[256,3072]{1,0:T(8,128)(2,1)}, bf16[256,256]{1,0:T(8,128)(2,1)}, f32[25...) custom-call(bf16[256,1536]{1,0:T(8,128)(2,1)} %bitcast_select_fusion, ...), custom_call_target="tpu_custom_call" | custom-call | flops 12000000000 | bytes 45000000 | tf_op jit(solution)/shard_map/layer_forward/pallas_call | solution.py:456
  680.5 14.9 %reshape.201 = bf16[1024,2,2,768]{3,2,1,0:T(2,128)(2,1)} reshape(bf16[1024,3072]{1,0:T(8,128)(2,1)} %pad_maximum_fusion.2) | data formatting | bytes 12582912 | tf_op jit(solution)/shard_map/reshape | solution.py:643
  725.6 41.2 %layer_backward.6 = (bf16[256,3072]{1,0:T(8,128)(2,1)}, bf16[256,3072]{1,0:T(8,128)(2,1)}, bf16[256,384]{1,0:T(8,128)(2,1)}, f32[256,1536]{1,0:T(8,128)}, bf16[2...) custom-call(bf16[256,1536]{1,0:T(8,128)(2,1)} %bitcast_select_fusion, ...), custom_call_target="tpu_custom_call" | custom-call | flops 24999999488 | bytes 55000000 | tf_op jit(solution)/shard_map/layer_backward/pallas_call | solution.py:511
  766.8 41.5 %layer_backward.7 = (bf16[256,3072]{1,0:T(8,128)(2,1)}, bf16[256,3072]{1,0:T(8,128)(2,1)}, bf16[256,384]{1,0:T(8,128)(2,1)}, f32[256,1536]{1,0:T(8,128)}, bf16[2...) custom-call(bf16[256,1536]{1,0:T(8,128)(2,1)} %get-tuple-element.348, ...), custom_call_target="tpu_custom_call" | custom-call | flops 24999999488 | bytes 55000000 | tf_op jit(solution)/shard_map/layer_backward/pallas_call | solution.py:511
  834.8 15.2 %copy.40 = bf16[1024,2,1,768]{0,3,1,2:T(8,128)(2,1)} copy(bf16[1024,2,1,768]{3,2,1,0:T(2,128)(2,1)} %get-tuple-element.306) | data formatting | bytes 6291456
  862.9 41.1 %layer_backward.8 = (bf16[256,3072]{1,0:T(8,128)(2,1)}, bf16[256,3072]{1,0:T(8,128)(2,1)}, bf16[256,384]{1,0:T(8,128)(2,1)}, f32[256,1536]{1,0:T(8,128)}, bf16[2...) custom-call(bf16[256,1536]{1,0:T(8,128)(2,1)} %get-tuple-element.349, ...), custom_call_target="tpu_custom_call" | custom-call | flops 24999999488 | bytes 55000000 | tf_op jit(solution)/shard_map/layer_backward/pallas_call | solution.py:511
  904.0 41.6 %layer_backward.9 = (bf16[256,3072]{1,0:T(8,128)(2,1)}, bf16[256,3072]{1,0:T(8,128)(2,1)}, bf16[256,384]{1,0:T(8,128)(2,1)}, f32[256,1536]{1,0:T(8,128)}, bf16[2...) custom-call(bf16[256,1536]{1,0:T(8,128)(2,1)} %get-tuple-element.340, ...), custom_call_target="tpu_custom_call" | custom-call | flops 24999999488 | bytes 55000000 | tf_op jit(solution)/shard_map/layer_backward/pallas_call | solution.py:511
  955.0 25.8 %collective-permute-done.59 = bf16[256,1536]{1,0:T(8,128)(2,1)S(1)} collective-permute-done((bf16[256,1536]{1,0:T(8,128)(2,1)S(1)}, bf16[256,1536]{1,0:T(8,128)(2,1)S(1)}, u32[]{:S(2)}, u32[]{:S(2)}) %collective-permute-start.59) | collective-permute-done | bytes 786464 | tf_op jit(solution)/shard_map/ppermute | solution.py:777
  982.1 41.4 %layer_backward.10 = (bf16[256,3072]{1,0:T(8,128)(2,1)}, bf16[256,3072]{1,0:T(8,128)(2,1)}, bf16[256,384]{1,0:T(8,128)(2,1)}, f32[256,1536]{1,0:T(8,128)}, bf16[...) custom-call(bf16[256,1536]{1,0:T(8,128)(2,1)} %get-tuple-element.341, ...), custom_call_target="tpu_custom_call" | custom-call | flops 24999999488 | bytes 55000000 | tf_op jit(solution)/shard_map/layer_backward/pallas_call | solution.py:511
  1024.9 42.1 %layer_backward.11 = (bf16[256,3072]{1,0:T(8,128)(2,1)}, bf16[256,3072]{1,0:T(8,128)(2,1)}, bf16[256,384]{1,0:T(8,128)(2,1)}, f32[256,1536]{1,0:T(8,128)}, bf16[...) custom-call(bf16[256,1536]{1,0:T(8,128)(2,1)} %bitcast_select_fusion, ...), custom_call_target="tpu_custom_call" | custom-call | flops 24999999488 | bytes 55000000 | tf_op jit(solution)/shard_map/layer_backward/pallas_call | solution.py:511
  1088.0 30.8 %convolution_convert_fusion.1 = bf16[768,3456]{1,0:T(8,128)(2,1)} fusion(bf16[1024,768]{0,1:T(8,128)(2,1)S(1)} %bitcast.391, bf16[256,384]{1,0:T(8,128)(2,1)S(1)} %get-tuple-element.385, bf16[256,384]{1,0:T(8,128)(2,1)S(1)} %get-tuple-element.383, bf16[256,384]{1,0:T(8,128)(2,1)S(1)} %get-tuple-element.384, bf16[256,384]{1,0:T(8,128)(2,1)S(1)} %get-tuple-element.382, ...), kind=kOutput, calls=%fused_computation.10 | convolution fusion | flops 5495095296 | bytes 13959168 | tf_op jit(solution)/shard_map/td,te->de/dot_general | solution.py:634
  1147.3 27.8 %collective-permute-done.99 = f32[169,128]{1,0:T(8,128)S(1)} collective-permute-done((f32[169,128]{1,0:T(8,128)S(1)}, f32[169,128]{1,0:T(8,128)S(1)}, u32[]{:S(2)}, u32[]{:S(2)}) %collective-permute-start.99) | collective-permute-done | bytes 86560 | tf_op jit(solution)/shard_map/ppermute | solution.py:556
  1201.3 33.5 %collective-permute-done.62 = bf16[256,1536]{1,0:T(8,128)(2,1)S(1)} collective-permute-done((bf16[256,1536]{1,0:T(8,128)(2,1)}, bf16[256,1536]{1,0:T(8,128)(2,1)S(1)}, u32[]{:S(2)}, u32[]{:S(2)}) %collective-permute-start.62) | collective-permute-done | bytes 786464 | tf_op jit(solution)/shard_map/ppermute | solution.py:659
  1282.2 16.9 %collective-permute-done.87 = bf16[192,1536]{1,0:T(8,128)(2,1)S(1)} collective-permute-done((bf16[192,1536]{1,0:T(8,128)(2,1)}, bf16[192,1536]{1,0:T(8,128)(2,1)S(1)}, u32[]{:S(2)}, u32[]{:S(2)}) %collective-permute-start.87) | collective-permute-done | bytes 589856 | tf_op jit(solution)/shard_map/ppermute | solution.py:613
  (617 shorter events, 698.1 us)
Async XLA Ops:
  2.6 266.6 %collective-permute-start.19 = (bf16[96,3072]{1,0:T(8,128)(2,1)}, bf16[96,3072]{1,0:T(8,128)(2,1)}, u32[]{:S(2)}, u32[]{:S(2)}) collective-permute-start(bf16[96,3072]{1,0:T(8,128)(2,1)} %slice.184), channel_id=1, source_target_pairs={{0,8},{4,12},{8,0},{12,4},{1,9},{5,13},{9,1},{13,5},{2,10},{6,14},... | collective-permute-start | bytes 1769480 | tf_op jit(solution)/shard_map/ppermute | solution.py:580
  5.5 58.7 %collective-permute-start.9 = (bf16[96,3072]{1,0:T(8,128)(2,1)}, bf16[96,3072]{1,0:T(8,128)(2,1)}, u32[]{:S(2)}, u32[]{:S(2)}) collective-permute-start(bf16[96,3072]{1,0:T(8,128)(2,1)} %slice.184), channel_id=1, source_target_pairs={{1,0},{2,1},{3,2},{5,4},{6,5},{7,6},{9,8},{10,9},{11,10},{13,12},{... | collective-permute-start | bytes 1769480 | tf_op jit(solution)/shard_map/ppermute | solution.py:584
  12.2 283.8 %collective-permute-start.47 = (bf16[192,1536]{1,0:T(8,128)(2,1)}, bf16[192,1536]{1,0:T(8,128)(2,1)}, u32[]{:S(2)}, u32[]{:S(2)}) collective-permute-start(bf16[192,1536]{1,0:T(8,128)(2,1)} %bitcast.395), channel_id=1, source_target_pairs={{0,8},{4,12},{8,0},{12,4},{1,9},{5,13},{9,1},{13,5},{2,10},{6,14},... | collective-permute-start | bytes 1769480 | tf_op jit(solution)/shard_map/ppermute | solution.py:580
  36.3 56.4 %collective-permute-start.37 = (bf16[192,1536]{1,0:T(8,128)(2,1)}, bf16[192,1536]{1,0:T(8,128)(2,1)S(1)}, u32[]{:S(2)}, u32[]{:S(2)}) collective-permute-start(bf16[192,1536]{1,0:T(8,128)(2,1)} %bitcast.397), channel_id=1, source_target_pairs={{1,0},{2,1},{3,2},{5,4},{6,5},{7,6},{9,8},{10,9},{11,10},{13,12},{... | collective-permute-start | bytes 1769480 | tf_op jit(solution)/shard_map/ppermute | solution.py:584
  64.2 241.3 %collective-permute-start.33 = (bf16[96,3456]{1,0:T(8,128)(2,1)S(1)}, bf16[96,3456]{1,0:T(8,128)(2,1)S(1)}, u32[]{:S(2)}, u32[]{:S(2)}) collective-permute-start(bf16[96,3456]{1,0:T(8,128)(2,1)S(1)} %pad.12), channel_id=1, source_target_pairs={{0,8},{4,12},{8,0},{12,4},{1,9},{5,13},{9,1},{13,5},{2,10},{6,14},... | collective-permute-start | bytes 1990664 | tf_op jit(solution)/shard_map/ppermute | solution.py:580
  253.9 53.4 %collective-permute-start.3 = (bf16[1,1328]{1,0:T(2,128)(2,1)S(1)}, bf16[1,1328]{1,0:T(2,128)(2,1)S(1)}, u32[]{:S(2)}, u32[]{:S(2)}) collective-permute-start(bf16[1,1328]{1,0:T(2,128)(2,1)S(1)} %broadcast_in_dim.215), channel_id=1, source_target_pairs={{0,1},{1,0},{2,3},{3,2},{4,5},{5,4},{6,7},{7,6},{8,9},{9,8},{10,11... | collective-permute-start | bytes 7976 | tf_op jit(solution)/shard_map/ppermute | solution.py:543
  296.0 92.4 %collective-permute-start.20 = (bf16[2,4,96,3072]{3,2,1,0:T(8,128)(2,1)}, bf16[2,4,96,3072]{3,2,1,0:T(8,128)(2,1)}, u32[]{:S(2)}, u32[]{:S(2)}) collective-permute-start(bf16[2,4,96,3072]{3,2,1,0:T(8,128)(2,1)} %bitcast_dynamic-update-slice_fusion.33), channel_id=1, source_target_pairs={{0,4},{4,0},{8,12},{12,8},{1,5},{5,1},{9,13},{13,9},{2,6},{6,2},{1... | collective-permute-start | bytes 14155784 | tf_op jit(solution)/shard_map/ppermute | solution.py:593
  298.8 102.0 %collective-permute-start.48 = (bf16[2,4,192,1536]{3,2,1,0:T(8,128)(2,1)}, bf16[2,4,192,1536]{3,2,1,0:T(8,128)(2,1)}, u32[]{:S(2)}, u32[]{:S(2)}) collective-permute-start(bf16[2,4,192,1536]{3,2,1,0:T(8,128)(2,1)} %bitcast_dynamic-update-slice_fusion.19), channel_id=1, source_target_pairs={{0,4},{4,0},{8,12},{12,8},{1,5},{5,1},{9,13},{13,9},{2,6},{6,2},{1... | collective-permute-start | bytes 14155784 | tf_op jit(solution)/shard_map/ppermute | solution.py:593
  307.3 105.1 %collective-permute-start.34 = (bf16[2,4,96,3456]{3,2,1,0:T(8,128)(2,1)}, bf16[2,4,96,3456]{3,2,1,0:T(8,128)(2,1)}, u32[]{:S(2)}, u32[]{:S(2)}) collective-permute-start(bf16[2,4,96,3456]{3,2,1,0:T(8,128)(2,1)} %bitcast_dynamic-update-slice_fusion.5), channel_id=1, source_target_pairs={{0,4},{4,0},{8,12},{12,8},{1,5},{5,1},{9,13},{13,9},{2,6},{6,2},{1... | collective-permute-start | bytes 15925256 | tf_op jit(solution)/shard_map/ppermute | solution.py:593
  322.2 62.5 %collective-permute-start.1 = (bf16[256,1536]{1,0:T(8,128)(2,1)}, bf16[256,1536]{1,0:T(8,128)(2,1)S(1)}, u32[]{:S(2)}, u32[]{:S(2)}) collective-permute-start(bf16[256,1536]{1,0:T(8,128)(2,1)} %get-tuple-element.352), channel_id=1, source_target_pairs={{0,2},{1,3},{2,0},{3,1},{4,6},{5,7},{6,4},{7,5},{8,10},{9,11},{10,... | collective-permute-start | bytes 2359304 | tf_op jit(solution)/shard_map/ppermute | solution.py:659
  333.0 51.6 %collective-permute-start = (bf16[256,1536]{1,0:T(8,128)(2,1)}, bf16[256,1536]{1,0:T(8,128)(2,1)S(1)}, u32[]{:S(2)}, u32[]{:S(2)}) collective-permute-start(bf16[256,1536]{1,0:T(8,128)(2,1)} %get-tuple-element.353), channel_id=1, source_target_pairs={{0,1},{1,2},{2,3},{3,0},{4,5},{5,6},{6,7},{7,4},{8,9},{9,10},{10,1... | collective-permute-start | bytes 2359304 | tf_op jit(solution)/shard_map/ppermute | solution.py:659
  508.6 48.1 %collective-permute-start.50 = (bf16[256,1536]{1,0:T(8,128)(2,1)}, bf16[256,1536]{1,0:T(8,128)(2,1)}, u32[]{:S(2)}, u32[]{:S(2)}) collective-permute-start(bf16[256,1536]{1,0:T(8,128)(2,1)} %get-tuple-element.161), channel_id=1, source_target_pairs={{0,16},{1,17},{2,18},{3,19},{4,20},{5,21},{6,22},{7,23},{8,24},{9,... | collective-permute-start | bytes 2359304 | tf_op jit(solution)/shard_map/ppermute | solution.py:751
  722.3 229.3 %collective-permute-start.55 = (bf16[256,1536]{1,0:T(8,128)(2,1)}, bf16[256,1536]{1,0:T(8,128)(2,1)}, u32[]{:S(2)}, u32[]{:S(2)}) collective-permute-start(bf16[256,1536]{1,0:T(8,128)(2,1)} %get-tuple-element.343), channel_id=1, source_target_pairs={{0,3},{1,0},{2,1},{3,2},{4,7},{5,4},{6,5},{7,6},{8,11},{9,8},{10,9... | collective-permute-start | bytes 2359304 | tf_op jit(solution)/shard_map/ppermute | solution.py:659
  722.3 227.4 %collective-permute-start.54 = (bf16[256,1536]{1,0:T(8,128)(2,1)}, bf16[256,1536]{1,0:T(8,128)(2,1)}, u32[]{:S(2)}, u32[]{:S(2)}) collective-permute-start(bf16[256,1536]{1,0:T(8,128)(2,1)} %get-tuple-element.344), channel_id=1, source_target_pairs={{0,2},{1,3},{2,0},{3,1},{4,6},{5,7},{6,4},{7,5},{8,10},{9,11},{10,... | collective-permute-start | bytes 2359304 | tf_op jit(solution)/shard_map/ppermute | solution.py:659
  722.3 226.1 %collective-permute-start.53 = (bf16[256,1536]{1,0:T(8,128)(2,1)}, bf16[256,1536]{1,0:T(8,128)(2,1)}, u32[]{:S(2)}, u32[]{:S(2)}) collective-permute-start(bf16[256,1536]{1,0:T(8,128)(2,1)} %get-tuple-element.345), channel_id=1, source_target_pairs={{0,1},{1,2},{2,3},{3,0},{4,5},{5,6},{6,7},{7,4},{8,9},{9,10},{10,1... | collective-permute-start | bytes 2359304 | tf_op jit(solution)/shard_map/ppermute | solution.py:659
  808.4 50.5 %collective-permute-start.56 = (bf16[256,1536]{1,0:T(8,128)(2,1)}, bf16[256,1536]{1,0:T(8,128)(2,1)}, u32[]{:S(2)}, u32[]{:S(2)}) collective-permute-start(bf16[256,1536]{1,0:T(8,128)(2,1)} %get-tuple-element.191), channel_id=1, source_target_pairs={{16,0},{17,1},{18,2},{19,3},{20,4},{21,5},{22,6},{23,7},{24,8},{25... | collective-permute-start | bytes 2359304 | tf_op jit(solution)/shard_map/ppermute | solution.py:777
  809.7 49.2 %collective-permute-start.57 = (bf16[256,1536]{1,0:T(8,128)(2,1)}, bf16[256,1536]{1,0:T(8,128)(2,1)}, u32[]{:S(2)}, u32[]{:S(2)}) collective-permute-start(bf16[256,1536]{1,0:T(8,128)(2,1)} %get-tuple-element.199), channel_id=1, source_target_pairs={{16,0},{17,1},{18,2},{19,3},{20,4},{21,5},{22,6},{23,7},{24,8},{25... | collective-permute-start | bytes 2359304 | tf_op jit(solution)/shard_map/ppermute | solution.py:777
  945.7 77.7 %collective-permute-start.58 = (bf16[256,1536]{1,0:T(8,128)(2,1)}, bf16[256,1536]{1,0:T(8,128)(2,1)S(1)}, u32[]{:S(2)}, u32[]{:S(2)}) collective-permute-start(bf16[256,1536]{1,0:T(8,128)(2,1)} %get-tuple-element.213), channel_id=1, source_target_pairs={{16,0},{17,1},{18,2},{19,3},{20,4},{21,5},{22,6},{23,7},{24,8},{25... | collective-permute-start | bytes 2359304 | tf_op jit(solution)/shard_map/ppermute | solution.py:777
  1070.7 58.4 %collective-permute-start.96 = (f32[169,128]{1,0:T(8,128)S(1)}, f32[169,128]{1,0:T(8,128)S(1)}, u32[]{:S(2)}, u32[]{:S(2)}) collective-permute-start(f32[169,128]{1,0:T(8,128)S(1)} %bitcast.398), channel_id=1, source_target_pairs={{0,4},{4,0},{8,12},{12,8},{1,5},{5,1},{9,13},{13,9},{2,6},{6,2},{1... | collective-permute-start | bytes 259592 | tf_op jit(solution)/shard_map/ppermute | solution.py:556
  1082.3 164.1 %collective-permute-start.63 = (bf16[2,4,96,3072]{3,2,1,0:T(8,128)(2,1)}, bf16[2,4,96,3072]{3,2,1,0:T(8,128)(2,1)}, u32[]{:S(2)}, u32[]{:S(2)}) collective-permute-start(bf16[2,4,96,3072]{3,2,1,0:T(8,128)(2,1)} %bitcast.96), channel_id=1, source_target_pairs={{0,4},{4,0},{8,12},{12,8},{1,5},{5,1},{9,13},{13,9},{2,6},{6,2},{1... | collective-permute-start | bytes 14155784 | tf_op jit(solution)/shard_map/ppermute | solution.py:603
  1118.8 144.8 %collective-permute-start.74 = (bf16[2,4,96,3456]{3,2,1,0:T(8,128)(2,1)}, bf16[2,4,96,3456]{3,2,1,0:T(8,128)(2,1)}, u32[]{:S(2)}, u32[]{:S(2)}) collective-permute-start(bf16[2,4,96,3456]{3,2,1,0:T(8,128)(2,1)} %bitcast.113), channel_id=1, source_target_pairs={{0,4},{4,0},{8,12},{12,8},{1,5},{5,1},{9,13},{13,9},{2,6},{6,2},{1... | collective-permute-start | bytes 15925256 | tf_op jit(solution)/shard_map/ppermute | solution.py:603
  1125.8 110.3 %collective-permute-start.85 = (bf16[2,4,192,1536]{3,2,1,0:T(8,128)(2,1)}, bf16[2,4,192,1536]{3,2,1,0:T(8,128)(2,1)}, u32[]{:S(2)}, u32[]{:S(2)}) collective-permute-start(bf16[2,4,192,1536]{3,2,1,0:T(8,128)(2,1)} %bitcast.129), channel_id=1, source_target_pairs={{0,4},{4,0},{8,12},{12,8},{1,5},{5,1},{9,13},{13,9},{2,6},{6,2},{1... | collective-permute-start | bytes 14155784 | tf_op jit(solution)/shard_map/ppermute | solution.py:603
  1144.6 55.4 %collective-permute-start.61 = (bf16[256,1536]{1,0:T(8,128)(2,1)}, bf16[256,1536]{1,0:T(8,128)(2,1)S(1)}, u32[]{:S(2)}, u32[]{:S(2)}) collective-permute-start(bf16[256,1536]{1,0:T(8,128)(2,1)} %get-tuple-element.308), channel_id=1, source_target_pairs={{0,2},{1,3},{2,0},{3,1},{4,6},{5,7},{6,4},{7,5},{8,10},{9,11},{10,... | collective-permute-start | bytes 2359304 | tf_op jit(solution)/shard_map/ppermute | solution.py:659
  1256.3 58.6 %collective-permute-start.65 = (bf16[96,3072]{1,0:T(8,128)(2,1)}, bf16[96,3072]{1,0:T(8,128)(2,1)S(1)}, u32[]{:S(2)}, u32[]{:S(2)}) collective-permute-start(bf16[96,3072]{1,0:T(8,128)(2,1)} %get-tuple-element.332), channel_id=1, source_target_pairs={{0,8},{4,12},{8,0},{12,4},{1,9},{5,13},{9,1},{13,5},{2,10},{6,14},... | collective-permute-start | bytes 1769480 | tf_op jit(solution)/shard_map/ppermute | solution.py:613
  (193 other events, 3954.0 us)

commit v2 on v1

--- a/solution.py
+++ b/solution.py
@@ -17,9 +17,9 @@
 GROUP = 8
 WIDTH = GROUP * HEAD_DIM
 GROUPS = HEADS // GROUP
-OUT_TILE = 256
 LANES = 128
 EPS = 1e-05
+LOG2_E = 1.4426950408889634
 f32 = jnp.float32
 bf16 = jnp.bfloat16
 VMEM_LIMIT = 56 * 2**20
@@ -45,7 +45,7 @@
 
 
 def sigmoid(v):
-    return 1.0 / (1.0 + jnp.exp(-v))
+    return 0.5 * jnp.tanh(0.5 * v) + 0.5
 
 
 def head_steps(step_raw, head_rows):
@@ -59,32 +59,48 @@
     return dot(ones, value, NN, lax.Precision.HIGHEST)
 
 
-def conv_pre(ext_ref, taps, length, width):
-    summed = taps[CONV : CONV + 1]
+def earlier_rows(tail, rows):
+    joined = jnp.concatenate([tail[8:16].astype(f32), rows], axis=0)
+    shifted = [pltpu.roll(joined, shift, 0)[8:] for shift in range(CONV - 1, 0, -1)]
+    return shifted + [rows]
+
+
+def later_rows(rows, head):
+    length = rows.shape[0]
+    joined = jnp.concatenate([rows, head], axis=0)
+    shifted = [pltpu.roll(joined, length + 8 - shift, 0)[:length] for shift in range(CONV - 1, 0, -1)]
+    return shifted + [rows]
+
+
+def conv_sum(taps, shifted, start=0.0):
     for j in range(CONV):
-        summed = summed + ext_ref[5 + j : 5 + j + length, 0:width] * taps[j : j + 1]
-    return summed
-
-
-def fill_ext(ext_ref, tail, rows, length, width):
-    ext_ref[0:8, 0:width] = tail[8:16].astype(f32)
-    ext_ref[8 : 8 + length, 0:width] = rows
+        start = start + shifted[j] * taps[j : j + 1]
+    return start
+
+
+def chosen(flag, own, other):
+    return jnp.where(flag == 1, own[...].astype(f32), other[...].astype(f32))
+
+
+def chosen_grad(flag, own, other):
+    other_or_zero = jnp.where(flag == 0, other[...].astype(f32), 0.0)
+    return jnp.where(flag == 1, own[...].astype(f32), other_or_zero)
 
 
 def fwd_body(
-    h_ref, h_tile, ngain, wg, wc, wbc, wo, taps, taps_bc, head_rows, skip, gate_gain, spread, tail_in,
+    flag, own_ref, other_ref, ngain, wg, wc, wbc, wo, taps, taps_bc, head_rows, skip, gate_gain, spread, tail_in,
     tail_bc_in, state_in,
     normed_o, gate_o, cin_o, cin_bc_o, step_o, ssm_o, state_o, gout_o, r_o, branch_o, out_o,
     tail_o, tail_bc_o,
-    u_s, ssq_s, k_s, c_s, bt_s, dt_s, ec_s, w_s, cum_s, cumt_s, ext_s,
+    u_s, ssq_s, k_s, c_s, bt_s, dt_s, ec_s, w_s, cum_s, cumt_s,
 ):
     step = pl.program_id(0)
-    length = h_ref.shape[0]
+    length = own_ref.shape[0]
     half = length // 2
 
     @pl.when(step == 0)
     def _():
-        h = h_ref[...].astype(f32)
+        h = chosen(flag[0, 0], own_ref, other_ref)
         scale = lax.rsqrt(jnp.mean(h * h, axis=1, keepdims=True) + EPS)
         normed = (h * scale * ngain[...]).astype(bf16)
         normed_o[...] = normed
@@ -94,8 +110,9 @@
         conv_in = projected[:, :BC].astype(bf16)
         cin_bc_o[...] = conv_in
         tail_bc_o[...] = conv_in[length - 16 :]
-        fill_ext(ext_s, tail_bc_in[...], conv_in.astype(f32), length, BC)
-        pre = conv_pre(ext_s, taps_bc[...], length, BC)
+        tap_rows = taps_bc[...]
+        shifted = earlier_rows(tail_bc_in[...], conv_in.astype(f32))
+        pre = conv_sum(tap_rows, shifted, tap_rows[CONV : CONV + 1])
         act = (pre * sigmoid(pre)).astype(bf16)
         b_rows, c_rows = act[:, :STATE], act[:, STATE:]
         c_s[...] = c_rows
@@ -108,9 +125,10 @@
         ec_s[...] = halves(jnp.exp(cum))
         w_s[...] = halves(dt * jnp.exp(total - cum))
         for g in range(GROUPS):
-            cum_s[g] = cum[:, g * GROUP : (g + 1) * GROUP]
-        cumt_s[...] = cum.T
+            cum_s[g] = cum[:, g * GROUP : (g + 1) * GROUP] * LOG2_E
+        cumt_s[...] = (cum * LOG2_E).T
         ssq_s[...] = jnp.zeros_like(ssq_s)
+        branch_o[...] = jnp.zeros_like(branch_o)
 
     @pl.when(step < GROUPS)
     def _():
@@ -120,8 +138,9 @@
         conv_in = dot(normed, wc[...], NN).astype(bf16)
         cin_o[...] = conv_in
         tail_o[...] = conv_in[length - 16 :]
-        fill_ext(ext_s, tail_in[...], conv_in.astype(f32), length, WIDTH)
-        pre = conv_pre(ext_s, taps[...], length, WIDTH)
+        tap_rows = taps[...]
+        shifted = earlier_rows(tail_in[...], conv_in.astype(f32))
+        pre = conv_sum(tap_rows, shifted, tap_rows[CONV : CONV + 1])
         act = (pre * sigmoid(pre)).astype(bf16).astype(f32)
         where = spread[...]
         x_dt = (act * dot(dt_s[...], where, NN)).astype(bf16)
@@ -141,9 +160,9 @@
             results = []
             for i in (2 * pair, 2 * pair + 1):
                 col, row = cum[:, i : i + 1], cumt[i : i + 1, :]
-                top = jnp.exp(jnp.where(mask, col[:half] - row[:, :half], -1e30))
-                low_left = jnp.exp(col[half:] - row[:, :half])
-                low_right = jnp.exp(jnp.where(mask, col[half:] - row[:, half:], -1e30))
+                top = jnp.exp2(jnp.where(mask, col[:half] - row[:, :half], -1e30))
+                low_left = jnp.exp2(col[half:] - row[:, :half])
+                low_right = jnp.exp2(jnp.where(mask, col[half:] - row[:, half:], -1e30))
                 top = (top * k[:half, :half]).astype(bf16)
                 low = jnp.concatenate(
                     [
@@ -160,41 +179,43 @@
         ssm = within + carried + skip[...] * act
         ssm_o[...] = ssm
         u = ssm * (gate * sigmoid(gate))
-        u_s[:, pl.ds(pl.multiple_of(step * WIDTH, WIDTH), WIDTH)] = u
+        gained = u * gate_gain[...]
+        u_s[:, pl.ds(pl.multiple_of(step * WIDTH, WIDTH), WIDTH)] = gained
         ssq_s[...] += jnp.sum(u * u, axis=1, keepdims=True)
+        branch_o[...] += dot(gained.astype(bf16), wo[...], NN)
 
     @pl.when(step == GROUPS)
     def _():
         r = lax.rsqrt(ssq_s[...] * (1.0 / DI) + EPS)
         r_o[...] = r
+        r = r[:, 0:1]
         for g in range(GROUPS):
             cols = slice(g * WIDTH, (g + 1) * WIDTH)
-            gout_o[:, cols] = (u_s[:, cols] * r[:, 0:1] * gate_gain[:, cols]).astype(bf16)
-
-    @pl.when(step >= GROUPS)
-    def _():
-        branch = dot(gout_o[...], wo[...], NN)
+            gout_o[:, cols] = (u_s[:, cols] * r).astype(bf16)
+        branch = branch_o[...] * r
         branch_o[...] = branch
-        out_o[...] = (h_tile[...].astype(f32) + branch).astype(bf16)
+        out_o[...] = (chosen(flag[0, 0], own_ref, other_ref) + branch).astype(bf16)
 
 
 def bwd_body(
-    h_ref, gout_ref, ngain, branch, r_ref, wo, wg, wc, wbc, taps, taps_bc, head_rows, skip,
+    flag, own_ref, other_ref, own_grad, other_grad, ngain, branch, r_ref, wo, wg, wc, wbc, taps, taps_bc, head_rows, skip,
     gate_gain, spread, gather, gate_ref, ssm_ref, cin, cin_bc, step_ref, tail_in, tail_bc_in,
     state_in, adj_in, next_in, next_bc_in,
-    gg_o, gc_o, gbc_o, gin_o, gin_low_o, adj_o, next_o, next_bc_o, chan_o, chan_bc_o, ngrad_o,
+    gout_ref, gg_o, gc_o, gin_o, gin_low_o, adj_o, next_o, next_bc_o, chan_o, chan_bc_o, ngrad_o,
     head_o,
     acc_s, kt_s, wt_s, b_s, c_s, ct_s, dt_s, ec_s, w_s, cum_s, cumt_s, db_s, dc_s, rows_s, cols_s,
-    direct_s, fresh_s, carry_s, edge_s, dsilu_s, q_s, ext_s, ext2_s,
+    direct_s, fresh_s, carry_s, edge_s, dsilu_s, q_s,
 ):
     step = pl.program_id(0)
-    length = h_ref.shape[0]
+    length = own_ref.shape[0]
     half = length // 2
 
     @pl.when(step == 0)
     def _():
-        fill_ext(ext_s, tail_bc_in[...], cin_bc[...].astype(f32), length, BC)
-        pre = conv_pre(ext_s, taps_bc[...], length, BC)
+        gout_ref[...] = chosen_grad(flag[0, 1], own_grad, other_grad).astype(bf16)
+        tap_rows = taps_bc[...]
+        shifted = earlier_rows(tail_bc_in[...], cin_bc[...].astype(f32))
+        pre = conv_sum(tap_rows, shifted, tap_rows[CONV : CONV + 1])
         sig = sigmoid(pre)
         dsilu_s[...] = sig * (1.0 + pre * (1.0 - sig))
         act = (pre * sig).astype(bf16)
@@ -210,8 +231,8 @@
         ec_s[...] = halves(jnp.exp(cum))
         w_s[...] = halves(jnp.exp(total - cum))
         for g in range(GROUPS):
-            cum_s[g] = cum[:, g * GROUP : (g + 1) * GROUP]
-        cumt_s[...] = cum.T
+            cum_s[g] = cum[:, g * GROUP : (g + 1) * GROUP] * LOG2_E
+        cumt_s[...] = (cum * LOG2_E).T
         for ref in (acc_s, wt_s, db_s, dc_s, rows_s, cols_s, direct_s, fresh_s, carry_s, edge_s):
             ref[...] = jnp.zeros_like(ref)
         rowdot = jnp.sum(branch[...] * gout_ref[...].astype(f32), axis=1, keepdims=True)
@@ -230,9 +251,9 @@
         grad_ssm = grad_u * silu
         grad_gate = (grad_u * ssm * (sig * (1.0 + gate * (1.0 - sig)))).astype(bf16)
         gg_o[...] = grad_gate
-        conv_in = cin[...].astype(f32)
-        fill_ext(ext_s, tail_in[...], conv_in, length, WIDTH)
-        pre = conv_pre(ext_s, taps[...], length, WIDTH)
+        tap_rows = taps[...]
+        shifted = earlier_rows(tail_in[...], cin[...].astype(f32))
+        pre = conv_sum(tap_rows, shifted, tap_rows[CONV : CONV + 1])
         sig = sigmoid(pre)
         act = (pre * sig).astype(bf16).astype(f32)
         dsilu = sig * (1.0 + pre * (1.0 - sig))
@@ -251,7 +272,7 @@
         last = ec[length - 1 : length]
         adj_o[...] = last * adj + dot(ct_s[...], g_ec, NN)
         edge = last * jnp.sum(state * adj, axis=0, keepdims=True)
-        edge_s[...] += dot(halves(edge), pick, NN)
+        edge_s[...] += dot(edge.astype(bf16), pick, NN)
         cum = cum_s[step]
         start = pl.multiple_of(step * GROUP, GROUP)
         cumt = cumt_s[pl.ds(start, GROUP), :]
@@ -272,9 +293,9 @@
                 col, row = cum[:, i : i + 1], cumt[i : i + 1, :]
                 mine = left_lane if i % 2 == 0 else jnp.logical_not(left_lane)
                 x_head = jnp.where(mine, x_pair, jnp.zeros_like(x_pair))
-                l_tl = jnp.exp(jnp.where(mask, row[:, :half] - col[:half], -1e30))
-                l_tr = jnp.exp(row[:, half:] - col[:half])
-                l_br = jnp.exp(jnp.where(mask, row[:, half:] - col[half:], -1e30))
+                l_tl = jnp.exp2(jnp.where(mask, row[:, :half] - col[:half], -1e30))
+                l_tr = jnp.exp2(row[:, half:] - col[:half])
+                l_br = jnp.exp2(jnp.where(mask, row[:, half:] - col[half:], -1e30))
                 lk_tl, lk_tr, lk_br = (
                     l_tl * kt[:half, :half],
                     l_tr * kt[:half, half:],
@@ -316,23 +337,16 @@
         rows_s[...] = row_sums
         cols_s[pl.ds(start, GROUP), :] = jnp.concatenate(col_sums, axis=0)
         mixed_grad = jnp.concatenate(pieces, axis=1) + from_adj
-        direct_s[...] += dot(halves(act * mixed_grad), pick, NN)
-        fresh_s[...] += dot(halves(x_dt * from_adj), pick, NN)
-        carry_s[...] += dot(halves(grad_ssm * carried), pick, NN)
+        direct_s[...] += dot((act * mixed_grad).astype(bf16), pick, NN)
+        fresh_s[...] += dot((x_dt * from_adj).astype(bf16), pick, NN)
+        carry_s[...] += dot((grad_ssm * carried).astype(bf16), pick, NN)
         grad_pre = (dt * mixed_grad + skip[...] * grad_ssm) * dsilu
         next_o[...] = grad_pre[0:8]
-        ext2_s[0:length] = grad_pre
-        ext2_s[length : length + 8] = next_in[...]
-        tap_rows = taps[...]
-        grad_conv = grad_pre * tap_rows[CONV - 1 : CONV]
-        for j in range(CONV - 1):
-            shift = CONV - 1 - j
-            grad_conv = grad_conv + ext2_s[shift : shift + length] * tap_rows[j : j + 1]
+        grad_conv = conv_sum(tap_rows, later_rows(grad_pre, next_in[...]))
         grad_conv = grad_conv.astype(bf16)
-        gc_o[...] = grad_conv
+        gc_o[:, pl.ds(pl.multiple_of(step * WIDTH, WIDTH), WIDTH)] = grad_conv
         sums = [
-            jnp.sum(grad_pre * ext_s[5 + j : 5 + j + length], axis=0, keepdims=True)
-            for j in range(CONV)
+            jnp.sum(grad_pre * rows, axis=0, keepdims=True) for rows in shifted
         ]
         sums += [jnp.sum(grad_pre, axis=0, keepdims=True), gain_grad, skip_grad]
         chan_o[...] = jnp.concatenate(sums + [jnp.zeros_like(skip_grad)], axis=0)
@@ -345,17 +359,11 @@
         grad_c = dc_s[...] + dot(wt, b_s[...], TN)
         grad_pre = jnp.concatenate([grad_b, grad_c], axis=1) * dsilu_s[...]
         next_bc_o[...] = grad_pre[0:8]
-        ext2_s[0:length, 0:BC] = grad_pre
-        ext2_s[length : length + 8, 0:BC] = next_bc_in[...]
-        fill_ext(ext_s, tail_bc_in[...], cin_bc[...].astype(f32), length, BC)
         tap_rows = taps_bc[...]
-        grad_conv = grad_pre * tap_rows[CONV - 1 : CONV]
-        for j in range(CONV - 1):
-            shift = CONV - 1 - j
-            grad_conv = grad_conv + ext2_s[shift : shift + length, 0:BC] * tap_rows[j : j + 1]
+        grad_conv = conv_sum(tap_rows, later_rows(grad_pre, next_bc_in[...]))
+        shifted = earlier_rows(tail_bc_in[...], cin_bc[...].astype(f32))
         sums = [
-            jnp.sum(grad_pre * ext_s[5 + j : 5 + j + length, 0:BC], axis=0, keepdims=True)
-            for j in range(CONV)
+            jnp.sum(grad_pre * rows, axis=0, keepdims=True) for rows in shifted
         ]
         sums += [jnp.sum(grad_pre, axis=0, keepdims=True)]
         chan_bc_o[...] = jnp.concatenate(sums + [jnp.zeros((3, BC), f32)], axis=0)
@@ -381,9 +389,9 @@
             axis=0,
         )
         low = jnp.concatenate([grad_conv.astype(bf16), grad_step.astype(bf16)], axis=1)
-        gbc_o[...] = low
+        gc_o[:, DI:] = low
         grad_normed = acc_s[...] + dot(low, wbc[...], NT)
-        h = h_ref[...].astype(f32)
+        h = chosen(flag[0, 0], own_ref, other_ref)
         scale = lax.rsqrt(jnp.mean(h * h, axis=1, keepdims=True) + EPS)
         ngrad_o[...] = jnp.sum(grad_normed * h * scale, axis=0, keepdims=True)
         weighted = grad_normed * ngain[...]
@@ -405,31 +413,32 @@
     return pl.BlockSpec(shape, lambda i: (0,) * len(shape))
 
 
-def by_group(rows, width=WIDTH):
-    return pl.BlockSpec((rows, width), lambda i: (0, jnp.minimum(i, GROUPS - 1)))
-
-
-def tail_of(rows, width):
-    return pl.BlockSpec((rows, width), lambda i: (0, DI // width))
+def by_group(rows, width=WIDTH, skip=0):
+    return pl.BlockSpec((rows, width), lambda i: (0, jnp.minimum(i, GROUPS - 1) + skip))
+
+
+def tail_of(rows, width, at):
+    return pl.BlockSpec((rows, width), lambda i: (0, at // width))
 
 
 def gather_table():
-    table = np.zeros((GROUPS, 2, WIDTH, LANES), np.float32)
+    table = np.zeros((GROUPS, WIDTH, LANES), np.float32)
     for group in range(GROUPS):
         for column in range(WIDTH):
-            table[group, :, column, group * GROUP + column // HEAD_DIM] = 1.0
+            table[group, column, group * GROUP + column // HEAD_DIM] = 1.0
     return table.reshape(-1, LANES)
 
 
-def fwd_call(h, params, weights, state, tail, tail_bc):
-    length = h.shape[0]
-    wg, wc, wo = weights
-    out_tiles = D // OUT_TILE
-    by_out = pl.BlockSpec((length, OUT_TILE), lambda i: (0, jnp.maximum(i - GROUPS, 0)))
+FLAGS = pl.BlockSpec(memory_space=pltpu.SMEM)
+
+
+def fwd_call(flag, own, other, params, weights, state, tail, tail_bc):
+    length = own.shape[0]
+    win, wo = weights
     in_specs = [
-        whole((length, D)), by_out, whole((1, D)), by_group(D), by_group(D), tail_of(D, TAIL),
-        pl.BlockSpec((DI, OUT_TILE), lambda i: (0, jnp.maximum(i - GROUPS, 0))),
-        by_group(8), tail_of(8, BC), whole((8, LANES)), by_group(1), whole((1, DI)),
+        FLAGS, whole((length, D)), whole((length, D)), whole((1, D)), by_group(D), by_group(D, WIDTH, GROUPS), tail_of(D, TAIL, 2 * DI),
+        pl.BlockSpec((WIDTH, D), lambda i: (jnp.minimum(i, GROUPS - 1), 0)),
+        by_group(8), tail_of(8, BC, DI), whole((8, LANES)), by_group(1), by_group(1),
         by_group(2 * LANES), by_group(16), whole((16, BC)), by_group(STATE),
     ]
     out = [
@@ -442,8 +451,8 @@
         ((STATE, DI), f32, by_group(STATE)),
         ((length, DI), bf16, whole((length, DI))),
         ((length, LANES), f32, whole((length, LANES))),
-        ((length, D), f32, by_out),
-        ((length, D), bf16, by_out),
+        ((length, D), f32, whole((length, D))),
+        ((length, D), bf16, whole((length, D))),
         ((16, DI), bf16, by_group(16)),
         ((16, BC), bf16, whole((16, BC))),
     ]
@@ -451,11 +460,11 @@
         ((length, DI), f32), ((length, LANES), f32), ((length, length), f32),
         ((length, STATE), bf16), ((STATE, length), bf16), ((length, 2 * LANES), bf16),
         ((length, 2 * LANES), bf16), ((length, 2 * LANES), bf16), ((GROUPS, length, GROUP), f32),
-        ((LANES, length), f32), ((length + 8, WIDTH), f32),
+        ((LANES, length), f32),
     ]
     return pl.pallas_call(
         fwd_body,
-        grid=(GROUPS + out_tiles,),
+        grid=(GROUPS + 1,),
         in_specs=in_specs,
         out_specs=[spec for _, _, spec in out],
         out_shape=[jax.ShapeDtypeStruct(shape, dtype) for shape, dtype, _ in out],
@@ -466,28 +475,29 @@
         cost_estimate=pl.CostEstimate(flops=12 * 10**9, bytes_accessed=45 * 10**6, transcendentals=5 * 10**6),
         name="layer_forward",
     )(
-        h, h, params["norm_gain"], wg, wc, wc, wo, params["taps"], params["taps"],
+        flag, own, other, params["norm_gain"], win, win, win, wo, params["taps"], params["taps"],
         params["heads"], params["skip"], params["gate_gain"], params["spread"], tail, tail_bc, state,
     )
 
 
-def bwd_call(h, grad_out, kept, params, weights, adj, ahead, ahead_bc):
-    length = h.shape[0]
-    wg, wc, wo = weights
+def bwd_call(flag, own_grad, other_grad, kept, params, weights, adj, ahead, ahead_bc):
+    length = own_grad.shape[0]
+    win, wo = weights
     rows_of_wo = pl.BlockSpec((WIDTH, D), lambda i: (jnp.minimum(i, GROUPS - 1), 0))
-    pick = pl.BlockSpec((2 * WIDTH, LANES), lambda i: (jnp.minimum(i, GROUPS - 1), 0))
+    pick = pl.BlockSpec((WIDTH, LANES), lambda i: (jnp.minimum(i, GROUPS - 1), 0))
     in_specs = [
-        whole((length, D)), whole((length, D)), whole((1, D)), whole((length, D)),
-        whole((length, LANES)), rows_of_wo, by_group(D), by_group(D), tail_of(D, TAIL),
-        by_group(8), tail_of(8, BC), whole((8, LANES)), by_group(1), by_group(1),
+        FLAGS, whole((length, D)), whole((length, D)), whole((length, D)), whole((length, D)),
+        whole((1, D)), whole((length, D)),
+        whole((length, LANES)), rows_of_wo, by_group(D), by_group(D, WIDTH, GROUPS), tail_of(D, TAIL, 2 * DI),
+        by_group(8), tail_of(8, BC, DI), whole((8, LANES)), by_group(1), by_group(1),
         by_group(2 * LANES), pick, by_group(length), by_group(length), by_group(length),
         whole((length, BC)), whole((length, LANES)), by_group(16), whole((16, BC)),
         by_group(STATE), by_group(STATE), by_group(8), whole((8, BC)),
     ]
     out = [
+        ((length, D), bf16, whole((length, D))),
         ((length, DI), bf16, by_group(length)),
-        ((length, DI), bf16, by_group(length)),
-        ((length, TAIL), bf16, whole((length, TAIL))),
+        ((length, DI + TAIL), bf16, whole((length, DI + TAIL))),
         ((length, D), f32, whole((length, D))),
         ((length, D), bf16, whole((length, D))),
         ((STATE, DI), f32, by_group(STATE)),
@@ -505,8 +515,7 @@
         ((GROUPS, length, GROUP), f32), ((LANES, length), f32), ((length, STATE), f32),
         ((length, STATE), f32), ((length, LANES), f32), ((LANES, length), f32),
         ((length, LANES), f32), ((length, LANES), f32), ((length, LANES), f32), ((1, LANES), f32),
-        ((length, BC), f32), ((length, LANES), f32), ((length + 8, WIDTH), f32),
-        ((length + 8, WIDTH), f32),
+        ((length, BC), f32), ((length, LANES), f32),
     ]
     return pl.pallas_call(
         bwd_body,
@@ -521,7 +530,7 @@
         cost_estimate=pl.CostEstimate(flops=25 * 10**9, bytes_accessed=55 * 10**6, transcendentals=8 * 10**6),
         name="layer_backward",
     )(
-        h, grad_out, params["norm_gain"], kept["branch"], kept["r"], wo, wg, wc, wc,
+        flag, kept["own"], kept["other"], own_grad, other_grad, params["norm_gain"], kept["branch"], kept["r"], wo, win, win, win,
         params["taps"], params["taps"], params["heads"], params["skip"], params["gate_gain"],
         params["spread"], params["gather"], kept["gate"], kept["ssm"], kept["cin"], kept["cin_bc"],
         kept["step"], kept["tail"], kept["tail_bc"], kept["state"], adj, ahead, ahead_bc,
@@ -549,11 +558,17 @@
     return row
 
 
+def exchanges():
+    return [(axis, bit) for axis in ("dp", "seq") for bit in bits_of(lax.axis_size(axis))]
+
+
+def exchange(value, axis, bit):
+    return value + lax.ppermute(value, axis, xor_route(lax.axis_size(axis), bit))
+
+
 def sum_small(value):
-    for axis in ("dp", "seq"):
-        size = lax.axis_size(axis)
-        for bit in bits_of(size):
-            value = value + lax.ppermute(value, axis, xor_route(size, bit))
+    for axis, bit in exchanges():
+        value = exchange(value, axis, bit)
     return value
 
 
@@ -561,96 +576,137 @@
     return lax.axis_size("dp") == 4 and lax.axis_size("seq") == 4
 
 
-def pair_route(allowed):
-    return [(d * 4 + z, (d ^ 2) * 4 + z) for d in range(4) for z in range(4) if allowed(z)]
-
-
-def gather_rows(shard):
-    if not direct_paths():
-        return lax.all_gather(shard, ("dp", "seq"), axis=0, tiled=True)
-    rows, cols = shard.shape
-    dp, z = lax.axis_index("dp"), lax.axis_index("seq")
-    y, core = dp // 2, dp % 2
-    held = jnp.zeros((2, 4, rows, cols), shard.dtype)
-
-    def place(held, piece, at_y, at_z):
-        return lax.dynamic_update_slice(held, piece[None, None], (at_y, at_z, 0, 0))
-
-    up, down = shard, shard
-    beside = lax.ppermute(shard, "dp", xor_route(4, 2))
-    arrivals = []
-    for hop in range(1, 4):
-        up = lax.ppermute(up, "seq", [(i, i + 1) for i in range(hop - 1, 3)])
-        down = lax.ppermute(down, "seq", [(i, i - 1) for i in range(1, 5 - hop)])
-        up_beside = lax.ppermute(up, ("dp", "seq"), pair_route(lambda i: i >= hop))
-        down_beside = lax.ppermute(down, ("dp", "seq"), pair_route(lambda i: i <= 3 - hop))
-        arrivals.append((up, up_beside, jnp.where(z >= hop, z - hop, z)))
-        arrivals.append((down, down_beside, jnp.where(z + hop <= 3, z + hop, z)))
-    for piece, piece_beside, at in arrivals:
-        held = place(held, piece, y, at)
-        held = place(held, piece_beside, 1 - y, at)
-    held = place(place(held, beside, 1 - y, z), shard, y, z)
-    other = lax.ppermute(held, "dp", xor_route(4, 1))
-    full = jnp.where(
-        core == 0, jnp.stack([held, other], axis=1), jnp.stack([other, held], axis=1)
-    )
-    return full.reshape(16 * rows, cols)
-
-
-def reduce_rows(mine, rest):
+RING = 8
+
+
+def ring_place(position):
+    return jnp.where(position < 4, position, 11 - position)
+
+
+def ring_route(step):
+    def device(position, core):
+        y, z = (0, position) if position < 4 else (1, 7 - position)
+        return (y * 2 + core) * 4 + z
+
+    return [
+        (device(p, core), device((p + step) % RING, core)) for p in range(RING) for core in range(2)
+    ]
+
+
+def around(value, step):
+    return lax.ppermute(value, ("dp", "seq"), ring_route(step))
+
+
+def across(value):
+    return lax.ppermute(value, "dp", xor_route(4, 1))
+
+
+def own_position():
     dp, z = lax.axis_index("dp"), lax.axis_index("seq")
     y = dp // 2
-    from_core = lax.ppermute(rest(), "dp", xor_route(4, 1))
-    chip = mine(from_core)
-    order = jnp.array([[3, 2, 1, 0], [3, 2, 0, 1], [0, 1, 3, 2], [0, 1, 2, 3]], jnp.int32)[z]
-    sums = []
-    for j in range(4):
-        at = order[j]
-
-        def pick(at_y):
-            return lax.dynamic_slice(chip, (at_y, at, 0, 0), (1, 1) + chip.shape[2:])[0, 0]
-
-        arrived = lax.ppermute(pick(1 - y), "dp", xor_route(4, 2))
-        sums.append(pick(y).astype(f32) + arrived.astype(f32))
-
-    def up(value, hop):
-        return lax.ppermute(value.astype(bf16), "seq", [(i, i + 1) for i in range(hop)]).astype(f32)
-
-    def down(value, hop):
-        return lax.ppermute(
-            value.astype(bf16), "seq", [(i, i - 1) for i in range(4 - hop, 4)]
-        ).astype(f32)
-
-    up_1, down_1 = up(sums[0], 1), down(sums[0], 1)
-    up_2 = up(jnp.where(z == 0, sums[1], sums[0]) + up_1, 2)
-    down_2 = down(jnp.where(z == 3, sums[1], sums[0]) + down_1, 2)
-    up_3 = up(jnp.where(z == 1, sums[1], sums[2]) + up_2, 3)
-    down_3 = down(jnp.where(z == 2, sums[1], sums[2]) + down_2, 3)
-    return sums[3] + up_3 + down_3
-
-
-def weight_grad(left, right):
-    def term(columns):
+    return jnp.where(y == 0, z, 7 - z), dp % 2
+
+
+def together(up, down):
+    pairs = [lax.optimization_barrier(pair) for pair in zip(up, down)]
+    return [a for a, _ in pairs], [b for _, b in pairs]
+
+
+def gather_rows(shards):
+    if not direct_paths():
+        return [lax.all_gather(shard, ("dp", "seq"), axis=0, tiled=True) for shard in shards]
+    position, core = own_position()
+    held = [jnp.zeros((16,) + shard.shape, shard.dtype) for shard in shards]
+
+    def place(held, pieces, offset, start=0):
+        at = ring_place((position + offset) % RING)
+        at = (at // 4) * 8 + at % 4
+        others = [across(piece) for piece in pieces]
+        for of_core, values in ((core, pieces), (1 - core, others)):
+            held = [
+                lax.dynamic_update_slice(whole, value[None], (at + of_core * 4, start * rows, 0))
+                for whole, value, rows in zip(held, values, halves_of)
+            ]
+        return held
+
+    halves_of = [shard.shape[0] // 2 for shard in shards]
+    up, down = shards, shards
+    held = place(held, shards, 0)
+    for hop in range(1, 4):
+        up, down = [around(v, 1) for v in up], [around(v, -1) for v in down]
+        up, down = together(up, down)
+        held = place(place(held, up, -hop), down, hop)
+    up = [around(v[:rows], 1) for v, rows in zip(up, halves_of)]
+    down = [around(v[rows:], -1) for v, rows in zip(down, halves_of)]
+    held = place(place(held, up, 4), down, 4, 1)
+    return [whole.reshape((-1,) + whole.shape[2:]) for whole in held]
+
+
+def reduce_rows(chips, small, early):
+    position, _ = own_position()
+    hops = exchanges()
+
+    def term(chip, offset):
+        at = ring_place((position + offset) % RING)
+        return lax.dynamic_index_in_dim(chip, at, 0, keepdims=False)
+
+    half = [chip.shape[1] // 2 for chip in chips]
+    up = [around(term(chip, 4)[:rows], 1) for chip, rows in zip(chips, half)]
+    down = [around(term(chip, -4)[rows:], -1) for chip, rows in zip(chips, half)]
+    small = exchange(small, *hops[0])
+    up, down = together(up, down)
+    up[0], small, early = lax.optimization_barrier((up[0], small, early))
+    up = [jnp.pad(v, ((0, rows), (0, 0))) for v, rows in zip(up, half)]
+    down = [jnp.pad(v, ((rows, 0), (0, 0))) for v, rows in zip(down, half)]
+    for hop, offset in enumerate((3, 2, 1), 1):
+        up = [
+            around((term(chip, offset).astype(f32) + v.astype(f32)).astype(bf16), 1)
+            for chip, v in zip(chips, up)
+        ]
+        down = [
+            around((term(chip, -offset).astype(f32) + v.astype(f32)).astype(bf16), -1)
+            for chip, v in zip(chips, down)
+        ]
+        small = exchange(small, *hops[hop])
+        up, down = together(up, down)
+        up[0], small = lax.optimization_barrier((up[0], small))
+    sums = [
+        term(chip, 0).astype(f32) + a.astype(f32) + b.astype(f32)
+        for chip, a, b in zip(chips, up, down)
+    ]
+    return sums, small, early
+
+
+def weight_grads(pairs, small, early, ready):
+    def term(columns, right):
         return jnp.einsum("td,te->de", columns, right, preferred_element_type=f32)
 
-    dp, seq = lax.axis_size("dp"), lax.axis_size("seq")
     if not direct_paths():
-        return lax.optimization_barrier(
-            lax.psum_scatter(term(left), ("dp", "seq"), scatter_dimension=0, tiled=True)
+        sums = [
+            lax.optimization_barrier(
+                lax.psum_scatter(term(left, right), ("dp", "seq"), scatter_dimension=0, tiled=True)
+            )
+            for left, right in pairs
+        ]
+        return sums, sum_small(small), early, ready
+    core = lax.axis_index("dp") % 2
+
+    def owned(left, right, which):
+        quarter = left.shape[1] // 4
+        parts = [left[:, i * quarter : (i + 1) * quarter] for i in range(4)]
+        chosen = jnp.concatenate(
+            [jnp.where(which == 0, parts[0], parts[1]), jnp.where(which == 0, parts[2], parts[3])],
+            axis=1,
         )
-    rows = left.shape[1] // (dp * seq)
-    core = lax.axis_index("dp") % 2
-    by_core = left.reshape(left.shape[0], 2, 2, 4 * rows)
-    shape = (2, 4, rows, right.shape[1])
-
-    def owned(which):
-        chosen = jnp.where(which == 0, by_core[:, :, 0], by_core[:, :, 1])
-        return term(chosen.reshape(left.shape[0], 8 * rows))
-
-    return reduce_rows(
-        lambda arrived: (owned(core).reshape(shape) + arrived.astype(f32)).astype(bf16),
-        lambda: owned(1 - core).astype(bf16).reshape(shape),
-    )
+        return term(chosen, right).astype(bf16).reshape(RING, quarter // 4, right.shape[1])
+
+    arrived = [across(owned(left, right, 1 - core)) for left, right in pairs]
+    left, ready = lax.optimization_barrier((pairs[0][0], ready))
+    chips = [
+        (owned(left, right, core).astype(f32) + other.astype(f32)).astype(bf16)
+        for (_, right), other in zip(pairs, arrived)
+    ]
+    return *reduce_rows(chips, small, early), ready
 
 
 def turn(value, shift, parts):
@@ -678,10 +734,20 @@
     rank = lax.axis_index("seq") % parts
     stacked = jnp.stack(blocks)
     held = stacked
+    pieces = []
     for shift in range(parts):
         piece = lax.dynamic_index_in_dim(stacked, (rank + shift) % parts, 0, keepdims=False)
         if shift:
-            piece = turn(piece.astype(sent_type), shift, parts).astype(piece.dtype)
+            piece = turn(piece.astype(sent_type), shift, parts)
+        pieces.append(piece)
+    return stacked, pieces
+
+
+def laid_out(held, pieces):
+    parts = len(pieces)
+    rank = lax.axis_index("seq") % parts
+    for shift, piece in enumerate(pieces):
+        piece = piece.astype(held.dtype)
         held = lax.dynamic_update_slice(held, piece[None], ((rank - shift) % parts, 0, 0))
     return held
 
@@ -691,6 +757,10 @@
     "tail_out", "tail_bc_out",
 )
 SKEW = 2
+
+
+def flags(first, grad):
+    return jnp.stack([jnp.where(first, 1, 0), jnp.asarray(grad, jnp.int32)]).astype(jnp.int32)[None]
 
 
 def shards(
@@ -703,12 +773,11 @@
     owned = in_proj.shape[1]
     blocks_in = to_sequences(jnp.where(first, tokens, cotangent))
 
-    shard = in_proj[0]
-    shard_conv = jnp.pad(shard[:, DI:], ((0, 0), (0, TAIL - BC - HEADS)))
-    w_conv = gather_rows(shard_conv)
-    w_gate = gather_rows(shard[:, :DI])
-    w_out = gather_rows(out_proj[0])
-    weights = (w_gate, w_conv, w_out)
+    shard = jnp.pad(in_proj[0], ((0, 0), (0, TAIL - BC - HEADS)))
+    weights = (
+        lax.all_gather(shard, ("dp", "seq"), axis=0, tiled=True),
+        gather_rows([out_proj[0]])[0],
+    )
 
     sizes = [CONV * conv_bias.shape[1], conv_bias.shape[1], norm_gain.shape[1], gate_gain.shape[1]]
     packed = jnp.concatenate([conv_weight[0].reshape(-1), conv_bias[0], norm_gain[0], gate_gain[0]])
@@ -742,16 +811,17 @@
         for tick in range(ticks):
             if tick == SKEW:
                 carry = tuple(jnp.where(first, now, at) for now, at in zip(carry, start))
-            h = jnp.where(first, blocks_in[min(tick, parts - 1)], received[tick])
-            values = dict(zip(KEPT, fwd_call(h, params, weights, *carry)))
-            values.update(h=h, state=carry[0], tail=carry[1], tail_bc=carry[2])
+            own, other = blocks_in[min(tick, parts - 1)], received[tick]
+            values = dict(zip(KEPT, fwd_call(flags(first, 0), own, other, params, weights, *carry)))
+            values.update(own=own, other=other, state=carry[0], tail=carry[1], tail_bc=carry[2])
             carry = (values["state_out"], values["tail_out"], values["tail_bc_out"])
             kept.append(values)
             if tick < parts:
                 received.append(lax.ppermute(values["out"], "section", [(0, 1)]))
         return kept
 
-    def backward(kept, start):
+    def backward(kept, start, before_last=None):
+        early = None
         zeros = tuple(jnp.zeros_like(part) for part in start)
         carry = tuple(jnp.where(first, zero, at) for zero, at in zip(zeros, start))
         grads, received = [None] * ticks, [jnp.zeros((length, D), bf16)] * SKEW
@@ -760,24 +830,37 @@
                 carry = tuple(jnp.where(first, at, now) for now, at in zip(carry, start))
             if tick == parts:
                 carry = tuple(jnp.where(first, now, zero) for now, zero in zip(carry, zeros))
-            from_loss = blocks_in[parts - 1 - tick] if tick < parts else zeros_low
-            grad_out = jnp.where(first, received[tick], from_loss)
+            from_loss = blocks_in[max(parts - 1 - tick, 0)]
+            late = jnp.int32(2 if tick >= parts else 1)
+            if before_last is not None and tick == ticks - 1:
+                early = before_last(grads, received[tick])
+                from_loss, early = lax.optimization_barrier((from_loss, early))
             at = ticks - 1 - tick
             names = (
-                "gate", "conv", "tail", "in", "in_low", "adj", "next", "next_bc", "chan", "chan_bc",
+                "out", "gate", "conv", "in", "in_low", "adj", "next", "next_bc", "chan", "chan_bc",
                 "norm", "head",
             )
             values = dict(
-                zip(names, bwd_call(kept[at]["h"], grad_out, kept[at], params, weights, *carry))
+                zip(
+                    names,
+                    bwd_call(
+                        flags(first, jnp.where(first, 0, late)),
+                        from_loss,
+                        received[tick],
+                        kept[at],
+                        params,
+                        weights,
+                        *carry,
+                    ),
+                )
             )
-            values["out"] = grad_out
             carry = (values["adj"], values["next"], values["next_bc"])
             grads[at] = values
             if tick < parts:
-                received.append(lax.ppermute(values["in_low"], "section", [(1, 0)]))
-        return grads
-
-    zeros_low = jnp.zeros((length, D), bf16)
+                sent, received[-1] = lax.optimization_barrier((values["in_low"], received[-1]))
+                received.append(lax.ppermute(sent, "section", [(1, 0)]))
+        return grads, early
+
     start = (jnp.zeros((STATE, DI), f32), jnp.zeros((16, DI), bf16), jnp.zeros((16, BC), bf16))
     if hops > 1:
 
@@ -794,15 +877,17 @@
 
         start = lax.fori_loop(0, hops - 1, onward, start)
     kept = forward(start)
-    activations = to_pieces(
-        [jnp.where(first, kept[k]["out"], kept[k + SKEW]["out"]) for k in range(parts)], bf16
+    activations = laid_out(
+        *to_pieces(
+            [jnp.where(first, kept[k]["out"], kept[k + SKEW]["out"]) for k in range(parts)], bf16
+        )
     )[None]
 
     start = (jnp.zeros((STATE, DI), f32), jnp.zeros((8, DI), f32), jnp.zeros((8, BC), f32))
     if hops > 1:
 
         def back(_, start):
-            grads = backward(kept, start)
+            grads, _ = backward(kept, start)
             ends = (
                 tuple(grads[0][name] for name in ("adj", "next", "next_bc")),
                 tuple(grads[SKEW][name] for name in ("adj", "next", "next_bc")),
@@ -813,60 +898,68 @@
             )
 
         start = lax.fori_loop(0, hops - 1, back, start)
-    grads = backward(kept, start)
-
     def select(values, name):
         return jnp.concatenate(
             [jnp.where(first, values[k][name], values[k + SKEW][name]) for k in range(parts)], axis=0
         )
 
-    normed, gate_out = select(kept, "normed"), select(kept, "gout")
-    grad_out_proj = weight_grad(gate_out, select(grads, "out"))[None]
-    grad_gate = weight_grad(normed, select(grads, "gate"))
-    grad_conv = weight_grad(
-        normed, jnp.concatenate([select(grads, "conv"), select(grads, "tail")], axis=1)
-    )
-    grad_in_proj = jnp.concatenate([grad_gate, grad_conv[:, : DI + BC + HEADS]], axis=1)[None]
-    input_grads = to_pieces(
-        [jnp.where(first, grads[k]["in"], grads[k + SKEW]["in"]) for k in range(parts)], bf16
-    )[None]
-
+    def out_term(grads, received):
+        branch_grads = [jnp.where(first, received, blocks_in[0])] + [
+            jnp.where(first, grads[k]["out"], grads[k + SKEW]["out"]) for k in range(1, parts)
+        ]
+        return jnp.einsum(
+            "td,te->de",
+            select(kept, "gout"),
+            jnp.concatenate(branch_grads, axis=0),
+            preferred_element_type=f32,
+        ).astype(bf16)
+
+    grads, term = backward(kept, start, out_term)
+    grad_out_proj = lax.psum_scatter(
+        term, ("dp", "seq"), scatter_dimension=0, tiled=True
+    ).astype(f32)
+    normed = select(kept, "normed")
     def total(name):
         return sum(values[name] for values in grads)
 
     channels = jnp.concatenate([total("chan"), total("chan_bc")], axis=1)
-    norm = total("norm")
     head = total("head")
-    skip = channels[6, :DI].reshape(HEADS, HEAD_DIM).sum(axis=1)
-    small = jnp.concatenate(
-        [
-            channels[: CONV + 1].reshape(-1), channels[5, :DI], norm[0], head[0], head[1],
-            jnp.pad(skip, (0, LANES - HEADS)),
-        ]
+    last_row = jnp.concatenate([total("norm"), head[0:1], head[1:2]], axis=1)
+    fill = channels.shape[1] - last_row.shape[1]
+    small = (channels + jnp.pad(last_row, ((7, 0), (0, fill))))
+    held, pieces = to_pieces(
+        [jnp.where(first, grads[k]["in"], grads[k + SKEW]["in"]) for k in range(parts)], bf16
     )
-    small = sum_small(small.reshape(-1, LANES)).reshape(-1)
+    near = [pieces[1], pieces[-1]]
+    (grad_gate, grad_conv), small, grad_out_proj, near = weight_grads(
+        [(normed, select(grads, "gate")), (normed, select(grads, "conv"))],
+        small,
+        grad_out_proj,
+        near,
+    )
+    pieces[1], pieces[-1] = near
+    pieces, grad_gate = lax.optimization_barrier((pieces, grad_gate))
+    input_grads = laid_out(held, pieces)[None]
+    grad_in_proj = jnp.concatenate([grad_gate, grad_conv[:, : DI + BC + HEADS]], axis=1)[None]
+
     place = lax.axis_index("dp") * seq + lax.axis_index("seq")
 
     def mine(flat, width):
         return lax.dynamic_slice_in_dim(flat, place * width, width, axis=flat.ndim - 1)
 
     width = conv_bias.shape[1]
-    full = CONV * (DI + BC)
-    grad_taps = small[:full].reshape(CONV, -1)
-    grad_shift = small[full : full + DI + BC]
-    rest = small[full + DI + BC :]
     return (
         activations,
         input_grads,
         grad_in_proj,
-        grad_out_proj,
-        mine(grad_taps, width)[None],
-        mine(grad_shift, width)[None],
-        mine(rest[DI : DI + D], owned)[None],
-        mine(rest[:DI], gate_gain.shape[1])[None],
-        rest[DI + D : DI + D + HEADS][None],
-        rest[DI + D + LANES : DI + D + LANES + HEADS][None],
-        rest[DI + D + 2 * LANES : DI + D + 2 * LANES + HEADS][None],
+        grad_out_proj[None],
+        mine(small[:CONV], width)[None],
+        mine(small[CONV], width)[None],
+        mine(small[7, :D], owned)[None],
+        mine(small[5, :DI], gate_gain.shape[1])[None],
+        small[7:8, D : D + HEADS],
+        small[7:8, D + LANES : D + LANES + HEADS],
+        small[6, :DI].reshape(HEADS, HEAD_DIM).sum(axis=1)[None],
     )
 
 

time: 1440 us -> 968 us (0.67)
  starting transfers between devices: 236 us -> 106 us
  waiting for transfers between devices: 398 us -> 270 us
  local copies, waits for them, and re-layouts: 181 us -> 62.9 us
  other arithmetic: 107 us -> 67.3 us
  Pallas kernels: 424 us -> 385 us
  matrix products: 69.9 us -> 46.9 us
    ppermute x83 -> x43, waiting for transfers between devices: 297 us -> 130 us  [the longest x24 84.6 us: around(): return lax.ppermute(value, ('dp', 'seq'), ring_route(step))]
    ppermute x83 -> x43, starting transfers between devices: 170 us -> 70.8 us  [the longest x24 42.2 us: around(): return lax.ppermute(value, ('dp', 'seq'), ring_route(step))]
    unnamed x243 -> x175, local copies, waits for them, and re-layouts: 62.5 us -> 12.5 us
    select_n x9 -> x5, other arithmetic: 48.7 us -> 7.61 us  [the longest x2 4.95 us: out_term(): jnp.where(first, grads[k]['out'], grads[k + SKEW]['out'])]
    dot_general x6 -> x4, matrix products: 69.9 us -> 32.5 us  [term(): return jnp.einsum('td,te->de', columns, right, preferred_element_type=f32)]
    ppermute x9, starting transfers between devices: 47.1 us -> 18.4 us  [turn(): return lax.ppermute(value, 'seq', route)]
    all_gather x0 -> x1, waiting for transfers between devices: none -> 27 us  [shards(): lax.all_gather(shard, ('dp', 'seq'), axis=0, tiled=True)]
    dynamic_update_slice x47 -> x23, local copies, waits for them, and re-layouts: 48.4 us -> 24 us  [the longest x18 18.3 us: place(): lax.dynamic_update_slice(whole, value[None], (at + of_core * 4, start * r...]
  transfers between devices with their start and end apart: 100 -> 62, of which waited for: 38 -> 23; matrix products, arithmetic and copies ran while one was open for 18% -> 15% of each run, Pallas kernels for 19% -> 35%
where the time goes in v2:
time: 968 us; the launch traced here: 954 us
  Pallas kernels  385 us (40%)
  waiting for transfers between devices  270 us (28%)
  starting transfers between devices  106 us (11%)
  other arithmetic  67.3 us (7%)
  local copies, waits for them, and re-layouts  62.9 us (6%)
  matrix products  46.9 us (5%)
  between operations  16 us (2%)
    pallas_call x6, Pallas kernels, bwd_call(): pl.pallas_call(bwd_body, grid=(GROUPS + 1,), in_specs=in_specs, out_specs...  230 us
    pallas_call x6, Pallas kernels, fwd_call(): pl.pallas_call(fwd_body, grid=(GROUPS + 1,), in_specs=in_specs, out_specs...  156 us
    ppermute x24, waiting for transfers between devices, around(): return lax.ppermute(value, ('dp', 'seq'), ring_route(step))  84.6 us
    ppermute x9, waiting for transfers between devices, turn(): return lax.ppermute(value, 'seq', route)  84.5 us
    ppermute x24, starting transfers between devices, around(): return lax.ppermute(value, ('dp', 'seq'), ring_route(step))  42.2 us
    dot_general x4, matrix products, term(): return jnp.einsum('td,te->de', columns, right, preferred_element_type=f32)  32.5 us
    ppermute x4, waiting for transfers between devices, exchange(): lax.ppermute(value, axis, xor_route(lax.axis_size(axis), bit))  29.5 us
    ppermute x4, waiting for transfers between devices, gather_small(): other = lax.ppermute(row, axis, xor_route(size, bit))  28.2 us
  transfers between devices with their start and end apart: 62, of which 23 were waited for; matrix products, arithmetic and copies ran while one was open for 15% of the time, Pallas kernels for 35%

profile of v2, /device:TPU:0, one launch (start us, length us, event | category | flops | bytes accessed | tf_op | source)
XLA Modules:
  0.0 954.4 jit_solution(15539555979913786916)
XLA Ops:
  34.5 21.9 %collective-permute-done.4 = bf16[2,1328]{1,0:T(2,128)(2,1)S(1)} collective-permute-done((bf16[2,1328]{1,0:T(2,128)(2,1)S(1)}, bf16[2,1328]{1,0:T(2,128)(2,1)S(1)}, u32[]{:S(2)}, u32[]{:S(2)}) %collective-permute-start.4) | collective-permute-done | bytes 5344 | tf_op jit(solution)/shard_map/ppermute | solution.py:552
  73.5 53.3 %collective-permute-done.1 = bf16[256,1536]{1,0:T(8,128)(2,1)S(1)} collective-permute-done((bf16[256,1536]{1,0:T(8,128)(2,1)}, bf16[256,1536]{1,0:T(8,128)(2,1)S(1)}, u32[]{:S(2)}, u32[]{:S(2)}) %collective-permute-start.1) | collective-permute-done | bytes 786464 | tf_op jit(solution)/shard_map/ppermute | solution.py:715
  133.1 18.4 %collective-permute-start.16 = (bf16[192,1536]{1,0:T(8,128)(2,1)S(1)}, bf16[192,1536]{1,0:T(8,128)(2,1)S(1)}, u32[]{:S(2)}, u32[]{:S(2)}) collective-permute-start(bf16[192,1536]{1,0:T(8,128)(2,1)S(1)} %collective-permute-done.12), channel_id=1, source_target_pairs={{0,1},{4,5},{1,2},{5,6},{2,3},{6,7},{3,11},{7,15},{11,10},{15,14},... | collective-permute-start | bytes 1769480 | tf_op jit(solution)/shard_map/ppermute | solution.py:597
  156.5 14.3 %collective-permute-done.16 = bf16[192,1536]{1,0:T(8,128)(2,1)S(1)} collective-permute-done((bf16[192,1536]{1,0:T(8,128)(2,1)S(1)}, bf16[192,1536]{1,0:T(8,128)(2,1)S(1)}, u32[]{:S(2)}, u32[]{:S(2)}) %collective-permute-start.16) | collective-permute-done | bytes 589856 | tf_op jit(solution)/shard_map/ppermute | solution.py:597
  193.7 27.0 %all-gather.2.cloned.1.call-done.wg.wc.wbc = bf16[1536,6528]{1,0:T(8,128)(2,1)} async-done(((bf16[96,6528]{1,0:T(8,128)(2,1)}), bf16[1536,6528]{1,0:T(8,128)(2,1)}) %all-gather.2.cloned.1.call-update) | async-done | bytes 20054032 | tf_op jit(solution)/shard_map/all_gather | solution.py:778
  224.1 25.9 %layer_forward.6 = (bf16[256,1536]{1,0:T(8,128)(2,1)}, f32[256,3072]{1,0:T(8,128)}, bf16[256,3072]{1,0:T(8,128)(2,1)}, bf16[256,256]{1,0:T(8,128)(2,1)}, f32[256...) custom-call(s32[1,2]{1,0:T(1,128)} %add_bitcast_fusion.flag, ...), custom_call_target="tpu_custom_call" | custom-call | flops 12000000000 | bytes 45000000 | tf_op jit(solution)/shard_map/layer_forward/pallas_call | solution.py:465
  253.7 25.9 %layer_forward.7 = (bf16[256,1536]{1,0:T(8,128)(2,1)}, f32[256,3072]{1,0:T(8,128)}, bf16[256,3072]{1,0:T(8,128)(2,1)}, bf16[256,256]{1,0:T(8,128)(2,1)}, f32[256...) custom-call(s32[1,2]{1,0:T(1,128)} %add_bitcast_fusion.flag, ...), custom_call_target="tpu_custom_call" | custom-call | flops 12000000000 | bytes 45000000 | tf_op jit(solution)/shard_map/layer_forward/pallas_call | solution.py:465
  287.6 25.9 %layer_forward.8 = (bf16[256,1536]{1,0:T(8,128)(2,1)}, f32[256,3072]{1,0:T(8,128)}, bf16[256,3072]{1,0:T(8,128)(2,1)}, bf16[256,256]{1,0:T(8,128)(2,1)}, f32[256...) custom-call(s32[1,2]{1,0:T(1,128)} %add_bitcast_fusion.flag, ...), custom_call_target="tpu_custom_call" | custom-call | flops 12000000000 | bytes 45000000 | tf_op jit(solution)/shard_map/layer_forward/pallas_call | solution.py:465
  315.8 25.9 %layer_forward.9 = (bf16[256,1536]{1,0:T(8,128)(2,1)}, f32[256,3072]{1,0:T(8,128)}, bf16[256,3072]{1,0:T(8,128)(2,1)}, bf16[256,256]{1,0:T(8,128)(2,1)}, f32[256...) custom-call(s32[1,2]{1,0:T(1,128)} %add_bitcast_fusion.flag, ...), custom_call_target="tpu_custom_call" | custom-call | flops 12000000000 | bytes 45000000 | tf_op jit(solution)/shard_map/layer_forward/pallas_call | solution.py:465
  344.1 25.8 %layer_forward.10 = (bf16[256,1536]{1,0:T(8,128)(2,1)}, f32[256,3072]{1,0:T(8,128)}, bf16[256,3072]{1,0:T(8,128)(2,1)}, bf16[256,256]{1,0:T(8,128)(2,1)}, f32[25...) custom-call(s32[1,2]{1,0:T(1,128)} %add_bitcast_fusion.flag, ...), custom_call_target="tpu_custom_call" | custom-call | flops 12000000000 | bytes 45000000 | tf_op jit(solution)/shard_map/layer_forward/pallas_call | solution.py:465
  370.8 26.1 %layer_forward.11 = (bf16[256,1536]{1,0:T(8,128)(2,1)}, f32[256,3072]{1,0:T(8,128)}, bf16[256,3072]{1,0:T(8,128)(2,1)}, bf16[256,256]{1,0:T(8,128)(2,1)}, f32[25...) custom-call(s32[1,2]{1,0:T(1,128)} %add_bitcast_fusion.flag, ...), custom_call_target="tpu_custom_call" | custom-call | flops 12000000000 | bytes 45000000 | tf_op jit(solution)/shard_map/layer_forward/pallas_call | solution.py:465
  411.0 39.4 %layer_backward.6 = (bf16[256,1536]{1,0:T(8,128)(2,1)}, bf16[256,3072]{1,0:T(8,128)(2,1)}, bf16[256,3456]{1,0:T(8,128)(2,1)}, f32[256,1536]{1,0:T(8,128)}, bf16[...) custom-call(s32[1,2]{1,0:T(1,128)} %add_bitcast_fusion.2.flag, ...), custom_call_target="tpu_custom_call" | custom-call | flops 24999999488 | bytes 55000000 | tf_op jit(solution)/shard_map/layer_backward/pallas_call | solution.py:520
  457.6 37.5 %layer_backward.7 = (bf16[256,1536]{1,0:T(8,128)(2,1)}, bf16[256,3072]{1,0:T(8,128)(2,1)}, bf16[256,3456]{1,0:T(8,128)(2,1)}, f32[256,1536]{1,0:T(8,128)}, bf16[...) custom-call(s32[1,2]{1,0:T(1,128)} %add_bitcast_fusion.2.flag, ...), custom_call_target="tpu_custom_call" | custom-call | flops 24999999488 | bytes 55000000 | tf_op jit(solution)/shard_map/layer_backward/pallas_call | solution.py:520
  500.0 37.5 %layer_backward.8 = (bf16[256,1536]{1,0:T(8,128)(2,1)}, bf16[256,3072]{1,0:T(8,128)(2,1)}, bf16[256,3456]{1,0:T(8,128)(2,1)}, f32[256,1536]{1,0:T(8,128)}, bf16[...) custom-call(s32[1,2]{1,0:T(1,128)} %add_bitcast_fusion.2.flag, ...), custom_call_target="tpu_custom_call" | custom-call | flops 24999999488 | bytes 55000000 | tf_op jit(solution)/shard_map/layer_backward/pallas_call | solution.py:520
  540.9 38.0 %layer_backward.9 = (bf16[256,1536]{1,0:T(8,128)(2,1)}, bf16[256,3072]{1,0:T(8,128)(2,1)}, bf16[256,3456]{1,0:T(8,128)(2,1)}, f32[256,1536]{1,0:T(8,128)}, bf16[...) custom-call(s32[1,2]{1,0:T(1,128)} %add_bitcast_fusion.2.flag, ...), custom_call_target="tpu_custom_call" | custom-call | flops 24999999488 | bytes 55000000 | tf_op jit(solution)/shard_map/layer_backward/pallas_call | solution.py:520
  586.6 16.1 %collective-permute-done.33.other_grad = bf16[256,1536]{1,0:T(8,128)(2,1)S(1)} collective-permute-done((bf16[256,1536]{1,0:T(8,128)(2,1)S(1)}, bf16[256,1536]{1,0:T(8,128)(2,1)S(1)}, u32[]{:S(2)}, u32[]{:S(2)}) %collective-permute-start.33) | collective-permute-done | bytes 786464 | tf_op jit(solution)/shard_map/ppermute | solution.py:861
  604.0 37.8 %layer_backward.10 = (bf16[256,1536]{1,0:T(8,128)(2,1)}, bf16[256,3072]{1,0:T(8,128)(2,1)}, bf16[256,3456]{1,0:T(8,128)(2,1)}, f32[256,1536]{1,0:T(8,128)}, bf16...) custom-call(s32[1,2]{1,0:T(1,128)} %add_bitcast_fusion.1.flag, ...), custom_call_target="tpu_custom_call" | custom-call | flops 24999999488 | bytes 55000000 | tf_op jit(solution)/shard_map/layer_backward/pallas_call | solution.py:520
  645.8 14.4 %convolution_convert_fusion = bf16[3072,1536]{1,0:T(8,128)(2,1)} fusion(bf16[256,3072]{1,0:T(8,128)(2,1)S(1)} %copy-done.29, bf16[256,3072]{1,0:T(8,128)(2,1)S(1)} %get-tuple-element.440, bf16[256,3072]{1,0:T(8,128)(2,1)S(1)} %copy-done.28, bf16[256,3072]{1,0:T(8,128)(2,1)S(1)} %get-tuple-element.439, bf16[256,1536]{1,0:T(8,128)(2,1)} %get-tuple-element.450, ...), kind=kOutput, calls=%fused_computation | convolution fusion | flops 9706143744 | bytes 18874368 | tf_op jit(solution)/shard_map/td,te->de/dot_general | solution.py:910
  660.3 39.8 %layer_backward.11 = (bf16[256,1536]{1,0:T(8,128)(2,1)}, bf16[256,3072]{1,0:T(8,128)(2,1)}, bf16[256,3456]{1,0:T(8,128)(2,1)}, f32[256,1536]{1,0:T(8,128)}, bf16...) custom-call(s32[1,2]{1,0:T(1,128)} %add_bitcast_fusion.1.flag, ...), custom_call_target="tpu_custom_call" | custom-call | flops 24999999488 | bytes 55000000 | tf_op jit(solution)/shard_map/layer_backward/pallas_call | solution.py:520
  751.7 19.1 %collective-permute-done.35 = bf16[256,1536]{1,0:T(8,128)(2,1)} collective-permute-done((bf16[256,1536]{1,0:T(8,128)(2,1)}, bf16[256,1536]{1,0:T(8,128)(2,1)}, u32[]{:S(2)}, u32[]{:S(2)}) %collective-permute-start.35) | collective-permute-done | bytes 786464 | tf_op jit(solution)/shard_map/ppermute | solution.py:715
  826.6 14.8 %collective-permute-done.40 = bf16[48,3072]{1,0:T(8,128)(2,1)S(1)} collective-permute-done((bf16[48,3072]{1,0:T(8,128)(2,1)S(1)}, bf16[48,3072]{1,0:T(8,128)(2,1)S(1)}, u32[]{:S(2)}, u32[]{:S(2)}) %collective-permute-start.40) | collective-permute-done | bytes 294944 | tf_op jit(solution)/shard_map/ppermute | solution.py:597
  879.0 12.9 %collective-permute-done.47 = f32[8,3328]{1,0:T(8,128)S(1)} collective-permute-done((f32[8,3328]{1,0:T(8,128)S(1)}, f32[8,3328]{1,0:T(8,128)S(1)}, u32[]{:S(2)}, u32[]{:S(2)}) %collective-permute-start.47) | collective-permute-done | bytes 106528 | tf_op jit(solution)/shard_map/ppermute | solution.py:566
  891.9 18.0 %collective-permute-start.50 = (f32[8,3328]{1,0:T(8,128)S(1)}, f32[8,3328]{1,0:T(8,128)S(1)}, u32[]{:S(2)}, u32[]{:S(2)}) collective-permute-start(f32[8,3328]{1,0:T(8,128)S(1)} %add.668), channel_id=1, source_target_pairs={{0,2},{1,3},{2,0},{3,1},{4,6},{5,7},{6,4},{7,5},{8,10},{9,11},{10,... | collective-permute-start | bytes 319496 | tf_op jit(solution)/shard_map/ppermute | solution.py:566
  912.7 16.7 %collective-permute-done.50 = f32[8,3328]{1,0:T(8,128)S(1)} collective-permute-done((f32[8,3328]{1,0:T(8,128)S(1)}, f32[8,3328]{1,0:T(8,128)S(1)}, u32[]{:S(2)}, u32[]{:S(2)}) %collective-permute-start.50) | collective-permute-done | bytes 106528 | tf_op jit(solution)/shard_map/ppermute | solution.py:566
  (425 shorter events, 306.1 us)
Async XLA Ops:
  7.2 213.4 %all-gather.2.cloned.1.call-start = ((), (), s32[]{:S(2)}) async-start(), calls=%async_computation.1 | async-start | bytes 21307392 | tf_op jit(solution)/shard_map/all_gather | solution.py:778
  9.9 831.9 %reduce-scatter.2.cloned.1.call-start = ((), (), s32[]{:S(2)}) async-start(), calls=%async_computation.2 | async-start | bytes 10027008 | tf_op jit(solution)/shard_map/reduce_scatter | solution.py:918
  9.9 56.5 %collective-permute-start.9 = (bf16[192,1536]{1,0:T(8,128)(2,1)}, bf16[192,1536]{1,0:T(8,128)(2,1)}, u32[]{:S(2)}, u32[]{:S(2)}) collective-permute-start(bf16[192,1536]{1,0:T(8,128)(2,1)} %bitcast.190), channel_id=1, source_target_pairs={{0,8},{4,12},{1,0},{5,4},{2,1},{6,5},{3,2},{7,6},{11,3},{15,7},{10... | collective-permute-start | bytes 1769480 | tf_op jit(solution)/shard_map/ppermute | solution.py:597
  12.9 54.7 %collective-permute-start.8 = (bf16[192,1536]{1,0:T(8,128)(2,1)}, bf16[192,1536]{1,0:T(8,128)(2,1)}, u32[]{:S(2)}, u32[]{:S(2)}) collective-permute-start(bf16[192,1536]{1,0:T(8,128)(2,1)} %bitcast.191), channel_id=1, source_target_pairs={{0,1},{4,5},{1,2},{5,6},{2,3},{6,7},{3,11},{7,15},{11,10},{15,14},... | collective-permute-start | bytes 1769480 | tf_op jit(solution)/shard_map/ppermute | solution.py:597
  13.1 56.3 %collective-permute-start.7 = (bf16[192,1536]{1,0:T(8,128)(2,1)}, bf16[192,1536]{1,0:T(8,128)(2,1)}, u32[]{:S(2)}, u32[]{:S(2)}) collective-permute-start(bf16[192,1536]{1,0:T(8,128)(2,1)} %bitcast.192), channel_id=1, source_target_pairs={{0,4},{4,0},{8,12},{12,8},{1,5},{5,1},{9,13},{13,9},{2,6},{6,2},{1... | collective-permute-start | bytes 1769480 | tf_op jit(solution)/shard_map/ppermute | solution.py:601
  17.1 56.2 %collective-permute-start.2 = (bf16[256,1536]{1,0:T(8,128)(2,1)}, bf16[256,1536]{1,0:T(8,128)(2,1)S(1)}, u32[]{:S(2)}, u32[]{:S(2)}) collective-permute-start(bf16[256,1536]{1,0:T(8,128)(2,1)} %get-tuple-element.426), channel_id=1, source_target_pairs={{0,3},{1,0},{2,1},{3,2},{4,7},{5,4},{6,5},{7,6},{8,11},{9,8},{10,9... | collective-permute-start | bytes 2359304 | tf_op jit(solution)/shard_map/ppermute | solution.py:715
  63.2 63.6 %collective-permute-start.1 = (bf16[256,1536]{1,0:T(8,128)(2,1)}, bf16[256,1536]{1,0:T(8,128)(2,1)S(1)}, u32[]{:S(2)}, u32[]{:S(2)}) collective-permute-start(bf16[256,1536]{1,0:T(8,128)(2,1)} %get-tuple-element.427), channel_id=1, source_target_pairs={{0,2},{1,3},{2,0},{3,1},{4,6},{5,7},{6,4},{7,5},{8,10},{9,11},{10,... | collective-permute-start | bytes 2359304 | tf_op jit(solution)/shard_map/ppermute | solution.py:715
  66.4 60.5 %collective-permute-start = (bf16[256,1536]{1,0:T(8,128)(2,1)S(1)}, bf16[256,1536]{1,0:T(8,128)(2,1)S(1)}, u32[]{:S(2)}, u32[]{:S(2)}) collective-permute-start(bf16[256,1536]{1,0:T(8,128)(2,1)S(1)} %get-tuple-element.428), channel_id=1, source_target_pairs={{0,1},{1,2},{2,3},{3,0},{4,5},{5,6},{6,7},{7,4},{8,9},{9,10},{10,1... | collective-permute-start | bytes 2359304 | tf_op jit(solution)/shard_map/ppermute | solution.py:715
  67.7 65.5 %collective-permute-start.12 = (bf16[192,1536]{1,0:T(8,128)(2,1)}, bf16[192,1536]{1,0:T(8,128)(2,1)S(1)}, u32[]{:S(2)}, u32[]{:S(2)}) collective-permute-start(bf16[192,1536]{1,0:T(8,128)(2,1)} %collective-permute-done.8), channel_id=1, source_target_pairs={{0,1},{4,5},{1,2},{5,6},{2,3},{6,7},{3,11},{7,15},{11,10},{15,14},... | collective-permute-start | bytes 1769480 | tf_op jit(solution)/shard_map/ppermute | solution.py:597
  69.4 82.1 %collective-permute-start.10 = (bf16[192,1536]{1,0:T(8,128)(2,1)}, bf16[192,1536]{1,0:T(8,128)(2,1)S(1)}, u32[]{:S(2)}, u32[]{:S(2)}) collective-permute-start(bf16[192,1536]{1,0:T(8,128)(2,1)} %collective-permute-done.8), channel_id=1, source_target_pairs={{0,4},{4,0},{8,12},{12,8},{1,5},{5,1},{9,13},{13,9},{2,6},{6,2},{1... | collective-permute-start | bytes 1769480 | tf_op jit(solution)/shard_map/ppermute | solution.py:601
  73.3 59.8 %collective-permute-start.13 = (bf16[192,1536]{1,0:T(8,128)(2,1)}, bf16[192,1536]{1,0:T(8,128)(2,1)S(1)}, u32[]{:S(2)}, u32[]{:S(2)}) collective-permute-start(bf16[192,1536]{1,0:T(8,128)(2,1)} %collective-permute-done.9), channel_id=1, source_target_pairs={{0,8},{4,12},{1,0},{5,4},{2,1},{6,5},{3,2},{7,6},{11,3},{15,7},{10... | collective-permute-start | bytes 1769480 | tf_op jit(solution)/shard_map/ppermute | solution.py:597
  133.1 37.7 %collective-permute-start.16 = (bf16[192,1536]{1,0:T(8,128)(2,1)S(1)}, bf16[192,1536]{1,0:T(8,128)(2,1)S(1)}, u32[]{:S(2)}, u32[]{:S(2)}) collective-permute-start(bf16[192,1536]{1,0:T(8,128)(2,1)S(1)} %collective-permute-done.12), channel_id=1, source_target_pairs={{0,1},{4,5},{1,2},{5,6},{2,3},{6,7},{3,11},{7,15},{11,10},{15,14},... | collective-permute-start | bytes 1769480 | tf_op jit(solution)/shard_map/ppermute | solution.py:597
  399.3 423.0 %collective-permute-start.30 = (bf16[256,1536]{1,0:T(8,128)(2,1)}, bf16[256,1536]{1,0:T(8,128)(2,1)}, u32[]{:S(2)}, u32[]{:S(2)}) collective-permute-start(bf16[256,1536]{1,0:T(8,128)(2,1)} %get-tuple-element.416), channel_id=1, source_target_pairs={{0,3},{1,0},{2,1},{3,2},{4,7},{5,4},{6,5},{7,6},{8,11},{9,8},{10,9... | collective-permute-start | bytes 2359304 | tf_op jit(solution)/shard_map/ppermute | solution.py:715
  399.4 139.3 %collective-permute-start.29 = (bf16[256,1536]{1,0:T(8,128)(2,1)}, bf16[256,1536]{1,0:T(8,128)(2,1)}, u32[]{:S(2)}, u32[]{:S(2)}) collective-permute-start(bf16[256,1536]{1,0:T(8,128)(2,1)} %get-tuple-element.417), channel_id=1, source_target_pairs={{0,2},{1,3},{2,0},{3,1},{4,6},{5,7},{6,4},{7,5},{8,10},{9,11},{10,... | collective-permute-start | bytes 2359304 | tf_op jit(solution)/shard_map/ppermute | solution.py:715
  409.5 128.0 %collective-permute-start.28 = (bf16[256,1536]{1,0:T(8,128)(2,1)}, bf16[256,1536]{1,0:T(8,128)(2,1)}, u32[]{:S(2)}, u32[]{:S(2)}) collective-permute-start(bf16[256,1536]{1,0:T(8,128)(2,1)} %get-tuple-element.418), channel_id=1, source_target_pairs={{0,1},{1,2},{2,3},{3,0},{4,5},{5,6},{6,7},{7,4},{8,9},{9,10},{10,1... | collective-permute-start | bytes 2359304 | tf_op jit(solution)/shard_map/ppermute | solution.py:715
  450.4 48.1 %collective-permute-start.31 = (bf16[256,1536]{1,0:T(8,128)(2,1)}, bf16[256,1536]{1,0:T(8,128)(2,1)}, u32[]{:S(2)}, u32[]{:S(2)}) collective-permute-start(bf16[256,1536]{1,0:T(8,128)(2,1)} %get-tuple-element.254), channel_id=1, source_target_pairs={{16,0},{17,1},{18,2},{19,3},{20,4},{21,5},{22,6},{23,7},{24,8},{25... | collective-permute-start | bytes 2359304 | tf_op jit(solution)/shard_map/ppermute | solution.py:861
  498.5 41.4 %collective-permute-start.32 = (bf16[256,1536]{1,0:T(8,128)(2,1)}, bf16[256,1536]{1,0:T(8,128)(2,1)S(1)}, u32[]{:S(2)}, u32[]{:S(2)}) collective-permute-start(bf16[256,1536]{1,0:T(8,128)(2,1)} %get-tuple-element.267), channel_id=1, source_target_pairs={{16,0},{17,1},{18,2},{19,3},{20,4},{21,5},{22,6},{23,7},{24,8},{25... | collective-permute-start | bytes 2359304 | tf_op jit(solution)/shard_map/ppermute | solution.py:861
  602.7 42.0 %collective-permute-start.34 = (bf16[256,1536]{1,0:T(8,128)(2,1)}, bf16[256,1536]{1,0:T(8,128)(2,1)S(1)}, u32[]{:S(2)}, u32[]{:S(2)}) collective-permute-start(bf16[256,1536]{1,0:T(8,128)(2,1)} %get-tuple-element.281), channel_id=1, source_target_pairs={{16,0},{17,1},{18,2},{19,3},{20,4},{21,5},{22,6},{23,7},{24,8},{25... | collective-permute-start | bytes 2359304 | tf_op jit(solution)/shard_map/ppermute | solution.py:861
  711.6 67.5 %collective-permute-start.51 = (bf16[8,96,3456]{2,1,0:T(8,128)(2,1)}, bf16[8,96,3456]{2,1,0:T(8,128)(2,1)S(1)}, u32[]{:S(2)}, u32[]{:S(2)}) collective-permute-start(bf16[8,96,3456]{2,1,0:T(8,128)(2,1)} %bitcast.197), channel_id=1, source_target_pairs={{0,4},{4,0},{8,12},{12,8},{1,5},{5,1},{9,13},{13,9},{2,6},{6,2},{1... | collective-permute-start | bytes 15925256 | tf_op jit(solution)/shard_map/ppermute | solution.py:601
  712.1 113.6 %collective-permute-start.41 = (f32[8,3328]{1,0:T(8,128)S(1)}, f32[8,3328]{1,0:T(8,128)}, u32[]{:S(2)}, u32[]{:S(2)}) collective-permute-start(f32[8,3328]{1,0:T(8,128)S(1)} %fusion.33), channel_id=1, source_target_pairs={{0,4},{4,0},{8,12},{12,8},{1,5},{5,1},{9,13},{13,9},{2,6},{6,2},{1... | collective-permute-start | bytes 319496 | tf_op jit(solution)/shard_map/ppermute | solution.py:566
  726.5 44.3 %collective-permute-start.35 = (bf16[256,1536]{1,0:T(8,128)(2,1)}, bf16[256,1536]{1,0:T(8,128)(2,1)}, u32[]{:S(2)}, u32[]{:S(2)}) collective-permute-start(bf16[256,1536]{1,0:T(8,128)(2,1)} %get-tuple-element.393), channel_id=1, source_target_pairs={{0,1},{1,2},{2,3},{3,0},{4,5},{5,6},{6,7},{7,4},{8,9},{9,10},{10,1... | collective-permute-start | bytes 2359304 | tf_op jit(solution)/shard_map/ppermute | solution.py:715
  751.7 51.4 %collective-permute-start.38 = (bf16[8,96,3072]{2,1,0:T(8,128)(2,1)}, bf16[8,96,3072]{2,1,0:T(8,128)(2,1)}, u32[]{:S(2)}, u32[]{:S(2)}) collective-permute-start(bf16[8,96,3072]{2,1,0:T(8,128)(2,1)} %bitcast.198), channel_id=1, source_target_pairs={{0,4},{4,0},{8,12},{12,8},{1,5},{5,1},{9,13},{13,9},{2,6},{6,2},{1... | collective-permute-start | bytes 14155784 | tf_op jit(solution)/shard_map/ppermute | solution.py:601
  877.4 56.1 %collective-permute-start.37 = (bf16[256,1536]{1,0:T(8,128)(2,1)S(1)}, bf16[256,1536]{1,0:T(8,128)(2,1)}, u32[]{:S(2)}, u32[]{:S(2)}) collective-permute-start(bf16[256,1536]{1,0:T(8,128)(2,1)S(1)} %copy-done.40), channel_id=1, source_target_pairs={{0,2},{1,3},{2,0},{3,1},{4,6},{5,7},{6,4},{7,5},{8,10},{9,11},{10,... | collective-permute-start | bytes 2359304 | tf_op jit(solution)/shard_map/ppermute | solution.py:715
  891.9 37.4 %collective-permute-start.50 = (f32[8,3328]{1,0:T(8,128)S(1)}, f32[8,3328]{1,0:T(8,128)S(1)}, u32[]{:S(2)}, u32[]{:S(2)}) collective-permute-start(f32[8,3328]{1,0:T(8,128)S(1)} %add.668), channel_id=1, source_target_pairs={{0,2},{1,3},{2,0},{3,1},{4,6},{5,7},{6,4},{7,5},{8,10},{9,11},{10,... | collective-permute-start | bytes 319496 | tf_op jit(solution)/shard_map/ppermute | solution.py:566
  (125 other events, 2029.7 us)
Sparse Core Ops, SparseCore 0:
  10.2 210.4 all-gather.1
  660.4 139.1 reduce-scatter.1

commit v3 on v2

--- a/solution.py
+++ b/solution.py
@@ -90,9 +90,9 @@
 def fwd_body(
     flag, own_ref, other_ref, ngain, wg, wc, wbc, wo, taps, taps_bc, head_rows, skip, gate_gain, spread, tail_in,
     tail_bc_in, state_in,
-    normed_o, gate_o, cin_o, cin_bc_o, step_o, ssm_o, state_o, gout_o, r_o, branch_o, out_o,
+    normed_o, cin_o, act_o, slope_o, cin_bc_o, step_o, silu_o, turned_o, u_o, state_o, gout_o, r_o, branch_o, out_o,
     tail_o, tail_bc_o,
-    u_s, ssq_s, k_s, c_s, bt_s, dt_s, ec_s, w_s, cum_s, cumt_s,
+    u_s, ssq_s, k_s, c_s, bt_s, sp_s, cum_s, cumt_s,
 ):
     step = pl.program_id(0)
     length = own_ref.shape[0]
@@ -121,9 +121,9 @@
         dt = head_steps(step_raw, head_rows[...])
         cum = running_sum(dt * head_rows[1:2])
         total = cum[length - 1 : length]
-        dt_s[...] = halves(dt)
-        ec_s[...] = halves(jnp.exp(cum))
-        w_s[...] = halves(dt * jnp.exp(total - cum))
+        sp_s[0:length] = halves(dt)
+        sp_s[length : 2 * length] = halves(jnp.exp(cum))
+        sp_s[2 * length :] = halves(dt * jnp.exp(total - cum))
         for g in range(GROUPS):
             cum_s[g] = cum[:, g * GROUP : (g + 1) * GROUP] * LOG2_E
         cumt_s[...] = (cum * LOG2_E).T
@@ -134,18 +134,22 @@
     def _():
         normed = normed_o[...]
         gate = dot(normed, wg[...], NN)
-        gate_o[...] = gate
         conv_in = dot(normed, wc[...], NN).astype(bf16)
         cin_o[...] = conv_in
         tail_o[...] = conv_in[length - 16 :]
         tap_rows = taps[...]
         shifted = earlier_rows(tail_in[...], conv_in.astype(f32))
         pre = conv_sum(tap_rows, shifted, tap_rows[CONV : CONV + 1])
-        act = (pre * sigmoid(pre)).astype(bf16).astype(f32)
+        sig = sigmoid(pre)
+        act = pre * sig
+        slope_o[...] = (sig + act * (1.0 - sig)).astype(bf16)
+        act_o[...] = act.astype(bf16)
+        act = act_o[...].astype(f32)
         where = spread[...]
-        x_dt = (act * dot(dt_s[...], where, NN)).astype(bf16)
-        x_w = (act * dot(w_s[...], where, NN)).astype(bf16)
-        ec = dot(ec_s[...], where, NN)
+        spreads = dot(sp_s[...], where, NN)
+        x_dt = (act * spreads[:length]).astype(bf16)
+        x_w = (act * spreads[2 * length :]).astype(bf16)
+        ec = spreads[length : 2 * length]
         state = state_in[...]
         state_o[...] = ec[length - 1 : length] * state + dot(bt_s[...], x_w, NN)
         carried = dot(c_s[...], state.astype(bf16), NN) * ec
@@ -153,17 +157,17 @@
         cumt = cumt_s[pl.ds(pl.multiple_of(step * GROUP, GROUP), GROUP), :]
         k = k_s[...]
         mask = lower_mask(half, half)
-        left_lane = lax.broadcasted_iota(jnp.int32, (length, LANES), 1) < HEAD_DIM
+        left_lane = lax.broadcasted_iota(jnp.int32, (half, LANES), 1) < HEAD_DIM
         pieces = []
         for pair in range(GROUP // 2):
             x_pair = x_dt[:, pair * LANES : (pair + 1) * LANES]
-            results = []
+            tops, lows = [], []
             for i in (2 * pair, 2 * pair + 1):
                 col, row = cum[:, i : i + 1], cumt[i : i + 1, :]
                 top = jnp.exp2(jnp.where(mask, col[:half] - row[:, :half], -1e30))
                 low_left = jnp.exp2(col[half:] - row[:, :half])
                 low_right = jnp.exp2(jnp.where(mask, col[half:] - row[:, half:], -1e30))
-                top = (top * k[:half, :half]).astype(bf16)
+                tops.append((top * k[:half, :half]).astype(bf16))
                 low = jnp.concatenate(
                     [
                         (low_left * k[half:, :half]).astype(bf16),
@@ -171,14 +175,23 @@
                     ],
                     axis=1,
                 )
-                results.append(
-                    jnp.concatenate([dot(top, x_pair[:half], NN), dot(low, x_pair, NN)], axis=0)
+                lows.append(low)
+            tops = dot(jnp.concatenate(tops, axis=0), x_pair[:half], NN)
+            lows = dot(jnp.concatenate(lows, axis=0), x_pair, NN)
+            pieces.append(
+                jnp.concatenate(
+                    [jnp.where(left_lane, both[:half], both[half:]) for both in (tops, lows)],
+                    axis=0,
                 )
-            pieces.append(jnp.where(left_lane, results[0], results[1]))
+            )
         within = jnp.concatenate(pieces, axis=1)
         ssm = within + carried + skip[...] * act
-        ssm_o[...] = ssm
-        u = ssm * (gate * sigmoid(gate))
+        sig = sigmoid(gate)
+        silu = gate * sig
+        silu_o[...] = silu.astype(bf16)
+        turned_o[...] = (ssm * (sig + silu * (1.0 - sig))).astype(bf16)
+        u = ssm * silu
+        u_o[...] = u.astype(bf16)
         gained = u * gate_gain[...]
         u_s[:, pl.ds(pl.multiple_of(step * WIDTH, WIDTH), WIDTH)] = gained
         ssq_s[...] += jnp.sum(u * u, axis=1, keepdims=True)
@@ -199,11 +212,12 @@
 
 def bwd_body(
     flag, own_ref, other_ref, own_grad, other_grad, ngain, branch, r_ref, wo, wg, wc, wbc, taps, taps_bc, head_rows, skip,
-    gate_gain, spread, gather, gate_ref, ssm_ref, cin, cin_bc, step_ref, tail_in, tail_bc_in,
+    gate_gain, spread, gather, silu_ref, turned_ref, u_ref, act_ref, slope_ref, cin, cin_bc, step_ref,
+    tail_bc_in,
     state_in, adj_in, next_in, next_bc_in,
     gout_ref, gg_o, gc_o, gin_o, gin_low_o, adj_o, next_o, next_bc_o, chan_o, chan_bc_o, ngrad_o,
     head_o,
-    acc_s, kt_s, wt_s, b_s, c_s, ct_s, dt_s, ec_s, w_s, cum_s, cumt_s, db_s, dc_s, rows_s, cols_s,
+    acc_s, kt_s, wt_s, b_s, c_s, ct_s, sp_s, cum_s, cumt_s, db_s, dc_s, rows_s, cols_s,
     direct_s, fresh_s, carry_s, edge_s, dsilu_s, q_s,
 ):
     step = pl.program_id(0)
@@ -227,9 +241,9 @@
         dt = head_steps(step_ref[...], head_rows[...])
         cum = running_sum(dt * head_rows[1:2])
         total = cum[length - 1 : length]
-        dt_s[...] = halves(dt)
-        ec_s[...] = halves(jnp.exp(cum))
-        w_s[...] = halves(jnp.exp(total - cum))
+        sp_s[0:length] = halves(dt)
+        sp_s[length : 2 * length] = halves(jnp.exp(cum))
+        sp_s[2 * length :] = halves(jnp.exp(total - cum))
         for g in range(GROUPS):
             cum_s[g] = cum[:, g * GROUP : (g + 1) * GROUP] * LOG2_E
         cumt_s[...] = (cum * LOG2_E).T
@@ -241,24 +255,17 @@
     @pl.when(step < GROUPS)
     def _():
         grad_gated = dot(gout_ref[...], wo[...], NT)
-        gate, ssm = gate_ref[...], ssm_ref[...]
-        sig = sigmoid(gate)
-        silu = gate * sig
-        u = ssm * silu
+        u = u_ref[...].astype(f32)
         scaled = r_ref[:, 0:1] * grad_gated
         gain_grad = jnp.sum(scaled * u, axis=0, keepdims=True)
         grad_u = scaled * gate_gain[...] - u * q_s[:, 0:1]
-        grad_ssm = grad_u * silu
-        grad_gate = (grad_u * ssm * (sig * (1.0 + gate * (1.0 - sig)))).astype(bf16)
+        grad_ssm = grad_u * silu_ref[...].astype(f32)
+        grad_gate = (grad_u * turned_ref[...].astype(f32)).astype(bf16)
         gg_o[...] = grad_gate
-        tap_rows = taps[...]
-        shifted = earlier_rows(tail_in[...], cin[...].astype(f32))
-        pre = conv_sum(tap_rows, shifted, tap_rows[CONV : CONV + 1])
-        sig = sigmoid(pre)
-        act = (pre * sig).astype(bf16).astype(f32)
-        dsilu = sig * (1.0 + pre * (1.0 - sig))
+        act = act_ref[...].astype(f32)
         where, pick = spread[...], gather[...]
-        dt, ec, w = (dot(ref[...], where, NN) for ref in (dt_s, ec_s, w_s))
+        spreads = dot(sp_s[...], where, NN)
+        dt, ec, w = (spreads[i * length : (i + 1) * length] for i in range(3))
         skip_grad = jnp.sum(act * grad_ssm, axis=0, keepdims=True)
         x_dt = act * dt
         x_low, g_low = x_dt.astype(bf16), grad_ssm.astype(bf16)
@@ -280,7 +287,7 @@
         mask = lax.broadcasted_iota(jnp.int32, (half, half), 0) <= lax.broadcasted_iota(
             jnp.int32, (half, half), 1
         )
-        left_lane = lax.broadcasted_iota(jnp.int32, (length, LANES), 1) < HEAD_DIM
+        left_lane = lax.broadcasted_iota(jnp.int32, (half, LANES), 1) < HEAD_DIM
         lane_id = lax.broadcasted_iota(jnp.int32, (1, LANES), 1)
         pieces, col_sums = [], []
         row_sums = rows_s[...]
@@ -288,11 +295,16 @@
         for pair in range(GROUP // 2):
             lanes = slice(pair * LANES, (pair + 1) * LANES)
             x_pair, g_pair = x_low[:, lanes], g_low[:, lanes]
-            results = []
+            x_heads = [
+                jnp.where(mine, x_pair[rows], jnp.zeros_like(x_pair[rows]))
+                for rows in (slice(0, half), slice(half, length))
+                for mine in (left_lane, jnp.logical_not(left_lane))
+            ]
+            p_top = dot(jnp.concatenate(x_heads[:2], axis=0), g_pair, NT)
+            p_low = dot(jnp.concatenate(x_heads[2:], axis=0), g_pair[half:], NT)
+            tops, lows = [], []
             for i in (2 * pair, 2 * pair + 1):
                 col, row = cum[:, i : i + 1], cumt[i : i + 1, :]
-                mine = left_lane if i % 2 == 0 else jnp.logical_not(left_lane)
-                x_head = jnp.where(mine, x_pair, jnp.zeros_like(x_pair))
                 l_tl = jnp.exp2(jnp.where(mask, row[:, :half] - col[:half], -1e30))
                 l_tr = jnp.exp2(row[:, half:] - col[:half])
                 l_br = jnp.exp2(jnp.where(mask, row[:, half:] - col[half:], -1e30))
@@ -301,15 +313,10 @@
                     l_tr * kt[:half, half:],
                     l_br * kt[half:, half:],
                 )
-                mixed = jnp.concatenate([lk_tl.astype(bf16), lk_tr.astype(bf16)], axis=1)
-                results.append(
-                    jnp.concatenate(
-                        [dot(mixed, g_pair, NN), dot(lk_br.astype(bf16), g_pair[half:], NN)], axis=0
-                    )
-                )
-                p_top = dot(x_head[:half], g_pair, NT)
-                p_br = dot(x_head[half:], g_pair[half:], NT)
-                p_tl, p_tr = p_top[:, :half], p_top[:, half:]
+                tops.append(jnp.concatenate([lk_tl.astype(bf16), lk_tr.astype(bf16)], axis=1))
+                lows.append(lk_br.astype(bf16))
+                of_head = slice((i % 2) * half, (i % 2 + 1) * half)
+                p_tl, p_tr, p_br = p_top[of_head, :half], p_top[of_head, half:], p_low[of_head]
                 w_tl, w_tr, w_br = w_tl + l_tl * p_tl, w_tr + l_tr * p_tr, w_br + l_br * p_br
                 z_tl, z_tr, z_br = lk_tl * p_tl, lk_tr * p_tr, lk_br * p_br
                 sums = jnp.concatenate(
@@ -324,30 +331,38 @@
                     jnp.concatenate(
                         [
                             jnp.sum(z_tl, axis=0, keepdims=True),
-                            jnp.sum(z_tr, axis=0, keepdims=True)
-                            + jnp.sum(z_br, axis=0, keepdims=True),
+                            jnp.sum(z_tr + z_br, axis=0, keepdims=True),
                         ],
                         axis=1,
                     )
                 )
-            pieces.append(jnp.where(left_lane, results[0], results[1]))
+            tops = dot(jnp.concatenate(tops, axis=0), g_pair, NN)
+            lows = dot(jnp.concatenate(lows, axis=0), g_pair[half:], NN)
+            pieces.append(
+                jnp.concatenate(
+                    [jnp.where(left_lane, both[:half], both[half:]) for both in (tops, lows)],
+                    axis=0,
+                )
+            )
         wt_s[:half, :half] = w_tl
         wt_s[:half, half:] = w_tr
         wt_s[half:, half:] = w_br
         rows_s[...] = row_sums
         cols_s[pl.ds(start, GROUP), :] = jnp.concatenate(col_sums, axis=0)
         mixed_grad = jnp.concatenate(pieces, axis=1) + from_adj
-        direct_s[...] += dot((act * mixed_grad).astype(bf16), pick, NN)
-        fresh_s[...] += dot((x_dt * from_adj).astype(bf16), pick, NN)
-        carry_s[...] += dot((grad_ssm * carried).astype(bf16), pick, NN)
-        grad_pre = (dt * mixed_grad + skip[...] * grad_ssm) * dsilu
+        products = [act * mixed_grad, x_dt * from_adj, grad_ssm * carried]
+        picked = dot(jnp.concatenate([v.astype(bf16) for v in products], axis=0), pick, NN)
+        direct_s[...] += picked[:length]
+        fresh_s[...] += picked[length : 2 * length]
+        carry_s[...] += picked[2 * length :]
+        grad_pre = (dt * mixed_grad + skip[...] * grad_ssm) * slope_ref[...].astype(f32)
         next_o[...] = grad_pre[0:8]
-        grad_conv = conv_sum(tap_rows, later_rows(grad_pre, next_in[...]))
+        later = later_rows(grad_pre, next_in[...])
+        grad_conv = conv_sum(taps[...], later)
         grad_conv = grad_conv.astype(bf16)
         gc_o[:, pl.ds(pl.multiple_of(step * WIDTH, WIDTH), WIDTH)] = grad_conv
-        sums = [
-            jnp.sum(grad_pre * rows, axis=0, keepdims=True) for rows in shifted
-        ]
+        conv_in = cin[...].astype(f32)
+        sums = [jnp.sum(conv_in * rows, axis=0, keepdims=True) for rows in later]
         sums += [jnp.sum(grad_pre, axis=0, keepdims=True), gain_grad, skip_grad]
         chan_o[...] = jnp.concatenate(sums + [jnp.zeros_like(skip_grad)], axis=0)
         acc_s[...] += dot(grad_gate, wg[...], NT) + dot(grad_conv, wc[...], NT)
@@ -360,11 +375,10 @@
         grad_pre = jnp.concatenate([grad_b, grad_c], axis=1) * dsilu_s[...]
         next_bc_o[...] = grad_pre[0:8]
         tap_rows = taps_bc[...]
-        grad_conv = conv_sum(tap_rows, later_rows(grad_pre, next_bc_in[...]))
-        shifted = earlier_rows(tail_bc_in[...], cin_bc[...].astype(f32))
-        sums = [
-            jnp.sum(grad_pre * rows, axis=0, keepdims=True) for rows in shifted
-        ]
+        later = later_rows(grad_pre, next_bc_in[...])
+        grad_conv = conv_sum(tap_rows, later)
+        conv_in = cin_bc[...].astype(f32)
+        sums = [jnp.sum(conv_in * rows, axis=0, keepdims=True) for rows in later]
         sums += [jnp.sum(grad_pre, axis=0, keepdims=True)]
         chan_bc_o[...] = jnp.concatenate(sums + [jnp.zeros((3, BC), f32)], axis=0)
         dt = head_steps(step_ref[...], head_rows[...])
@@ -443,11 +457,14 @@
     ]
     out = [
         ((length, D), bf16, whole((length, D))),
-        ((length, DI), f32, by_group(length)),
+        ((length, DI), bf16, by_group(length)),
+        ((length, DI), bf16, by_group(length)),
         ((length, DI), bf16, by_group(length)),
         ((length, BC), bf16, whole((length, BC))),
         ((length, LANES), f32, whole((length, LANES))),
-        ((length, DI), f32, by_group(length)),
+        ((length, DI), bf16, by_group(length)),
+        ((length, DI), bf16, by_group(length)),
+        ((length, DI), bf16, by_group(length)),
         ((STATE, DI), f32, by_group(STATE)),
         ((length, DI), bf16, whole((length, DI))),
         ((length, LANES), f32, whole((length, LANES))),
@@ -458,8 +475,8 @@
     ]
     scratch = [
         ((length, DI), f32), ((length, LANES), f32), ((length, length), f32),
-        ((length, STATE), bf16), ((STATE, length), bf16), ((length, 2 * LANES), bf16),
-        ((length, 2 * LANES), bf16), ((length, 2 * LANES), bf16), ((GROUPS, length, GROUP), f32),
+        ((length, STATE), bf16), ((STATE, length), bf16), ((3 * length, 2 * LANES), bf16),
+        ((GROUPS, length, GROUP), f32),
         ((LANES, length), f32),
     ]
     return pl.pallas_call(
@@ -491,7 +508,8 @@
         whole((length, LANES)), rows_of_wo, by_group(D), by_group(D, WIDTH, GROUPS), tail_of(D, TAIL, 2 * DI),
         by_group(8), tail_of(8, BC, DI), whole((8, LANES)), by_group(1), by_group(1),
         by_group(2 * LANES), pick, by_group(length), by_group(length), by_group(length),
-        whole((length, BC)), whole((length, LANES)), by_group(16), whole((16, BC)),
+        by_group(length), by_group(length), by_group(length), whole((length, BC)),
+        whole((length, LANES)), whole((16, BC)),
         by_group(STATE), by_group(STATE), by_group(8), whole((8, BC)),
     ]
     out = [
@@ -511,7 +529,7 @@
     scratch = [
         ((length, D), f32), ((length, length), f32), ((length, length), f32),
         ((length, STATE), bf16), ((length, STATE), bf16), ((STATE, length), bf16),
-        ((length, 2 * LANES), bf16), ((length, 2 * LANES), bf16), ((length, 2 * LANES), bf16),
+        ((3 * length, 2 * LANES), bf16),
         ((GROUPS, length, GROUP), f32), ((LANES, length), f32), ((length, STATE), f32),
         ((length, STATE), f32), ((length, LANES), f32), ((LANES, length), f32),
         ((length, LANES), f32), ((length, LANES), f32), ((length, LANES), f32), ((1, LANES), f32),
@@ -532,8 +550,8 @@
     )(
         flag, kept["own"], kept["other"], own_grad, other_grad, params["norm_gain"], kept["branch"], kept["r"], wo, win, win, win,
         params["taps"], params["taps"], params["heads"], params["skip"], params["gate_gain"],
-        params["spread"], params["gather"], kept["gate"], kept["ssm"], kept["cin"], kept["cin_bc"],
-        kept["step"], kept["tail"], kept["tail_bc"], kept["state"], adj, ahead, ahead_bc,
+        params["spread"], params["gather"], kept["silu"], kept["turned"], kept["u"], kept["act"],
+        kept["slope"], kept["cin"], kept["cin_bc"], kept["step"], kept["tail_bc"], kept["state"], adj, ahead, ahead_bc,
     )
 
 
@@ -715,18 +733,44 @@
     return lax.ppermute(value, "seq", route)
 
 
-def to_sequences(rows):
-    parts = rows.shape[0]
+def in_order(arrived):
+    parts = len(arrived)
     rank = lax.axis_index("seq") % parts
-    arrived = []
-    for shift in range(parts):
-        piece = lax.dynamic_index_in_dim(rows, (rank + shift) % parts, 0, keepdims=False)
-        arrived.append(piece if shift == 0 else turn(piece, shift, parts))
     arrived = jnp.stack(arrived)
     return [
         lax.dynamic_index_in_dim(arrived, (rank - k) % parts, 0, keepdims=False)
         for k in range(parts)
     ]
+
+
+def token_blocks(tokens):
+    parts, length = tokens.shape[0], tokens.shape[1]
+    rank, section = lax.axis_index("seq") % parts, lax.axis_index("section")
+    half = length // 2
+    arrived = []
+    for shift in range(1, parts):
+        at = ((rank + shift) % parts, section * half, 0)
+        piece = lax.dynamic_slice(tokens, at, (1, half, tokens.shape[2]))[0]
+        arrived.append(turn(piece, shift, parts))
+    handed = lax.ppermute(jnp.concatenate(arrived, axis=0), "section", [(1, 0)])
+    blocks = [lax.dynamic_index_in_dim(tokens, rank, 0, keepdims=False)]
+    for i, low in enumerate(arrived):
+        blocks.append(jnp.concatenate([low, handed[i * half : (i + 1) * half]], axis=0))
+    return in_order(blocks)
+
+
+def cotangent_blocks(rows):
+    parts = rows.shape[0]
+    size = lax.axis_size("seq")
+    rank = lax.axis_index("seq") % parts
+    arrived = [lax.dynamic_index_in_dim(rows, rank, 0, keepdims=False)]
+    for shift in range(1, parts):
+        piece = lax.dynamic_index_in_dim(rows, (rank + shift) % parts, 0, keepdims=False)
+        route = [
+            (size + i, size + i - i % parts + (i % parts + shift) % parts) for i in range(size)
+        ]
+        arrived.append(lax.ppermute(piece, ("section", "seq"), route))
+    return in_order(arrived)
 
 
 def to_pieces(blocks, sent_type):
@@ -753,7 +797,8 @@
 
 
 KEPT = (
-    "normed", "gate", "cin", "cin_bc", "step", "ssm", "state_out", "gout", "r", "branch", "out",
+    "normed", "cin", "act", "slope", "cin_bc", "step", "silu", "turned", "u", "state_out", "gout", "r",
+    "branch", "out",
     "tail_out", "tail_bc_out",
 )
 SKEW = 2
@@ -771,7 +816,7 @@
     seq = lax.axis_size("seq")
     parts, length = tokens.shape[0], tokens.shape[1]
     owned = in_proj.shape[1]
-    blocks_in = to_sequences(jnp.where(first, tokens, cotangent))
+    tokens_in = token_blocks(tokens)
 
     shard = jnp.pad(in_proj[0], ((0, 0), (0, TAIL - BC - HEADS)))
     weights = (
@@ -811,7 +856,7 @@
         for tick in range(ticks):
             if tick == SKEW:
                 carry = tuple(jnp.where(first, now, at) for now, at in zip(carry, start))
-            own, other = blocks_in[min(tick, parts - 1)], received[tick]
+            own, other = tokens_in[min(tick, parts - 1)], received[tick]
             values = dict(zip(KEPT, fwd_call(flags(first, 0), own, other, params, weights, *carry)))
             values.update(own=own, other=other, state=carry[0], tail=carry[1], tail_bc=carry[2])
             carry = (values["state_out"], values["tail_out"], values["tail_bc_out"])
@@ -830,7 +875,7 @@
                 carry = tuple(jnp.where(first, at, now) for now, at in zip(carry, start))
             if tick == parts:
                 carry = tuple(jnp.where(first, now, zero) for now, zero in zip(carry, zeros))
-            from_loss = blocks_in[max(parts - 1 - tick, 0)]
+            from_loss = loss_in[max(parts - 1 - tick, 0)]
             late = jnp.int32(2 if tick >= parts else 1)
             if before_last is not None and tick == ticks - 1:
                 early = before_last(grads, received[tick])
@@ -877,6 +922,8 @@
 
         start = lax.fori_loop(0, hops - 1, onward, start)
     kept = forward(start)
+    cotangent, _ = lax.optimization_barrier((cotangent, kept[0]["r"]))
+    loss_in = cotangent_blocks(cotangent)
     activations = laid_out(
         *to_pieces(
             [jnp.where(first, kept[k]["out"], kept[k + SKEW]["out"]) for k in range(parts)], bf16
@@ -904,7 +951,7 @@
         )
 
     def out_term(grads, received):
-        branch_grads = [jnp.where(first, received, blocks_in[0])] + [
+        branch_grads = [jnp.where(first, received, loss_in[0])] + [
             jnp.where(first, grads[k]["out"], grads[k + SKEW]["out"]) for k in range(1, parts)
         ]
         return jnp.einsum(

time: 968 us -> 935 us (0.966)
  waiting for transfers between devices: 270 us -> 257 us
  Pallas kernels: 385 us -> 373 us
    ppermute x9, waiting for transfers between devices: 84.5 us -> 67.4 us  [turn(): return lax.ppermute(value, 'seq', route)]
    ppermute x24, starting transfers between devices: 42.2 us -> 26.3 us  [around(): return lax.ppermute(value, ('dp', 'seq'), ring_route(step))]
    pallas_call x6, Pallas kernels: 230 us -> 214 us  [bwd_call(): pl.pallas_call(bwd_body, grid=(GROUPS + 1,), in_specs=in_specs, out_specs...]
    ppermute x4, waiting for transfers between devices: 28.2 us -> 15.2 us  [gather_small(): other = lax.ppermute(row, axis, xor_route(size, bit))]
    ppermute x4, starting transfers between devices: 7.85 us -> 20.1 us  [forward(): received.append(lax.ppermute(values['out'], 'section', [(0, 1)]))]
    ppermute x24, waiting for transfers between devices: 84.6 us -> 95.9 us  [around(): return lax.ppermute(value, ('dp', 'seq'), ring_route(step))]
  transfers between devices with their start and end apart: 62 -> 66, of which waited for: 23 -> 27; matrix products, arithmetic and copies ran while one was open for 15% -> 15% of each run, Pallas kernels for 35% -> 35%
where the time goes in v3:
time: 935 us; the launch traced here: 925 us
  Pallas kernels  373 us (40%)
  waiting for transfers between devices  257 us (27%)
  starting transfers between devices  100 us (11%)
  local copies, waits for them, and re-layouts  66.1 us (7%)
  other arithmetic  65.9 us (7%)
  matrix products  46.4 us (5%)
  between operations  15.9 us (2%)
    pallas_call x6, Pallas kernels, bwd_call(): pl.pallas_call(bwd_body, grid=(GROUPS + 1,), in_specs=in_specs, out_specs...  214 us
    pallas_call x6, Pallas kernels, fwd_call(): pl.pallas_call(fwd_body, grid=(GROUPS + 1,), in_specs=in_specs, out_specs...  159 us
    ppermute x24, waiting for transfers between devices, around(): return lax.ppermute(value, ('dp', 'seq'), ring_route(step))  95.9 us
    ppermute x9, waiting for transfers between devices, turn(): return lax.ppermute(value, 'seq', route)  67.4 us
    dot_general x4, matrix products, term(): return jnp.einsum('td,te->de', columns, right, preferred_element_type=f32)  32.1 us
    all_gather x1, waiting for transfers between devices, shards(): lax.all_gather(shard, ('dp', 'seq'), axis=0, tiled=True)  32 us
    ppermute x4, waiting for transfers between devices, exchange(): lax.ppermute(value, axis, xor_route(lax.axis_size(axis), bit))  29.9 us
    ppermute x24, starting transfers between devices, around(): return lax.ppermute(value, ('dp', 'seq'), ring_route(step))  26.3 us
  transfers between devices with their start and end apart: 66, of which 27 were waited for; matrix products, arithmetic and copies ran while one was open for 15% of the time, Pallas kernels for 35%

profile of v3, /device:TPU:0, one launch (start us, length us, event | category | flops | bytes accessed | tf_op | source)
XLA Modules:
  0.0 924.7 jit_solution(15145714752422084604)
XLA Ops:
  66.0 22.0 %collective-permute-done.1 = bf16[128,1536]{1,0:T(8,128)(2,1)S(1)} collective-permute-done((bf16[128,1536]{1,0:T(8,128)(2,1)}, bf16[128,1536]{1,0:T(8,128)(2,1)S(1)}, u32[]{:S(2)}, u32[]{:S(2)}) %collective-permute-start.1) | collective-permute-done | bytes 393248 | tf_op jit(solution)/shard_map/ppermute | solution.py:733
  95.5 14.4 %collective-permute-done.13 = bf16[192,1536]{1,0:T(8,128)(2,1)S(1)} collective-permute-done((bf16[192,1536]{1,0:T(8,128)(2,1)}, bf16[192,1536]{1,0:T(8,128)(2,1)S(1)}, u32[]{:S(2)}, u32[]{:S(2)}) %collective-permute-start.13) | collective-permute-done | bytes 589856 | tf_op jit(solution)/shard_map/ppermute | solution.py:615
  119.9 13.2 %collective-permute-done.17 = bf16[192,1536]{1,0:T(8,128)(2,1)S(1)} collective-permute-done((bf16[192,1536]{1,0:T(8,128)(2,1)S(1)}, bf16[192,1536]{1,0:T(8,128)(2,1)S(1)}, u32[]{:S(2)}, u32[]{:S(2)}) %collective-permute-start.17) | collective-permute-done | bytes 589856 | tf_op jit(solution)/shard_map/ppermute | solution.py:615
  154.6 32.0 %all-gather.2.cloned.1.call-done.wg.wc.wbc = bf16[1536,6528]{1,0:T(8,128)(2,1)} async-done(((bf16[96,6528]{1,0:T(8,128)(2,1)}), bf16[1536,6528]{1,0:T(8,128)(2,1)}) %all-gather.2.cloned.1.call-update) | async-done | bytes 20054032 | tf_op jit(solution)/shard_map/all_gather | solution.py:823
  190.2 26.4 %layer_forward.6 = (bf16[256,1536]{1,0:T(8,128)(2,1)}, bf16[256,3072]{1,0:T(8,128)(2,1)}, bf16[256,3072]{1,0:T(8,128)(2,1)}, bf16[256,3072]{1,0:T(8,128)(2,1)}, ...) custom-call(s32[1,2]{1,0:T(1,128)} %add_bitcast_fusion.flag, ...), custom_call_target="tpu_custom_call" | custom-call | flops 12000000000 | bytes 45000000 | tf_op jit(solution)/shard_map/layer_forward/pallas_call | solution.py:482
  223.5 26.5 %layer_forward.7 = (bf16[256,1536]{1,0:T(8,128)(2,1)}, bf16[256,3072]{1,0:T(8,128)(2,1)}, bf16[256,3072]{1,0:T(8,128)(2,1)}, bf16[256,3072]{1,0:T(8,128)(2,1)}, ...) custom-call(s32[1,2]{1,0:T(1,128)} %add_bitcast_fusion.flag, ...), custom_call_target="tpu_custom_call" | custom-call | flops 12000000000 | bytes 45000000 | tf_op jit(solution)/shard_map/layer_forward/pallas_call | solution.py:482
  252.8 13.9 %collective-permute-start.26 = (bf16[256,1536]{1,0:T(8,128)(2,1)}, bf16[256,1536]{1,0:T(8,128)(2,1)S(1)}, u32[]{:S(2)}, u32[]{:S(2)}) collective-permute-start(bf16[256,1536]{1,0:T(8,128)(2,1)} %get-tuple-element.234), channel_id=1, source_target_pairs={{0,16},{1,17},{2,18},{3,19},{4,20},{5,21},{6,22},{7,23},{8,24},{9,... | collective-permute-start | bytes 2359304 | tf_op jit(solution)/shard_map/ppermute | solution.py:865
  270.4 26.3 %layer_forward.8 = (bf16[256,1536]{1,0:T(8,128)(2,1)}, bf16[256,3072]{1,0:T(8,128)(2,1)}, bf16[256,3072]{1,0:T(8,128)(2,1)}, bf16[256,3072]{1,0:T(8,128)(2,1)}, ...) custom-call(s32[1,2]{1,0:T(1,128)} %add_bitcast_fusion.flag, ...), custom_call_target="tpu_custom_call" | custom-call | flops 12000000000 | bytes 45000000 | tf_op jit(solution)/shard_map/layer_forward/pallas_call | solution.py:482
  299.0 26.5 %layer_forward.9 = (bf16[256,1536]{1,0:T(8,128)(2,1)}, bf16[256,3072]{1,0:T(8,128)(2,1)}, bf16[256,3072]{1,0:T(8,128)(2,1)}, bf16[256,3072]{1,0:T(8,128)(2,1)}, ...) custom-call(s32[1,2]{1,0:T(1,128)} %add_bitcast_fusion.flag, ...), custom_call_target="tpu_custom_call" | custom-call | flops 12000000000 | bytes 45000000 | tf_op jit(solution)/shard_map/layer_forward/pallas_call | solution.py:482
  330.2 26.4 %layer_forward.10 = (bf16[256,1536]{1,0:T(8,128)(2,1)}, bf16[256,3072]{1,0:T(8,128)(2,1)}, bf16[256,3072]{1,0:T(8,128)(2,1)}, bf16[256,3072]{1,0:T(8,128)(2,1)},...) custom-call(s32[1,2]{1,0:T(1,128)} %add_bitcast_fusion.flag, ...), custom_call_target="tpu_custom_call" | custom-call | flops 12000000000 | bytes 45000000 | tf_op jit(solution)/shard_map/layer_forward/pallas_call | solution.py:482
  357.6 26.5 %layer_forward.11 = (bf16[256,1536]{1,0:T(8,128)(2,1)}, bf16[256,3072]{1,0:T(8,128)(2,1)}, bf16[256,3072]{1,0:T(8,128)(2,1)}, bf16[256,3072]{1,0:T(8,128)(2,1)},...) custom-call(s32[1,2]{1,0:T(1,128)} %add_bitcast_fusion.flag, ...), custom_call_target="tpu_custom_call" | custom-call | flops 12000000000 | bytes 45000000 | tf_op jit(solution)/shard_map/layer_forward/pallas_call | solution.py:482
  394.6 35.7 %layer_backward.6 = (bf16[256,1536]{1,0:T(8,128)(2,1)}, bf16[256,3072]{1,0:T(8,128)(2,1)}, bf16[256,3456]{1,0:T(8,128)(2,1)}, f32[256,1536]{1,0:T(8,128)}, bf16[...) custom-call(s32[1,2]{1,0:T(1,128)} %add_bitcast_fusion.2.flag, ...), custom_call_target="tpu_custom_call" | custom-call | flops 24999999488 | bytes 55000000 | tf_op jit(solution)/shard_map/layer_backward/pallas_call | solution.py:538
  436.8 35.7 %layer_backward.7 = (bf16[256,1536]{1,0:T(8,128)(2,1)}, bf16[256,3072]{1,0:T(8,128)(2,1)}, bf16[256,3456]{1,0:T(8,128)(2,1)}, f32[256,1536]{1,0:T(8,128)}, bf16[...) custom-call(s32[1,2]{1,0:T(1,128)} %add_bitcast_fusion.2.flag, ...), custom_call_target="tpu_custom_call" | custom-call | flops 24999999488 | bytes 55000000 | tf_op jit(solution)/shard_map/layer_backward/pallas_call | solution.py:538
  476.2 35.6 %layer_backward.8 = (bf16[256,1536]{1,0:T(8,128)(2,1)}, bf16[256,3072]{1,0:T(8,128)(2,1)}, bf16[256,3456]{1,0:T(8,128)(2,1)}, f32[256,1536]{1,0:T(8,128)}, bf16[...) custom-call(s32[1,2]{1,0:T(1,128)} %add_bitcast_fusion.2.flag, ...), custom_call_target="tpu_custom_call" | custom-call | flops 24999999488 | bytes 55000000 | tf_op jit(solution)/shard_map/layer_backward/pallas_call | solution.py:538
  514.5 35.5 %layer_backward.9 = (bf16[256,1536]{1,0:T(8,128)(2,1)}, bf16[256,3072]{1,0:T(8,128)(2,1)}, bf16[256,3456]{1,0:T(8,128)(2,1)}, f32[256,1536]{1,0:T(8,128)}, bf16[...) custom-call(s32[1,2]{1,0:T(1,128)} %add_bitcast_fusion.2.flag, ...), custom_call_target="tpu_custom_call" | custom-call | flops 24999999488 | bytes 55000000 | tf_op jit(solution)/shard_map/layer_backward/pallas_call | solution.py:538
  556.2 16.4 %collective-permute-done.37.other_grad = bf16[256,1536]{1,0:T(8,128)(2,1)S(1)} collective-permute-done((bf16[256,1536]{1,0:T(8,128)(2,1)S(1)}, bf16[256,1536]{1,0:T(8,128)(2,1)S(1)}, u32[]{:S(2)}, u32[]{:S(2)}) %collective-permute-start.37) | collective-permute-done | bytes 786464 | tf_op jit(solution)/shard_map/ppermute | solution.py:906
  573.9 35.7 %layer_backward.10 = (bf16[256,1536]{1,0:T(8,128)(2,1)}, bf16[256,3072]{1,0:T(8,128)(2,1)}, bf16[256,3456]{1,0:T(8,128)(2,1)}, f32[256,1536]{1,0:T(8,128)}, bf16...) custom-call(s32[1,2]{1,0:T(1,128)} %add_bitcast_fusion.1.flag, ...), custom_call_target="tpu_custom_call" | custom-call | flops 24999999488 | bytes 55000000 | tf_op jit(solution)/shard_map/layer_backward/pallas_call | solution.py:538
  613.4 14.3 %convolution_convert_fusion = bf16[3072,1536]{1,0:T(8,128)(2,1)} fusion(bf16[256,3072]{1,0:T(8,128)(2,1)} %get-tuple-element.487, bf16[256,3072]{1,0:T(8,128)(2,1)S(1)} %get-tuple-element.485, bf16[256,3072]{1,0:T(8,128)(2,1)S(1)} %copy-done.28, bf16[256,3072]{1,0:T(8,128)(2,1)S(1)} %get-tuple-element.484, bf16[256,1536]{1,0:T(8,128)(2,1)} %get-tuple-element.498, ...), kind=kOutput, calls=%fused_computation | convolution fusion | flops 9706143744 | bytes 18874368 | tf_op jit(solution)/shard_map/td,te->de/dot_general | solution.py:957
  627.8 36.2 %layer_backward.11 = (bf16[256,1536]{1,0:T(8,128)(2,1)}, bf16[256,3072]{1,0:T(8,128)(2,1)}, bf16[256,3456]{1,0:T(8,128)(2,1)}, f32[256,1536]{1,0:T(8,128)}, bf16...) custom-call(s32[1,2]{1,0:T(1,128)} %add_bitcast_fusion.1.flag, ...), custom_call_target="tpu_custom_call" | custom-call | flops 24999999488 | bytes 55000000 | tf_op jit(solution)/shard_map/layer_backward/pallas_call | solution.py:538
  704.1 16.3 %collective-permute-done.40 = bf16[256,1536]{1,0:T(8,128)(2,1)} collective-permute-done((bf16[256,1536]{1,0:T(8,128)(2,1)}, bf16[256,1536]{1,0:T(8,128)(2,1)}, u32[]{:S(2)}, u32[]{:S(2)}) %collective-permute-start.40) | collective-permute-done | bytes 786464 | tf_op jit(solution)/shard_map/ppermute | solution.py:733
  720.5 19.0 %collective-permute-done.39 = bf16[256,1536]{1,0:T(8,128)(2,1)} collective-permute-done((bf16[256,1536]{1,0:T(8,128)(2,1)}, bf16[256,1536]{1,0:T(8,128)(2,1)}, u32[]{:S(2)}, u32[]{:S(2)}) %collective-permute-start.39) | collective-permute-done | bytes 786464 | tf_op jit(solution)/shard_map/ppermute | solution.py:733
  797.0 14.8 %collective-permute-done.44 = bf16[48,3072]{1,0:T(8,128)(2,1)S(1)} collective-permute-done((bf16[48,3072]{1,0:T(8,128)(2,1)S(1)}, bf16[48,3072]{1,0:T(8,128)(2,1)S(1)}, u32[]{:S(2)}, u32[]{:S(2)}) %collective-permute-start.44) | collective-permute-done | bytes 294944 | tf_op jit(solution)/shard_map/ppermute | solution.py:615
  862.6 17.9 %collective-permute-start.54 = (f32[8,3328]{1,0:T(8,128)S(1)}, f32[8,3328]{1,0:T(8,128)S(1)}, u32[]{:S(2)}, u32[]{:S(2)}) collective-permute-start(f32[8,3328]{1,0:T(8,128)S(1)} %add.697), channel_id=1, source_target_pairs={{0,2},{1,3},{2,0},{3,1},{4,6},{5,7},{6,4},{7,5},{8,10},{9,11},{10,... | collective-permute-start | bytes 319496 | tf_op jit(solution)/shard_map/ppermute | solution.py:584
  883.3 16.7 %collective-permute-done.54 = f32[8,3328]{1,0:T(8,128)S(1)} collective-permute-done((f32[8,3328]{1,0:T(8,128)S(1)}, f32[8,3328]{1,0:T(8,128)S(1)}, u32[]{:S(2)}, u32[]{:S(2)}) %collective-permute-start.54) | collective-permute-done | bytes 106528 | tf_op jit(solution)/shard_map/ppermute | solution.py:584
  (441 shorter events, 324.7 us)
Async XLA Ops:
  7.2 179.4 %all-gather.2.cloned.1.call-start = ((), (), s32[]{:S(2)}) async-start(), calls=%async_computation.1 | async-start | bytes 21307392 | tf_op jit(solution)/shard_map/all_gather | solution.py:823
  9.8 802.5 %reduce-scatter.2.cloned.1.call-start = ((), (), s32[]{:S(2)}) async-start(), calls=%async_computation.2 | async-start | bytes 10027008 | tf_op jit(solution)/shard_map/reduce_scatter | solution.py:965
  9.8 79.5 %collective-permute-start.10 = (bf16[192,1536]{1,0:T(8,128)(2,1)S(1)}, bf16[192,1536]{1,0:T(8,128)(2,1)S(1)}, u32[]{:S(2)}, u32[]{:S(2)}) collective-permute-start(bf16[192,1536]{1,0:T(8,128)(2,1)S(1)} %bitcast.210), channel_id=1, source_target_pairs={{0,8},{4,12},{1,0},{5,4},{2,1},{6,5},{3,2},{7,6},{11,3},{15,7},{10... | collective-permute-start | bytes 1769480 | tf_op jit(solution)/shard_map/ppermute | solution.py:615
  12.9 76.5 %collective-permute-start.9 = (bf16[192,1536]{1,0:T(8,128)(2,1)S(1)}, bf16[192,1536]{1,0:T(8,128)(2,1)}, u32[]{:S(2)}, u32[]{:S(2)}) collective-permute-start(bf16[192,1536]{1,0:T(8,128)(2,1)S(1)} %bitcast.211), channel_id=1, source_target_pairs={{0,1},{4,5},{1,2},{5,6},{2,3},{6,7},{3,11},{7,15},{11,10},{15,14},... | collective-permute-start | bytes 1769480 | tf_op jit(solution)/shard_map/ppermute | solution.py:615
  13.0 78.4 %collective-permute-start.8 = (bf16[192,1536]{1,0:T(8,128)(2,1)S(1)}, bf16[192,1536]{1,0:T(8,128)(2,1)}, u32[]{:S(2)}, u32[]{:S(2)}) collective-permute-start(bf16[192,1536]{1,0:T(8,128)(2,1)S(1)} %bitcast.212), channel_id=1, source_target_pairs={{0,4},{4,0},{8,12},{12,8},{1,5},{5,1},{9,13},{13,9},{2,6},{6,2},{1... | collective-permute-start | bytes 1769480 | tf_op jit(solution)/shard_map/ppermute | solution.py:619
  17.4 35.0 %collective-permute-start = (bf16[128,1536]{1,0:T(8,128)(2,1)S(1)}, bf16[128,1536]{1,0:T(8,128)(2,1)S(1)}, u32[]{:S(2)}, u32[]{:S(2)}) collective-permute-start(bf16[128,1536]{1,0:T(8,128)(2,1)S(1)} %get-tuple-element.471), channel_id=1, source_target_pairs={{0,1},{1,2},{2,3},{3,0},{4,5},{5,6},{6,7},{7,4},{8,9},{9,10},{10,1... | collective-permute-start | bytes 1179656 | tf_op jit(solution)/shard_map/ppermute | solution.py:733
  52.4 35.5 %collective-permute-start.1 = (bf16[128,1536]{1,0:T(8,128)(2,1)}, bf16[128,1536]{1,0:T(8,128)(2,1)S(1)}, u32[]{:S(2)}, u32[]{:S(2)}) collective-permute-start(bf16[128,1536]{1,0:T(8,128)(2,1)} %get-tuple-element.473), channel_id=1, source_target_pairs={{0,2},{1,3},{2,0},{3,1},{4,6},{5,7},{6,4},{7,5},{8,10},{9,11},{10,... | collective-permute-start | bytes 1179656 | tf_op jit(solution)/shard_map/ppermute | solution.py:733
  216.6 52.9 %collective-permute-start.25 = (bf16[256,1536]{1,0:T(8,128)(2,1)}, bf16[256,1536]{1,0:T(8,128)(2,1)S(1)}, u32[]{:S(2)}, u32[]{:S(2)}) collective-permute-start(bf16[256,1536]{1,0:T(8,128)(2,1)} %get-tuple-element.226), channel_id=1, source_target_pairs={{0,16},{1,17},{2,18},{3,19},{4,20},{5,21},{6,22},{7,23},{8,24},{9,... | collective-permute-start | bytes 2359304 | tf_op jit(solution)/shard_map/ppermute | solution.py:865
  221.4 105.7 %collective-permute-start.34 = (bf16[256,1536]{1,0:T(8,128)(2,1)}, bf16[256,1536]{1,0:T(8,128)(2,1)S(1)}, u32[]{:S(2)}, u32[]{:S(2)}) collective-permute-start(bf16[256,1536]{1,0:T(8,128)(2,1)} %get-tuple-element.459), channel_id=1, source_target_pairs={{16,19},{17,16},{18,17},{19,18},{20,23},{21,20},{22,21},{23,22},{2... | collective-permute-start | bytes 2359304 | tf_op jit(solution)/shard_map/ppermute | solution.py:772
  222.1 105.0 %collective-permute-start.33 = (bf16[256,1536]{1,0:T(8,128)(2,1)}, bf16[256,1536]{1,0:T(8,128)(2,1)S(1)}, u32[]{:S(2)}, u32[]{:S(2)}) collective-permute-start(bf16[256,1536]{1,0:T(8,128)(2,1)} %get-tuple-element.460), channel_id=1, source_target_pairs={{16,18},{17,19},{18,16},{19,17},{20,22},{21,23},{22,20},{23,21},{2... | collective-permute-start | bytes 2359304 | tf_op jit(solution)/shard_map/ppermute | solution.py:772
  222.8 104.3 %collective-permute-start.32 = (bf16[256,1536]{1,0:T(8,128)(2,1)}, bf16[256,1536]{1,0:T(8,128)(2,1)S(1)}, u32[]{:S(2)}, u32[]{:S(2)}) collective-permute-start(bf16[256,1536]{1,0:T(8,128)(2,1)} %get-tuple-element.461), channel_id=1, source_target_pairs={{16,17},{17,18},{18,19},{19,16},{20,21},{21,22},{22,23},{23,20},{2... | collective-permute-start | bytes 2359304 | tf_op jit(solution)/shard_map/ppermute | solution.py:772
  252.8 45.3 %collective-permute-start.26 = (bf16[256,1536]{1,0:T(8,128)(2,1)}, bf16[256,1536]{1,0:T(8,128)(2,1)S(1)}, u32[]{:S(2)}, u32[]{:S(2)}) collective-permute-start(bf16[256,1536]{1,0:T(8,128)(2,1)} %get-tuple-element.234), channel_id=1, source_target_pairs={{0,16},{1,17},{2,18},{3,19},{4,20},{5,21},{6,22},{7,23},{8,24},{9,... | collective-permute-start | bytes 2359304 | tf_op jit(solution)/shard_map/ppermute | solution.py:865
  388.7 404.0 %collective-permute-start.31 = (bf16[256,1536]{1,0:T(8,128)(2,1)}, bf16[256,1536]{1,0:T(8,128)(2,1)}, u32[]{:S(2)}, u32[]{:S(2)}) collective-permute-start(bf16[256,1536]{1,0:T(8,128)(2,1)} %get-tuple-element.462), channel_id=1, source_target_pairs={{0,3},{1,0},{2,1},{3,2},{4,7},{5,4},{6,5},{7,6},{8,11},{9,8},{10,9... | collective-permute-start | bytes 2359304 | tf_op jit(solution)/shard_map/ppermute | solution.py:733
  392.6 120.2 %collective-permute-start.30 = (bf16[256,1536]{1,0:T(8,128)(2,1)}, bf16[256,1536]{1,0:T(8,128)(2,1)S(1)}, u32[]{:S(2)}, u32[]{:S(2)}) collective-permute-start(bf16[256,1536]{1,0:T(8,128)(2,1)} %get-tuple-element.463), channel_id=1, source_target_pairs={{0,2},{1,3},{2,0},{3,1},{4,6},{5,7},{6,4},{7,5},{8,10},{9,11},{10,... | collective-permute-start | bytes 2359304 | tf_op jit(solution)/shard_map/ppermute | solution.py:733
  392.6 119.2 %collective-permute-start.29 = (bf16[256,1536]{1,0:T(8,128)(2,1)}, bf16[256,1536]{1,0:T(8,128)(2,1)S(1)}, u32[]{:S(2)}, u32[]{:S(2)}) collective-permute-start(bf16[256,1536]{1,0:T(8,128)(2,1)} %get-tuple-element.464), channel_id=1, source_target_pairs={{0,1},{1,2},{2,3},{3,0},{4,5},{5,6},{6,7},{7,4},{8,9},{9,10},{10,1... | collective-permute-start | bytes 2359304 | tf_op jit(solution)/shard_map/ppermute | solution.py:733
  430.3 44.2 %collective-permute-start.35 = (bf16[256,1536]{1,0:T(8,128)(2,1)}, bf16[256,1536]{1,0:T(8,128)(2,1)}, u32[]{:S(2)}, u32[]{:S(2)}) collective-permute-start(bf16[256,1536]{1,0:T(8,128)(2,1)} %get-tuple-element.281), channel_id=1, source_target_pairs={{16,0},{17,1},{18,2},{19,3},{20,4},{21,5},{22,6},{23,7},{24,8},{25... | collective-permute-start | bytes 2359304 | tf_op jit(solution)/shard_map/ppermute | solution.py:906
  474.4 39.2 %collective-permute-start.36 = (bf16[256,1536]{1,0:T(8,128)(2,1)}, bf16[256,1536]{1,0:T(8,128)(2,1)S(1)}, u32[]{:S(2)}, u32[]{:S(2)}) collective-permute-start(bf16[256,1536]{1,0:T(8,128)(2,1)} %get-tuple-element.297), channel_id=1, source_target_pairs={{16,0},{17,1},{18,2},{19,3},{20,4},{21,5},{22,6},{23,7},{24,8},{25... | collective-permute-start | bytes 2359304 | tf_op jit(solution)/shard_map/ppermute | solution.py:906
  572.6 39.8 %collective-permute-start.38 = (bf16[256,1536]{1,0:T(8,128)(2,1)}, bf16[256,1536]{1,0:T(8,128)(2,1)S(1)}, u32[]{:S(2)}, u32[]{:S(2)}) collective-permute-start(bf16[256,1536]{1,0:T(8,128)(2,1)} %get-tuple-element.314), channel_id=1, source_target_pairs={{16,0},{17,1},{18,2},{19,3},{20,4},{21,5},{22,6},{23,7},{24,8},{25... | collective-permute-start | bytes 2359304 | tf_op jit(solution)/shard_map/ppermute | solution.py:906
  675.4 72.4 %collective-permute-start.55 = (bf16[8,96,3456]{2,1,0:T(8,128)(2,1)}, bf16[8,96,3456]{2,1,0:T(8,128)(2,1)S(1)}, u32[]{:S(2)}, u32[]{:S(2)}) collective-permute-start(bf16[8,96,3456]{2,1,0:T(8,128)(2,1)} %bitcast.217), channel_id=1, source_target_pairs={{0,4},{4,0},{8,12},{12,8},{1,5},{5,1},{9,13},{13,9},{2,6},{6,2},{1... | collective-permute-start | bytes 15925256 | tf_op jit(solution)/shard_map/ppermute | solution.py:619
  675.8 120.3 %collective-permute-start.45 = (f32[8,3328]{1,0:T(8,128)S(1)}, f32[8,3328]{1,0:T(8,128)}, u32[]{:S(2)}, u32[]{:S(2)}) collective-permute-start(f32[8,3328]{1,0:T(8,128)S(1)} %fusion.33), channel_id=1, source_target_pairs={{0,4},{4,0},{8,12},{12,8},{1,5},{5,1},{9,13},{13,9},{2,6},{6,2},{1... | collective-permute-start | bytes 319496 | tf_op jit(solution)/shard_map/ppermute | solution.py:584
  690.9 48.6 %collective-permute-start.39 = (bf16[256,1536]{1,0:T(8,128)(2,1)}, bf16[256,1536]{1,0:T(8,128)(2,1)}, u32[]{:S(2)}, u32[]{:S(2)}) collective-permute-start(bf16[256,1536]{1,0:T(8,128)(2,1)} %get-tuple-element.431), channel_id=1, source_target_pairs={{0,1},{1,2},{2,3},{3,0},{4,5},{5,6},{6,7},{7,4},{8,9},{9,10},{10,1... | collective-permute-start | bytes 2359304 | tf_op jit(solution)/shard_map/ppermute | solution.py:733
  720.4 53.1 %collective-permute-start.42 = (bf16[8,96,3072]{2,1,0:T(8,128)(2,1)}, bf16[8,96,3072]{2,1,0:T(8,128)(2,1)}, u32[]{:S(2)}, u32[]{:S(2)}) collective-permute-start(bf16[8,96,3072]{2,1,0:T(8,128)(2,1)} %bitcast.218), channel_id=1, source_target_pairs={{0,4},{4,0},{8,12},{12,8},{1,5},{5,1},{9,13},{13,9},{2,6},{6,2},{1... | collective-permute-start | bytes 14155784 | tf_op jit(solution)/shard_map/ppermute | solution.py:619
  848.1 55.9 %collective-permute-start.41 = (bf16[256,1536]{1,0:T(8,128)(2,1)S(1)}, bf16[256,1536]{1,0:T(8,128)(2,1)}, u32[]{:S(2)}, u32[]{:S(2)}) collective-permute-start(bf16[256,1536]{1,0:T(8,128)(2,1)S(1)} %copy-done.39), channel_id=1, source_target_pairs={{0,2},{1,3},{2,0},{3,1},{4,6},{5,7},{6,4},{7,5},{8,10},{9,11},{10,... | collective-permute-start | bytes 2359304 | tf_op jit(solution)/shard_map/ppermute | solution.py:733
  862.6 37.4 %collective-permute-start.54 = (f32[8,3328]{1,0:T(8,128)S(1)}, f32[8,3328]{1,0:T(8,128)S(1)}, u32[]{:S(2)}, u32[]{:S(2)}) collective-permute-start(f32[8,3328]{1,0:T(8,128)S(1)} %add.697), channel_id=1, source_target_pairs={{0,2},{1,3},{2,0},{3,1},{4,6},{5,7},{6,4},{7,5},{8,10},{9,11},{10,... | collective-permute-start | bytes 319496 | tf_op jit(solution)/shard_map/ppermute | solution.py:584
  (129 other events, 2038.9 us)
Sparse Core Ops, SparseCore 0:
  10.2 176.4 all-gather.1
  627.9 144.1 reduce-scatter.1

commit v4 on v3

--- a/solution.py
+++ b/solution.py
@@ -97,8 +97,9 @@
     step = pl.program_id(0)
     length = own_ref.shape[0]
     half = length // 2
-
-    @pl.when(step == 0)
+    valid = flag[0, 2] == 1
+
+    @pl.when(jnp.logical_and(step == 0, valid))
     def _():
         h = chosen(flag[0, 0], own_ref, other_ref)
         scale = lax.rsqrt(jnp.mean(h * h, axis=1, keepdims=True) + EPS)
@@ -130,7 +131,7 @@
         ssq_s[...] = jnp.zeros_like(ssq_s)
         branch_o[...] = jnp.zeros_like(branch_o)
 
-    @pl.when(step < GROUPS)
+    @pl.when(jnp.logical_and(step < GROUPS, valid))
     def _():
         normed = normed_o[...]
         gate = dot(normed, wg[...], NN)
@@ -197,7 +198,7 @@
         ssq_s[...] += jnp.sum(u * u, axis=1, keepdims=True)
         branch_o[...] += dot(gained.astype(bf16), wo[...], NN)
 
-    @pl.when(step == GROUPS)
+    @pl.when(jnp.logical_and(step == GROUPS, valid))
     def _():
         r = lax.rsqrt(ssq_s[...] * (1.0 / DI) + EPS)
         r_o[...] = r
@@ -223,8 +224,17 @@
     step = pl.program_id(0)
     length = own_ref.shape[0]
     half = length // 2
-
-    @pl.when(step == 0)
+    valid = flag[0, 2] == 1
+
+    def carried_in(ref):
+        return jnp.where(flag[0, 3] == 1, ref[...], 0.0)
+
+    @pl.when(jnp.logical_not(valid))
+    def _():
+        for ref in (chan_o, chan_bc_o, ngrad_o, head_o):
+            ref[...] = jnp.zeros_like(ref)
+
+    @pl.when(jnp.logical_and(step == 0, valid))
     def _():
         gout_ref[...] = chosen_grad(flag[0, 1], own_grad, other_grad).astype(bf16)
         tap_rows = taps_bc[...]
@@ -252,7 +262,7 @@
         rowdot = jnp.sum(branch[...] * gout_ref[...].astype(f32), axis=1, keepdims=True)
         q_s[...] = jnp.broadcast_to(rowdot * (1.0 / DI), q_s.shape) * r_ref[...] * r_ref[...]
 
-    @pl.when(step < GROUPS)
+    @pl.when(jnp.logical_and(step < GROUPS, valid))
     def _():
         grad_gated = dot(gout_ref[...], wo[...], NT)
         u = u_ref[...].astype(f32)
@@ -270,7 +280,7 @@
         x_dt = act * dt
         x_low, g_low = x_dt.astype(bf16), grad_ssm.astype(bf16)
         g_ec = (grad_ssm * ec).astype(bf16)
-        state, adj = state_in[...], adj_in[...]
+        state, adj = state_in[...], carried_in(adj_in)
         state_low, adj_low = state.astype(bf16), adj.astype(bf16)
         from_adj = w * dot(b_s[...], adj_low, NN)
         carried = ec * dot(c_s[...], state_low, NN)
@@ -357,7 +367,7 @@
         carry_s[...] += picked[2 * length :]
         grad_pre = (dt * mixed_grad + skip[...] * grad_ssm) * slope_ref[...].astype(f32)
         next_o[...] = grad_pre[0:8]
-        later = later_rows(grad_pre, next_in[...])
+        later = later_rows(grad_pre, carried_in(next_in))
         grad_conv = conv_sum(taps[...], later)
         grad_conv = grad_conv.astype(bf16)
         gc_o[:, pl.ds(pl.multiple_of(step * WIDTH, WIDTH), WIDTH)] = grad_conv
@@ -367,7 +377,7 @@
         chan_o[...] = jnp.concatenate(sums + [jnp.zeros_like(skip_grad)], axis=0)
         acc_s[...] += dot(grad_gate, wg[...], NT) + dot(grad_conv, wc[...], NT)
 
-    @pl.when(step == GROUPS)
+    @pl.when(jnp.logical_and(step == GROUPS, valid))
     def _():
         wt = wt_s[...].astype(bf16)
         grad_b = db_s[...] + dot(wt, c_s[...], NN)
@@ -375,7 +385,7 @@
         grad_pre = jnp.concatenate([grad_b, grad_c], axis=1) * dsilu_s[...]
         next_bc_o[...] = grad_pre[0:8]
         tap_rows = taps_bc[...]
-        later = later_rows(grad_pre, next_bc_in[...])
+        later = later_rows(grad_pre, carried_in(next_bc_in))
         grad_conv = conv_sum(tap_rows, later)
         conv_in = cin_bc[...].astype(f32)
         sums = [jnp.sum(conv_in * rows, axis=0, keepdims=True) for rows in later]
@@ -759,7 +769,7 @@
     return in_order(blocks)
 
 
-def cotangent_blocks(rows):
+def cotangent_blocks(rows, late):
     parts = rows.shape[0]
     size = lax.axis_size("seq")
     rank = lax.axis_index("seq") % parts
@@ -770,6 +780,7 @@
             (size + i, size + i - i % parts + (i % parts + shift) % parts) for i in range(size)
         ]
         arrived.append(lax.ppermute(piece, ("section", "seq"), route))
+    arrived, _ = lax.optimization_barrier((arrived, late))
     return in_order(arrived)
 
 
@@ -804,8 +815,10 @@
 SKEW = 2
 
 
-def flags(first, grad):
-    return jnp.stack([jnp.where(first, 1, 0), jnp.asarray(grad, jnp.int32)]).astype(jnp.int32)[None]
+def flags(first, grad, valid, carried=True):
+    values = [jnp.where(first, 1, 0), jnp.asarray(grad, jnp.int32)]
+    values += [jnp.where(flag, 1, 0) for flag in (valid, carried)]
+    return jnp.stack(values).astype(jnp.int32)[None]
 
 
 def shards(
@@ -857,7 +870,8 @@
             if tick == SKEW:
                 carry = tuple(jnp.where(first, now, at) for now, at in zip(carry, start))
             own, other = tokens_in[min(tick, parts - 1)], received[tick]
-            values = dict(zip(KEPT, fwd_call(flags(first, 0), own, other, params, weights, *carry)))
+            valid = jnp.where(first, tick < parts, tick >= SKEW)
+            values = dict(zip(KEPT, fwd_call(flags(first, 0, valid), own, other, params, weights, *carry)))
             values.update(own=own, other=other, state=carry[0], tail=carry[1], tail_bc=carry[2])
             carry = (values["state_out"], values["tail_out"], values["tail_bc_out"])
             kept.append(values)
@@ -871,12 +885,12 @@
         carry = tuple(jnp.where(first, zero, at) for zero, at in zip(zeros, start))
         grads, received = [None] * ticks, [jnp.zeros((length, D), bf16)] * SKEW
         for tick in range(ticks):
+            carried = jnp.logical_not(first) if tick == SKEW and hops == 1 else True
             if tick == SKEW and hops > 1:
                 carry = tuple(jnp.where(first, at, now) for now, at in zip(carry, start))
-            if tick == parts:
-                carry = tuple(jnp.where(first, now, zero) for now, zero in zip(carry, zeros))
             from_loss = loss_in[max(parts - 1 - tick, 0)]
             late = jnp.int32(2 if tick >= parts else 1)
+            valid = jnp.where(first, tick >= SKEW, tick < parts)
             if before_last is not None and tick == ticks - 1:
                 early = before_last(grads, received[tick])
                 from_loss, early = lax.optimization_barrier((from_loss, early))
@@ -889,7 +903,7 @@
                 zip(
                     names,
                     bwd_call(
-                        flags(first, jnp.where(first, 0, late)),
+                        flags(first, jnp.where(first, 0, late), valid, carried),
                         from_loss,
                         received[tick],
                         kept[at],
@@ -923,7 +937,7 @@
         start = lax.fori_loop(0, hops - 1, onward, start)
     kept = forward(start)
     cotangent, _ = lax.optimization_barrier((cotangent, kept[0]["r"]))
-    loss_in = cotangent_blocks(cotangent)
+    loss_in = cotangent_blocks(cotangent, kept[-1]["r"])
     activations = laid_out(
         *to_pieces(
             [jnp.where(first, kept[k]["out"], kept[k + SKEW]["out"]) for k in range(parts)], bf16

time: 935 us -> 891 us (0.953)
  Pallas kernels: 373 us -> 325 us
    pallas_call x6, Pallas kernels: 214 us -> 183 us  [bwd_call(): pl.pallas_call(bwd_body, grid=(GROUPS + 1,), in_specs=in_specs, out_specs...]
    pallas_call x6, Pallas kernels: 159 us -> 142 us  [fwd_call(): pl.pallas_call(fwd_body, grid=(GROUPS + 1,), in_specs=in_specs, out_specs...]
    ppermute x4, starting transfers between devices: 20.1 us -> 5.73 us  [forward(): received.append(lax.ppermute(values['out'], 'section', [(0, 1)]))]
  transfers between devices with their start and end apart: 66 -> 66, of which waited for: 27 -> 28; matrix products, arithmetic and copies ran while one was open for 15% -> 16% of each run, Pallas kernels for 35% -> 32%
where the time goes in v4:
time: 891 us; the launch traced here: 881 us
  Pallas kernels  325 us (36%)
  waiting for transfers between devices  263 us (30%)
  starting transfers between devices  91.8 us (10%)
  local copies, waits for them, and re-layouts  70.3 us (8%)
  other arithmetic  68.5 us (8%)
  matrix products  45.8 us (5%)
  between operations  15.9 us (2%)
    pallas_call x6, Pallas kernels, bwd_call(): pl.pallas_call(bwd_body, grid=(GROUPS + 1,), in_specs=in_specs, out_specs...  183 us
    pallas_call x6, Pallas kernels, fwd_call(): pl.pallas_call(fwd_body, grid=(GROUPS + 1,), in_specs=in_specs, out_specs...  142 us
    ppermute x24, waiting for transfers between devices, around(): return lax.ppermute(value, ('dp', 'seq'), ring_route(step))  99.5 us
    ppermute x9, waiting for transfers between devices, turn(): return lax.ppermute(value, 'seq', route)  70.5 us
    all_gather x1, waiting for transfers between devices, shards(): lax.all_gather(shard, ('dp', 'seq'), axis=0, tiled=True)  31.8 us
    dot_general x4, matrix products, term(): return jnp.einsum('td,te->de', columns, right, preferred_element_type=f32)  31.2 us
    ppermute x4, waiting for transfers between devices, exchange(): lax.ppermute(value, axis, xor_route(lax.axis_size(axis), bit))  29.4 us
    ppermute x24, starting transfers between devices, around(): return lax.ppermute(value, ('dp', 'seq'), ring_route(step))  26.5 us
  transfers between devices with their start and end apart: 66, of which 28 were waited for; matrix products, arithmetic and copies ran while one was open for 16% of the time, Pallas kernels for 32%

profile of v4, /device:TPU:0, one launch (start us, length us, event | category | flops | bytes accessed | tf_op | source)
XLA Modules:
  0.0 880.6 jit_solution(16918159286014237708)
XLA Ops:
  66.0 22.0 %collective-permute-done.1 = bf16[128,1536]{1,0:T(8,128)(2,1)S(1)} collective-permute-done((bf16[128,1536]{1,0:T(8,128)(2,1)}, bf16[128,1536]{1,0:T(8,128)(2,1)S(1)}, u32[]{:S(2)}, u32[]{:S(2)}) %collective-permute-start.1) | collective-permute-done | bytes 393248 | tf_op jit(solution)/shard_map/ppermute | solution.py:743
  95.5 14.4 %collective-permute-done.13 = bf16[192,1536]{1,0:T(8,128)(2,1)S(1)} collective-permute-done((bf16[192,1536]{1,0:T(8,128)(2,1)}, bf16[192,1536]{1,0:T(8,128)(2,1)S(1)}, u32[]{:S(2)}, u32[]{:S(2)}) %collective-permute-start.13) | collective-permute-done | bytes 589856 | tf_op jit(solution)/shard_map/ppermute | solution.py:625
  119.9 13.2 %collective-permute-done.17 = bf16[192,1536]{1,0:T(8,128)(2,1)S(1)} collective-permute-done((bf16[192,1536]{1,0:T(8,128)(2,1)S(1)}, bf16[192,1536]{1,0:T(8,128)(2,1)S(1)}, u32[]{:S(2)}, u32[]{:S(2)}) %collective-permute-start.17) | collective-permute-done | bytes 589856 | tf_op jit(solution)/shard_map/ppermute | solution.py:625
  154.8 31.8 %all-gather.2.cloned.1.call-done.wg.wc.wbc = bf16[1536,6528]{1,0:T(8,128)(2,1)} async-done(((bf16[96,6528]{1,0:T(8,128)(2,1)}), bf16[1536,6528]{1,0:T(8,128)(2,1)}) %all-gather.2.cloned.1.call-update) | async-done | bytes 20054032 | tf_op jit(solution)/shard_map/all_gather | solution.py:836
  190.2 26.5 %layer_forward.6 = (bf16[256,1536]{1,0:T(8,128)(2,1)}, bf16[256,3072]{1,0:T(8,128)(2,1)}, bf16[256,3072]{1,0:T(8,128)(2,1)}, bf16[256,3072]{1,0:T(8,128)(2,1)}, ...) custom-call(s32[1,4]{1,0:T(1,128)} %fusion.36.flag, ...), custom_call_target="tpu_custom_call" | custom-call | flops 12000000000 | bytes 45000000 | tf_op jit(solution)/shard_map/layer_forward/pallas_call | solution.py:492
  222.5 26.5 %layer_forward.7 = (bf16[256,1536]{1,0:T(8,128)(2,1)}, bf16[256,3072]{1,0:T(8,128)(2,1)}, bf16[256,3072]{1,0:T(8,128)(2,1)}, bf16[256,3072]{1,0:T(8,128)(2,1)}, ...) custom-call(s32[1,4]{1,0:T(1,128)} %fusion.36.flag, ...), custom_call_target="tpu_custom_call" | custom-call | flops 12000000000 | bytes 45000000 | tf_op jit(solution)/shard_map/layer_forward/pallas_call | solution.py:492
  257.1 26.6 %layer_forward.8 = (bf16[256,1536]{1,0:T(8,128)(2,1)}, bf16[256,3072]{1,0:T(8,128)(2,1)}, bf16[256,3072]{1,0:T(8,128)(2,1)}, bf16[256,3072]{1,0:T(8,128)(2,1)}, ...) custom-call(s32[1,4]{1,0:T(1,128)} %get-tuple-element.517.flag, ...), custom_call_target="tpu_custom_call" | custom-call | flops 12000000000 | bytes 45000000 | tf_op jit(solution)/shard_map/layer_forward/pallas_call | solution.py:492
  285.9 26.3 %layer_forward.9 = (bf16[256,1536]{1,0:T(8,128)(2,1)}, bf16[256,3072]{1,0:T(8,128)(2,1)}, bf16[256,3072]{1,0:T(8,128)(2,1)}, bf16[256,3072]{1,0:T(8,128)(2,1)}, ...) custom-call(s32[1,4]{1,0:T(1,128)} %get-tuple-element.517.flag, ...), custom_call_target="tpu_custom_call" | custom-call | flops 12000000000 | bytes 45000000 | tf_op jit(solution)/shard_map/layer_forward/pallas_call | solution.py:492
  314.7 17.7 %layer_forward.10 = (bf16[256,1536]{1,0:T(8,128)(2,1)}, bf16[256,3072]{1,0:T(8,128)(2,1)}, bf16[256,3072]{1,0:T(8,128)(2,1)}, bf16[256,3072]{1,0:T(8,128)(2,1)},...) custom-call(s32[1,4]{1,0:T(1,128)} %fusion.38.flag, ...), custom_call_target="tpu_custom_call" | custom-call | flops 12000000000 | bytes 45000000 | tf_op jit(solution)/shard_map/layer_forward/pallas_call | solution.py:492
  333.3 18.4 %layer_forward.11 = (bf16[256,1536]{1,0:T(8,128)(2,1)}, bf16[256,3072]{1,0:T(8,128)(2,1)}, bf16[256,3072]{1,0:T(8,128)(2,1)}, bf16[256,3072]{1,0:T(8,128)(2,1)},...) custom-call(s32[1,4]{1,0:T(1,128)} %fusion.38.flag, ...), custom_call_target="tpu_custom_call" | custom-call | flops 12000000000 | bytes 45000000 | tf_op jit(solution)/shard_map/layer_forward/pallas_call | solution.py:492
  357.9 19.7 %layer_backward.6 = (bf16[256,1536]{1,0:T(8,128)(2,1)}, bf16[256,3072]{1,0:T(8,128)(2,1)}, bf16[256,3456]{1,0:T(8,128)(2,1)}, f32[256,1536]{1,0:T(8,128)}, bf16[...) custom-call(s32[1,4]{1,0:T(1,128)} %fusion.41.flag, ...), custom_call_target="tpu_custom_call" | custom-call | flops 24999999488 | bytes 55000000 | tf_op jit(solution)/shard_map/layer_backward/pallas_call | solution.py:548
  399.7 19.5 %layer_backward.7 = (bf16[256,1536]{1,0:T(8,128)(2,1)}, bf16[256,3072]{1,0:T(8,128)(2,1)}, bf16[256,3456]{1,0:T(8,128)(2,1)}, f32[256,1536]{1,0:T(8,128)}, bf16[...) custom-call(s32[1,4]{1,0:T(1,128)} %fusion.41.flag, ...), custom_call_target="tpu_custom_call" | custom-call | flops 24999999488 | bytes 55000000 | tf_op jit(solution)/shard_map/layer_backward/pallas_call | solution.py:548
  425.5 35.7 %layer_backward.8 = (bf16[256,1536]{1,0:T(8,128)(2,1)}, bf16[256,3072]{1,0:T(8,128)(2,1)}, bf16[256,3456]{1,0:T(8,128)(2,1)}, f32[256,1536]{1,0:T(8,128)}, bf16[...) custom-call(s32[1,4]{1,0:T(1,128)} %add_bitcast_fusion.flag, ...), custom_call_target="tpu_custom_call" | custom-call | flops 24999999488 | bytes 55000000 | tf_op jit(solution)/shard_map/layer_backward/pallas_call | solution.py:548
  463.1 15.1 %collective-permute-done.36.other_grad = bf16[256,1536]{1,0:T(8,128)(2,1)S(1)} collective-permute-done((bf16[256,1536]{1,0:T(8,128)(2,1)}, bf16[256,1536]{1,0:T(8,128)(2,1)S(1)}, u32[]{:S(2)}, u32[]{:S(2)}) %collective-permute-start.36) | collective-permute-done | bytes 786464 | tf_op jit(solution)/shard_map/ppermute | solution.py:920
  479.5 36.2 %layer_backward.9 = (bf16[256,1536]{1,0:T(8,128)(2,1)}, bf16[256,3072]{1,0:T(8,128)(2,1)}, bf16[256,3456]{1,0:T(8,128)(2,1)}, f32[256,1536]{1,0:T(8,128)}, bf16[...) custom-call(s32[1,4]{1,0:T(1,128)} %get-tuple-element.518.flag, ...), custom_call_target="tpu_custom_call" | custom-call | flops 24999999488 | bytes 55000000 | tf_op jit(solution)/shard_map/layer_backward/pallas_call | solution.py:548
  519.2 36.1 %layer_backward.10 = (bf16[256,1536]{1,0:T(8,128)(2,1)}, bf16[256,3072]{1,0:T(8,128)(2,1)}, bf16[256,3456]{1,0:T(8,128)(2,1)}, f32[256,1536]{1,0:T(8,128)}, bf16...) custom-call(s32[1,4]{1,0:T(1,128)} %fusion.39.flag, ...), custom_call_target="tpu_custom_call" | custom-call | flops 24999999488 | bytes 55000000 | tf_op jit(solution)/shard_map/layer_backward/pallas_call | solution.py:548
  567.1 14.6 %convolution_convert_fusion = bf16[3072,1536]{1,0:T(8,128)(2,1)} fusion(bf16[256,3072]{1,0:T(8,128)(2,1)} %get-tuple-element.495, bf16[256,3072]{1,0:T(8,128)(2,1)S(1)} %copy-done.27, bf16[256,3072]{1,0:T(8,128)(2,1)} %get-tuple-element.494, bf16[256,3072]{1,0:T(8,128)(2,1)S(1)} %get-tuple-element.492, bf16[256,1536]{1,0:T(8,128)(2,1)} %get-tuple-element.506, ...), kind=kOutput, calls=%fused_computation | convolution fusion | flops 9706143744 | bytes 18874368 | tf_op jit(solution)/shard_map/td,te->de/dot_general | solution.py:971
  581.7 36.2 %layer_backward.11 = (bf16[256,1536]{1,0:T(8,128)(2,1)}, bf16[256,3072]{1,0:T(8,128)(2,1)}, bf16[256,3456]{1,0:T(8,128)(2,1)}, f32[256,1536]{1,0:T(8,128)}, bf16...) custom-call(s32[1,4]{1,0:T(1,128)} %fusion.39.flag, ...), custom_call_target="tpu_custom_call" | custom-call | flops 24999999488 | bytes 55000000 | tf_op jit(solution)/shard_map/layer_backward/pallas_call | solution.py:548
  652.8 19.5 %collective-permute-done.40 = bf16[256,1536]{1,0:T(8,128)(2,1)} collective-permute-done((bf16[256,1536]{1,0:T(8,128)(2,1)}, bf16[256,1536]{1,0:T(8,128)(2,1)}, u32[]{:S(2)}, u32[]{:S(2)}) %collective-permute-start.40) | collective-permute-done | bytes 786464 | tf_op jit(solution)/shard_map/ppermute | solution.py:743
  672.4 18.9 %collective-permute-done.39 = bf16[256,1536]{1,0:T(8,128)(2,1)} collective-permute-done((bf16[256,1536]{1,0:T(8,128)(2,1)}, bf16[256,1536]{1,0:T(8,128)(2,1)}, u32[]{:S(2)}, u32[]{:S(2)}) %collective-permute-start.39) | collective-permute-done | bytes 786464 | tf_op jit(solution)/shard_map/ppermute | solution.py:743
  713.0 13.6 %collective-permute-done.57 = bf16[48,3456]{1,0:T(8,128)(2,1)S(1)} collective-permute-done((bf16[48,3456]{1,0:T(8,128)(2,1)S(1)}, bf16[48,3456]{1,0:T(8,128)(2,1)S(1)}, u32[]{:S(2)}, u32[]{:S(2)}) %collective-permute-start.57) | collective-permute-done | bytes 331808 | tf_op jit(solution)/shard_map/ppermute | solution.py:625
  751.9 14.6 %collective-permute-done.44 = bf16[48,3072]{1,0:T(8,128)(2,1)S(1)} collective-permute-done((bf16[48,3072]{1,0:T(8,128)(2,1)S(1)}, bf16[48,3072]{1,0:T(8,128)(2,1)S(1)}, u32[]{:S(2)}, u32[]{:S(2)}) %collective-permute-start.44) | collective-permute-done | bytes 294944 | tf_op jit(solution)/shard_map/ppermute | solution.py:625
  818.1 17.8 %collective-permute-start.54 = (f32[8,3328]{1,0:T(8,128)S(1)}, f32[8,3328]{1,0:T(8,128)S(1)}, u32[]{:S(2)}, u32[]{:S(2)}) collective-permute-start(f32[8,3328]{1,0:T(8,128)S(1)} %add.697), channel_id=1, source_target_pairs={{0,2},{1,3},{2,0},{3,1},{4,6},{5,7},{6,4},{7,5},{8,10},{9,11},{10,... | collective-permute-start | bytes 319496 | tf_op jit(solution)/shard_map/ppermute | solution.py:594
  838.6 16.8 %collective-permute-done.54 = f32[8,3328]{1,0:T(8,128)S(1)} collective-permute-done((f32[8,3328]{1,0:T(8,128)S(1)}, f32[8,3328]{1,0:T(8,128)S(1)}, u32[]{:S(2)}, u32[]{:S(2)}) %collective-permute-start.54) | collective-permute-done | bytes 106528 | tf_op jit(solution)/shard_map/ppermute | solution.py:594
  (463 shorter events, 327.0 us)
Async XLA Ops:
  7.2 179.4 %all-gather.2.cloned.1.call-start = ((), (), s32[]{:S(2)}) async-start(), calls=%async_computation.1 | async-start | bytes 21307392 | tf_op jit(solution)/shard_map/all_gather | solution.py:836
  9.8 757.8 %reduce-scatter.2.cloned.1.call-start = ((), (), s32[]{:S(2)}) async-start(), calls=%async_computation.2 | async-start | bytes 10027008 | tf_op jit(solution)/shard_map/reduce_scatter | solution.py:979
  9.8 79.5 %collective-permute-start.10 = (bf16[192,1536]{1,0:T(8,128)(2,1)S(1)}, bf16[192,1536]{1,0:T(8,128)(2,1)S(1)}, u32[]{:S(2)}, u32[]{:S(2)}) collective-permute-start(bf16[192,1536]{1,0:T(8,128)(2,1)S(1)} %bitcast.221), channel_id=1, source_target_pairs={{0,8},{4,12},{1,0},{5,4},{2,1},{6,5},{3,2},{7,6},{11,3},{15,7},{10... | collective-permute-start | bytes 1769480 | tf_op jit(solution)/shard_map/ppermute | solution.py:625
  12.9 76.5 %collective-permute-start.9 = (bf16[192,1536]{1,0:T(8,128)(2,1)S(1)}, bf16[192,1536]{1,0:T(8,128)(2,1)}, u32[]{:S(2)}, u32[]{:S(2)}) collective-permute-start(bf16[192,1536]{1,0:T(8,128)(2,1)S(1)} %bitcast.222), channel_id=1, source_target_pairs={{0,1},{4,5},{1,2},{5,6},{2,3},{6,7},{3,11},{7,15},{11,10},{15,14},... | collective-permute-start | bytes 1769480 | tf_op jit(solution)/shard_map/ppermute | solution.py:625
  13.0 78.4 %collective-permute-start.8 = (bf16[192,1536]{1,0:T(8,128)(2,1)S(1)}, bf16[192,1536]{1,0:T(8,128)(2,1)}, u32[]{:S(2)}, u32[]{:S(2)}) collective-permute-start(bf16[192,1536]{1,0:T(8,128)(2,1)S(1)} %bitcast.223), channel_id=1, source_target_pairs={{0,4},{4,0},{8,12},{12,8},{1,5},{5,1},{9,13},{13,9},{2,6},{6,2},{1... | collective-permute-start | bytes 1769480 | tf_op jit(solution)/shard_map/ppermute | solution.py:629
  17.4 35.0 %collective-permute-start = (bf16[128,1536]{1,0:T(8,128)(2,1)S(1)}, bf16[128,1536]{1,0:T(8,128)(2,1)S(1)}, u32[]{:S(2)}, u32[]{:S(2)}) collective-permute-start(bf16[128,1536]{1,0:T(8,128)(2,1)S(1)} %get-tuple-element.479), channel_id=1, source_target_pairs={{0,1},{1,2},{2,3},{3,0},{4,5},{5,6},{6,7},{7,4},{8,9},{9,10},{10,1... | collective-permute-start | bytes 1179656 | tf_op jit(solution)/shard_map/ppermute | solution.py:743
  52.4 35.5 %collective-permute-start.1 = (bf16[128,1536]{1,0:T(8,128)(2,1)}, bf16[128,1536]{1,0:T(8,128)(2,1)S(1)}, u32[]{:S(2)}, u32[]{:S(2)}) collective-permute-start(bf16[128,1536]{1,0:T(8,128)(2,1)} %get-tuple-element.481), channel_id=1, source_target_pairs={{0,2},{1,3},{2,0},{3,1},{4,6},{5,7},{6,4},{7,5},{8,10},{9,11},{10,... | collective-permute-start | bytes 1179656 | tf_op jit(solution)/shard_map/ppermute | solution.py:743
  216.6 39.6 %collective-permute-start.25 = (bf16[256,1536]{1,0:T(8,128)(2,1)}, bf16[256,1536]{1,0:T(8,128)(2,1)S(1)}, u32[]{:S(2)}, u32[]{:S(2)}) collective-permute-start(bf16[256,1536]{1,0:T(8,128)(2,1)} %get-tuple-element.230), channel_id=1, source_target_pairs={{0,16},{1,17},{2,18},{3,19},{4,20},{5,21},{6,22},{7,23},{8,24},{9,... | collective-permute-start | bytes 2359304 | tf_op jit(solution)/shard_map/ppermute | solution.py:879
  219.5 134.0 %collective-permute-start.34 = (bf16[256,1536]{1,0:T(8,128)(2,1)}, bf16[256,1536]{1,0:T(8,128)(2,1)S(1)}, u32[]{:S(2)}, u32[]{:S(2)}) collective-permute-start(bf16[256,1536]{1,0:T(8,128)(2,1)} %get-tuple-element.466), channel_id=1, source_target_pairs={{16,19},{17,16},{18,17},{19,18},{20,23},{21,20},{22,21},{23,22},{2... | collective-permute-start | bytes 2359304 | tf_op jit(solution)/shard_map/ppermute | solution.py:782
  220.2 133.3 %collective-permute-start.33 = (bf16[256,1536]{1,0:T(8,128)(2,1)}, bf16[256,1536]{1,0:T(8,128)(2,1)S(1)}, u32[]{:S(2)}, u32[]{:S(2)}) collective-permute-start(bf16[256,1536]{1,0:T(8,128)(2,1)} %get-tuple-element.467), channel_id=1, source_target_pairs={{16,18},{17,19},{18,16},{19,17},{20,22},{21,23},{22,20},{23,21},{2... | collective-permute-start | bytes 2359304 | tf_op jit(solution)/shard_map/ppermute | solution.py:782
  220.9 132.6 %collective-permute-start.32 = (bf16[256,1536]{1,0:T(8,128)(2,1)}, bf16[256,1536]{1,0:T(8,128)(2,1)}, u32[]{:S(2)}, u32[]{:S(2)}) collective-permute-start(bf16[256,1536]{1,0:T(8,128)(2,1)} %get-tuple-element.468), channel_id=1, source_target_pairs={{16,17},{17,18},{18,19},{19,16},{20,21},{21,22},{22,23},{23,20},{2... | collective-permute-start | bytes 2359304 | tf_op jit(solution)/shard_map/ppermute | solution.py:782
  377.7 46.5 %collective-permute-start.35 = (bf16[256,1536]{1,0:T(8,128)(2,1)}, bf16[256,1536]{1,0:T(8,128)(2,1)}, u32[]{:S(2)}, u32[]{:S(2)}) collective-permute-start(bf16[256,1536]{1,0:T(8,128)(2,1)} %get-tuple-element.289), channel_id=1, source_target_pairs={{16,0},{17,1},{18,2},{19,3},{20,4},{21,5},{22,6},{23,7},{24,8},{25... | collective-permute-start | bytes 2359304 | tf_op jit(solution)/shard_map/ppermute | solution.py:920
  383.3 364.5 %collective-permute-start.31 = (bf16[256,1536]{1,0:T(8,128)(2,1)}, bf16[256,1536]{1,0:T(8,128)(2,1)}, u32[]{:S(2)}, u32[]{:S(2)}) collective-permute-start(bf16[256,1536]{1,0:T(8,128)(2,1)} %get-tuple-element.470), channel_id=1, source_target_pairs={{0,3},{1,0},{2,1},{3,2},{4,7},{5,4},{6,5},{7,6},{8,11},{9,8},{10,9... | collective-permute-start | bytes 2359304 | tf_op jit(solution)/shard_map/ppermute | solution.py:743
  383.3 78.9 %collective-permute-start.30 = (bf16[256,1536]{1,0:T(8,128)(2,1)}, bf16[256,1536]{1,0:T(8,128)(2,1)S(1)}, u32[]{:S(2)}, u32[]{:S(2)}) collective-permute-start(bf16[256,1536]{1,0:T(8,128)(2,1)} %get-tuple-element.471), channel_id=1, source_target_pairs={{0,2},{1,3},{2,0},{3,1},{4,6},{5,7},{6,4},{7,5},{8,10},{9,11},{10,... | collective-permute-start | bytes 2359304 | tf_op jit(solution)/shard_map/ppermute | solution.py:743
  393.2 68.0 %collective-permute-start.29 = (bf16[256,1536]{1,0:T(8,128)(2,1)}, bf16[256,1536]{1,0:T(8,128)(2,1)S(1)}, u32[]{:S(2)}, u32[]{:S(2)}) collective-permute-start(bf16[256,1536]{1,0:T(8,128)(2,1)} %get-tuple-element.472), channel_id=1, source_target_pairs={{0,1},{1,2},{2,3},{3,0},{4,5},{5,6},{6,7},{7,4},{8,9},{9,10},{10,1... | collective-permute-start | bytes 2359304 | tf_op jit(solution)/shard_map/ppermute | solution.py:743
  424.2 54.0 %collective-permute-start.36 = (bf16[256,1536]{1,0:T(8,128)(2,1)}, bf16[256,1536]{1,0:T(8,128)(2,1)S(1)}, u32[]{:S(2)}, u32[]{:S(2)}) collective-permute-start(bf16[256,1536]{1,0:T(8,128)(2,1)} %get-tuple-element.305), channel_id=1, source_target_pairs={{16,0},{17,1},{18,2},{19,3},{20,4},{21,5},{22,6},{23,7},{24,8},{25... | collective-permute-start | bytes 2359304 | tf_op jit(solution)/shard_map/ppermute | solution.py:920
  478.2 39.6 %collective-permute-start.37 = (bf16[256,1536]{1,0:T(8,128)(2,1)S(1)}, bf16[256,1536]{1,0:T(8,128)(2,1)S(1)}, u32[]{:S(2)}, u32[]{:S(2)}) collective-permute-start(bf16[256,1536]{1,0:T(8,128)(2,1)S(1)} %copy-done.92), channel_id=1, source_target_pairs={{16,0},{17,1},{18,2},{19,3},{20,4},{21,5},{22,6},{23,7},{24,8},{25... | collective-permute-start | bytes 2359304 | tf_op jit(solution)/shard_map/ppermute | solution.py:920
  517.9 46.4 %collective-permute-start.38 = (bf16[256,1536]{1,0:T(8,128)(2,1)}, bf16[256,1536]{1,0:T(8,128)(2,1)}, u32[]{:S(2)}, u32[]{:S(2)}) collective-permute-start(bf16[256,1536]{1,0:T(8,128)(2,1)} %get-tuple-element.322), channel_id=1, source_target_pairs={{16,0},{17,1},{18,2},{19,3},{20,4},{21,5},{22,6},{23,7},{24,8},{25... | collective-permute-start | bytes 2359304 | tf_op jit(solution)/shard_map/ppermute | solution.py:920
  629.2 70.5 %collective-permute-start.55 = (bf16[8,96,3456]{2,1,0:T(8,128)(2,1)}, bf16[8,96,3456]{2,1,0:T(8,128)(2,1)S(1)}, u32[]{:S(2)}, u32[]{:S(2)}) collective-permute-start(bf16[8,96,3456]{2,1,0:T(8,128)(2,1)} %bitcast.228), channel_id=1, source_target_pairs={{0,4},{4,0},{8,12},{12,8},{1,5},{5,1},{9,13},{13,9},{2,6},{6,2},{1... | collective-permute-start | bytes 15925256 | tf_op jit(solution)/shard_map/ppermute | solution.py:629
  629.6 121.4 %collective-permute-start.45 = (f32[8,3328]{1,0:T(8,128)S(1)}, f32[8,3328]{1,0:T(8,128)}, u32[]{:S(2)}, u32[]{:S(2)}) collective-permute-start(f32[8,3328]{1,0:T(8,128)S(1)} %fusion.33), channel_id=1, source_target_pairs={{0,4},{4,0},{8,12},{12,8},{1,5},{5,1},{9,13},{13,9},{2,6},{6,2},{1... | collective-permute-start | bytes 319496 | tf_op jit(solution)/shard_map/ppermute | solution.py:594
  639.8 51.5 %collective-permute-start.39 = (bf16[256,1536]{1,0:T(8,128)(2,1)}, bf16[256,1536]{1,0:T(8,128)(2,1)}, u32[]{:S(2)}, u32[]{:S(2)}) collective-permute-start(bf16[256,1536]{1,0:T(8,128)(2,1)} %get-tuple-element.439), channel_id=1, source_target_pairs={{0,1},{1,2},{2,3},{3,0},{4,5},{5,6},{6,7},{7,4},{8,9},{9,10},{10,1... | collective-permute-start | bytes 2359304 | tf_op jit(solution)/shard_map/ppermute | solution.py:743
  672.3 56.5 %collective-permute-start.42 = (bf16[8,96,3072]{2,1,0:T(8,128)(2,1)}, bf16[8,96,3072]{2,1,0:T(8,128)(2,1)}, u32[]{:S(2)}, u32[]{:S(2)}) collective-permute-start(bf16[8,96,3072]{2,1,0:T(8,128)(2,1)} %bitcast.229), channel_id=1, source_target_pairs={{0,4},{4,0},{8,12},{12,8},{1,5},{5,1},{9,13},{13,9},{2,6},{6,2},{1... | collective-permute-start | bytes 14155784 | tf_op jit(solution)/shard_map/ppermute | solution.py:629
  803.6 56.4 %collective-permute-start.41 = (bf16[256,1536]{1,0:T(8,128)(2,1)S(1)}, bf16[256,1536]{1,0:T(8,128)(2,1)}, u32[]{:S(2)}, u32[]{:S(2)}) collective-permute-start(bf16[256,1536]{1,0:T(8,128)(2,1)S(1)} %copy-done.60), channel_id=1, source_target_pairs={{0,2},{1,3},{2,0},{3,1},{4,6},{5,7},{6,4},{7,5},{8,10},{9,11},{10,... | collective-permute-start | bytes 2359304 | tf_op jit(solution)/shard_map/ppermute | solution.py:743
  818.1 37.3 %collective-permute-start.54 = (f32[8,3328]{1,0:T(8,128)S(1)}, f32[8,3328]{1,0:T(8,128)S(1)}, u32[]{:S(2)}, u32[]{:S(2)}) collective-permute-start(f32[8,3328]{1,0:T(8,128)S(1)} %add.697), channel_id=1, source_target_pairs={{0,2},{1,3},{2,0},{3,1},{4,6},{5,7},{6,4},{7,5},{8,10},{9,11},{10,... | collective-permute-start | bytes 319496 | tf_op jit(solution)/shard_map/ppermute | solution.py:594
  (138 other events, 1762.7 us)
Sparse Core Ops, SparseCore 0:
  10.2 176.4 all-gather.1
  581.8 149.5 reduce-scatter.1

commit v5 on v4

--- a/solution.py
+++ b/solution.py
@@ -801,8 +801,8 @@
 def laid_out(held, pieces):
     parts = len(pieces)
     rank = lax.axis_index("seq") % parts
-    for shift, piece in enumerate(pieces):
-        piece = piece.astype(held.dtype)
+    for shift in sorted(range(parts), key=lambda shift: 1 < shift < parts - 1):
+        piece = pieces[shift].astype(held.dtype)
         held = lax.dynamic_update_slice(held, piece[None], ((rank - shift) % parts, 0, 0))
     return held
 
@@ -999,7 +999,7 @@
         near,
     )
     pieces[1], pieces[-1] = near
-    pieces, grad_gate = lax.optimization_barrier((pieces, grad_gate))
+    pieces[2:-1], grad_gate = lax.optimization_barrier((pieces[2:-1], grad_gate))
     input_grads = laid_out(held, pieces)[None]
     grad_in_proj = jnp.concatenate([grad_gate, grad_conv[:, : DI + BC + HEADS]], axis=1)[None]
 

time: 891 us -> 883 us (level)
  transfers between devices with their start and end apart: 66 -> 66, of which waited for: 28 -> 29; matrix products, arithmetic and copies ran while one was open for 16% -> 15% of each run, Pallas kernels for 32% -> 32%
where the time goes in v5:
time: 883 us; the launch traced here: 874 us
  Pallas kernels  324 us (37%)
  waiting for transfers between devices  263 us (30%)
  starting transfers between devices  93.2 us (11%)
  local copies, waits for them, and re-layouts  66.7 us (8%)
  other arithmetic  65 us (7%)
  matrix products  46 us (5%)
  between operations  16.1 us (2%)
    pallas_call x6, Pallas kernels, bwd_call(): pl.pallas_call(bwd_body, grid=(GROUPS + 1,), in_specs=in_specs, out_specs...  183 us
    pallas_call x6, Pallas kernels, fwd_call(): pl.pallas_call(fwd_body, grid=(GROUPS + 1,), in_specs=in_specs, out_specs...  141 us
    ppermute x24, waiting for transfers between devices, around(): return lax.ppermute(value, ('dp', 'seq'), ring_route(step))  101 us
    ppermute x9, waiting for transfers between devices, turn(): return lax.ppermute(value, 'seq', route)  71 us
    all_gather x1, waiting for transfers between devices, shards(): lax.all_gather(shard, ('dp', 'seq'), axis=0, tiled=True)  31.8 us
    dot_general x4, matrix products, term(): return jnp.einsum('td,te->de', columns, right, preferred_element_type=f32)  31.4 us
    ppermute x4, waiting for transfers between devices, exchange(): lax.ppermute(value, axis, xor_route(lax.axis_size(axis), bit))  29.2 us
    ppermute x24, starting transfers between devices, around(): return lax.ppermute(value, ('dp', 'seq'), ring_route(step))  26.5 us
  transfers between devices with their start and end apart: 66, of which 29 were waited for; matrix products, arithmetic and copies ran while one was open for 15% of the time, Pallas kernels for 32%

profile of v5, /device:TPU:0, one launch (start us, length us, event | category | flops | bytes accessed | tf_op | source)
XLA Modules:
  0.0 873.5 jit_solution(5346167676848639641)
XLA Ops:
  66.0 22.0 %collective-permute-done.1 = bf16[128,1536]{1,0:T(8,128)(2,1)S(1)} collective-permute-done((bf16[128,1536]{1,0:T(8,128)(2,1)}, bf16[128,1536]{1,0:T(8,128)(2,1)S(1)}, u32[]{:S(2)}, u32[]{:S(2)}) %collective-permute-start.1) | collective-permute-done | bytes 393248 | tf_op jit(solution)/shard_map/ppermute | solution.py:743
  95.5 14.5 %collective-permute-done.13 = bf16[192,1536]{1,0:T(8,128)(2,1)S(1)} collective-permute-done((bf16[192,1536]{1,0:T(8,128)(2,1)}, bf16[192,1536]{1,0:T(8,128)(2,1)S(1)}, u32[]{:S(2)}, u32[]{:S(2)}) %collective-permute-start.13) | collective-permute-done | bytes 589856 | tf_op jit(solution)/shard_map/ppermute | solution.py:625
  119.9 13.2 %collective-permute-done.17 = bf16[192,1536]{1,0:T(8,128)(2,1)S(1)} collective-permute-done((bf16[192,1536]{1,0:T(8,128)(2,1)S(1)}, bf16[192,1536]{1,0:T(8,128)(2,1)S(1)}, u32[]{:S(2)}, u32[]{:S(2)}) %collective-permute-start.17) | collective-permute-done | bytes 589856 | tf_op jit(solution)/shard_map/ppermute | solution.py:625
  154.9 31.8 %all-gather.2.cloned.1.call-done.wg.wc.wbc = bf16[1536,6528]{1,0:T(8,128)(2,1)} async-done(((bf16[96,6528]{1,0:T(8,128)(2,1)}), bf16[1536,6528]{1,0:T(8,128)(2,1)}) %all-gather.2.cloned.1.call-update) | async-done | bytes 20054032 | tf_op jit(solution)/shard_map/all_gather | solution.py:836
  190.2 26.4 %layer_forward.6 = (bf16[256,1536]{1,0:T(8,128)(2,1)}, bf16[256,3072]{1,0:T(8,128)(2,1)}, bf16[256,3072]{1,0:T(8,128)(2,1)}, bf16[256,3072]{1,0:T(8,128)(2,1)}, ...) custom-call(s32[1,4]{1,0:T(1,128)} %fusion.36.flag, ...), custom_call_target="tpu_custom_call" | custom-call | flops 12000000000 | bytes 45000000 | tf_op jit(solution)/shard_map/layer_forward/pallas_call | solution.py:492
  221.6 26.3 %layer_forward.7 = (bf16[256,1536]{1,0:T(8,128)(2,1)}, bf16[256,3072]{1,0:T(8,128)(2,1)}, bf16[256,3072]{1,0:T(8,128)(2,1)}, bf16[256,3072]{1,0:T(8,128)(2,1)}, ...) custom-call(s32[1,4]{1,0:T(1,128)} %fusion.36.flag, ...), custom_call_target="tpu_custom_call" | custom-call | flops 12000000000 | bytes 45000000 | tf_op jit(solution)/shard_map/layer_forward/pallas_call | solution.py:492
  256.0 26.3 %layer_forward.8 = (bf16[256,1536]{1,0:T(8,128)(2,1)}, bf16[256,3072]{1,0:T(8,128)(2,1)}, bf16[256,3072]{1,0:T(8,128)(2,1)}, bf16[256,3072]{1,0:T(8,128)(2,1)}, ...) custom-call(s32[1,4]{1,0:T(1,128)} %get-tuple-element.511.flag, ...), custom_call_target="tpu_custom_call" | custom-call | flops 12000000000 | bytes 45000000 | tf_op jit(solution)/shard_map/layer_forward/pallas_call | solution.py:492
  284.6 26.2 %layer_forward.9 = (bf16[256,1536]{1,0:T(8,128)(2,1)}, bf16[256,3072]{1,0:T(8,128)(2,1)}, bf16[256,3072]{1,0:T(8,128)(2,1)}, bf16[256,3072]{1,0:T(8,128)(2,1)}, ...) custom-call(s32[1,4]{1,0:T(1,128)} %get-tuple-element.511.flag, ...), custom_call_target="tpu_custom_call" | custom-call | flops 12000000000 | bytes 45000000 | tf_op jit(solution)/shard_map/layer_forward/pallas_call | solution.py:492
  313.3 17.7 %layer_forward.10 = (bf16[256,1536]{1,0:T(8,128)(2,1)}, bf16[256,3072]{1,0:T(8,128)(2,1)}, bf16[256,3072]{1,0:T(8,128)(2,1)}, bf16[256,3072]{1,0:T(8,128)(2,1)},...) custom-call(s32[1,4]{1,0:T(1,128)} %fusion.38.flag, ...), custom_call_target="tpu_custom_call" | custom-call | flops 12000000000 | bytes 45000000 | tf_op jit(solution)/shard_map/layer_forward/pallas_call | solution.py:492
  331.9 18.3 %layer_forward.11 = (bf16[256,1536]{1,0:T(8,128)(2,1)}, bf16[256,3072]{1,0:T(8,128)(2,1)}, bf16[256,3072]{1,0:T(8,128)(2,1)}, bf16[256,3072]{1,0:T(8,128)(2,1)},...) custom-call(s32[1,4]{1,0:T(1,128)} %fusion.38.flag, ...), custom_call_target="tpu_custom_call" | custom-call | flops 12000000000 | bytes 45000000 | tf_op jit(solution)/shard_map/layer_forward/pallas_call | solution.py:492
  355.4 19.7 %layer_backward.6 = (bf16[256,1536]{1,0:T(8,128)(2,1)}, bf16[256,3072]{1,0:T(8,128)(2,1)}, bf16[256,3456]{1,0:T(8,128)(2,1)}, f32[256,1536]{1,0:T(8,128)}, bf16[...) custom-call(s32[1,4]{1,0:T(1,128)} %fusion.41.flag, ...), custom_call_target="tpu_custom_call" | custom-call | flops 24999999488 | bytes 55000000 | tf_op jit(solution)/shard_map/layer_backward/pallas_call | solution.py:548
  396.4 19.5 %layer_backward.7 = (bf16[256,1536]{1,0:T(8,128)(2,1)}, bf16[256,3072]{1,0:T(8,128)(2,1)}, bf16[256,3456]{1,0:T(8,128)(2,1)}, f32[256,1536]{1,0:T(8,128)}, bf16[...) custom-call(s32[1,4]{1,0:T(1,128)} %fusion.41.flag, ...), custom_call_target="tpu_custom_call" | custom-call | flops 24999999488 | bytes 55000000 | tf_op jit(solution)/shard_map/layer_backward/pallas_call | solution.py:548
  423.9 35.8 %layer_backward.8 = (bf16[256,1536]{1,0:T(8,128)(2,1)}, bf16[256,3072]{1,0:T(8,128)(2,1)}, bf16[256,3456]{1,0:T(8,128)(2,1)}, f32[256,1536]{1,0:T(8,128)}, bf16[...) custom-call(s32[1,4]{1,0:T(1,128)} %add_bitcast_fusion.flag, ...), custom_call_target="tpu_custom_call" | custom-call | flops 24999999488 | bytes 55000000 | tf_op jit(solution)/shard_map/layer_backward/pallas_call | solution.py:548
  475.4 35.9 %layer_backward.9 = (bf16[256,1536]{1,0:T(8,128)(2,1)}, bf16[256,3072]{1,0:T(8,128)(2,1)}, bf16[256,3456]{1,0:T(8,128)(2,1)}, f32[256,1536]{1,0:T(8,128)}, bf16[...) custom-call(s32[1,4]{1,0:T(1,128)} %get-tuple-element.512.flag, ...), custom_call_target="tpu_custom_call" | custom-call | flops 24999999488 | bytes 55000000 | tf_op jit(solution)/shard_map/layer_backward/pallas_call | solution.py:548
  516.1 36.0 %layer_backward.10 = (bf16[256,1536]{1,0:T(8,128)(2,1)}, bf16[256,3072]{1,0:T(8,128)(2,1)}, bf16[256,3456]{1,0:T(8,128)(2,1)}, f32[256,1536]{1,0:T(8,128)}, bf16...) custom-call(s32[1,4]{1,0:T(1,128)} %fusion.39.flag, ...), custom_call_target="tpu_custom_call" | custom-call | flops 24999999488 | bytes 55000000 | tf_op jit(solution)/shard_map/layer_backward/pallas_call | solution.py:548
  564.4 14.6 %convolution_convert_fusion = bf16[3072,1536]{1,0:T(8,128)(2,1)} fusion(bf16[256,3072]{1,0:T(8,128)(2,1)} %get-tuple-element.489, bf16[256,3072]{1,0:T(8,128)(2,1)S(1)} %copy-done.32, bf16[256,3072]{1,0:T(8,128)(2,1)S(1)} %copy-done.34, bf16[256,3072]{1,0:T(8,128)(2,1)S(1)} %copy-done.31, bf16[256,1536]{1,0:T(8,128)(2,1)} %get-tuple-element.500, ...), kind=kOutput, calls=%fused_computation | convolution fusion | flops 9706143744 | bytes 18874368 | tf_op jit(solution)/shard_map/td,te->de/dot_general | solution.py:971
  579.0 36.0 %layer_backward.11 = (bf16[256,1536]{1,0:T(8,128)(2,1)}, bf16[256,3072]{1,0:T(8,128)(2,1)}, bf16[256,3456]{1,0:T(8,128)(2,1)}, f32[256,1536]{1,0:T(8,128)}, bf16...) custom-call(s32[1,4]{1,0:T(1,128)} %fusion.39.flag, ...), custom_call_target="tpu_custom_call" | custom-call | flops 24999999488 | bytes 55000000 | tf_op jit(solution)/shard_map/layer_backward/pallas_call | solution.py:548
  652.1 19.9 %collective-permute-done.40 = bf16[256,1536]{1,0:T(8,128)(2,1)} collective-permute-done((bf16[256,1536]{1,0:T(8,128)(2,1)}, bf16[256,1536]{1,0:T(8,128)(2,1)}, u32[]{:S(2)}, u32[]{:S(2)}) %collective-permute-start.40) | collective-permute-done | bytes 786464 | tf_op jit(solution)/shard_map/ppermute | solution.py:743
  672.0 19.0 %collective-permute-done.39 = bf16[256,1536]{1,0:T(8,128)(2,1)} collective-permute-done((bf16[256,1536]{1,0:T(8,128)(2,1)}, bf16[256,1536]{1,0:T(8,128)(2,1)}, u32[]{:S(2)}, u32[]{:S(2)}) %collective-permute-start.39) | collective-permute-done | bytes 786464 | tf_op jit(solution)/shard_map/ppermute | solution.py:743
  712.7 15.4 %collective-permute-done.57 = bf16[48,3456]{1,0:T(8,128)(2,1)S(1)} collective-permute-done((bf16[48,3456]{1,0:T(8,128)(2,1)S(1)}, bf16[48,3456]{1,0:T(8,128)(2,1)S(1)}, u32[]{:S(2)}, u32[]{:S(2)}) %collective-permute-start.57) | collective-permute-done | bytes 331808 | tf_op jit(solution)/shard_map/ppermute | solution.py:625
  751.4 14.6 %collective-permute-done.44 = bf16[48,3072]{1,0:T(8,128)(2,1)S(1)} collective-permute-done((bf16[48,3072]{1,0:T(8,128)(2,1)S(1)}, bf16[48,3072]{1,0:T(8,128)(2,1)S(1)}, u32[]{:S(2)}, u32[]{:S(2)}) %collective-permute-start.44) | collective-permute-done | bytes 294944 | tf_op jit(solution)/shard_map/ppermute | solution.py:625
  806.1 12.6 %collective-permute-done.51 = f32[8,3328]{1,0:T(8,128)S(1)} collective-permute-done((f32[8,3328]{1,0:T(8,128)S(1)}, f32[8,3328]{1,0:T(8,128)S(1)}, u32[]{:S(2)}, u32[]{:S(2)}) %collective-permute-start.51) | collective-permute-done | bytes 106528 | tf_op jit(solution)/shard_map/ppermute | solution.py:594
  818.7 18.0 %collective-permute-start.54 = (f32[8,3328]{1,0:T(8,128)S(1)}, f32[8,3328]{1,0:T(8,128)S(1)}, u32[]{:S(2)}, u32[]{:S(2)}) collective-permute-start(f32[8,3328]{1,0:T(8,128)S(1)} %add.697), channel_id=1, source_target_pairs={{0,2},{1,3},{2,0},{3,1},{4,6},{5,7},{6,4},{7,5},{8,10},{9,11},{10,... | collective-permute-start | bytes 319496 | tf_op jit(solution)/shard_map/ppermute | solution.py:594
  839.5 16.6 %collective-permute-done.54 = f32[8,3328]{1,0:T(8,128)S(1)} collective-permute-done((f32[8,3328]{1,0:T(8,128)S(1)}, f32[8,3328]{1,0:T(8,128)S(1)}, u32[]{:S(2)}, u32[]{:S(2)}) %collective-permute-start.54) | collective-permute-done | bytes 106528 | tf_op jit(solution)/shard_map/ppermute | solution.py:594
  (474 shorter events, 321.2 us)
Async XLA Ops:
  7.2 179.4 %all-gather.2.cloned.1.call-start = ((), (), s32[]{:S(2)}) async-start(), calls=%async_computation.1 | async-start | bytes 21307392 | tf_op jit(solution)/shard_map/all_gather | solution.py:836
  9.8 758.3 %reduce-scatter.2.cloned.1.call-start = ((), (), s32[]{:S(2)}) async-start(), calls=%async_computation.2 | async-start | bytes 10027008 | tf_op jit(solution)/shard_map/reduce_scatter | solution.py:979
  9.8 79.5 %collective-permute-start.10 = (bf16[192,1536]{1,0:T(8,128)(2,1)S(1)}, bf16[192,1536]{1,0:T(8,128)(2,1)S(1)}, u32[]{:S(2)}, u32[]{:S(2)}) collective-permute-start(bf16[192,1536]{1,0:T(8,128)(2,1)S(1)} %bitcast.220), channel_id=1, source_target_pairs={{0,8},{4,12},{1,0},{5,4},{2,1},{6,5},{3,2},{7,6},{11,3},{15,7},{10... | collective-permute-start | bytes 1769480 | tf_op jit(solution)/shard_map/ppermute | solution.py:625
  12.9 76.5 %collective-permute-start.9 = (bf16[192,1536]{1,0:T(8,128)(2,1)S(1)}, bf16[192,1536]{1,0:T(8,128)(2,1)}, u32[]{:S(2)}, u32[]{:S(2)}) collective-permute-start(bf16[192,1536]{1,0:T(8,128)(2,1)S(1)} %bitcast.221), channel_id=1, source_target_pairs={{0,1},{4,5},{1,2},{5,6},{2,3},{6,7},{3,11},{7,15},{11,10},{15,14},... | collective-permute-start | bytes 1769480 | tf_op jit(solution)/shard_map/ppermute | solution.py:625
  13.0 78.4 %collective-permute-start.8 = (bf16[192,1536]{1,0:T(8,128)(2,1)S(1)}, bf16[192,1536]{1,0:T(8,128)(2,1)}, u32[]{:S(2)}, u32[]{:S(2)}) collective-permute-start(bf16[192,1536]{1,0:T(8,128)(2,1)S(1)} %bitcast.222), channel_id=1, source_target_pairs={{0,4},{4,0},{8,12},{12,8},{1,5},{5,1},{9,13},{13,9},{2,6},{6,2},{1... | collective-permute-start | bytes 1769480 | tf_op jit(solution)/shard_map/ppermute | solution.py:629
  17.4 35.0 %collective-permute-start = (bf16[128,1536]{1,0:T(8,128)(2,1)S(1)}, bf16[128,1536]{1,0:T(8,128)(2,1)S(1)}, u32[]{:S(2)}, u32[]{:S(2)}) collective-permute-start(bf16[128,1536]{1,0:T(8,128)(2,1)S(1)} %get-tuple-element.473), channel_id=1, source_target_pairs={{0,1},{1,2},{2,3},{3,0},{4,5},{5,6},{6,7},{7,4},{8,9},{9,10},{10,1... | collective-permute-start | bytes 1179656 | tf_op jit(solution)/shard_map/ppermute | solution.py:743
  52.4 35.5 %collective-permute-start.1 = (bf16[128,1536]{1,0:T(8,128)(2,1)}, bf16[128,1536]{1,0:T(8,128)(2,1)S(1)}, u32[]{:S(2)}, u32[]{:S(2)}) collective-permute-start(bf16[128,1536]{1,0:T(8,128)(2,1)} %get-tuple-element.475), channel_id=1, source_target_pairs={{0,2},{1,3},{2,0},{3,1},{4,6},{5,7},{6,4},{7,5},{8,10},{9,11},{10,... | collective-permute-start | bytes 1179656 | tf_op jit(solution)/shard_map/ppermute | solution.py:743
  216.6 38.5 %collective-permute-start.25 = (bf16[256,1536]{1,0:T(8,128)(2,1)}, bf16[256,1536]{1,0:T(8,128)(2,1)S(1)}, u32[]{:S(2)}, u32[]{:S(2)}) collective-permute-start(bf16[256,1536]{1,0:T(8,128)(2,1)} %get-tuple-element.227), channel_id=1, source_target_pairs={{0,16},{1,17},{2,18},{3,19},{4,20},{5,21},{6,22},{7,23},{8,24},{9,... | collective-permute-start | bytes 2359304 | tf_op jit(solution)/shard_map/ppermute | solution.py:879
  219.5 132.5 %collective-permute-start.34 = (bf16[256,1536]{1,0:T(8,128)(2,1)}, bf16[256,1536]{1,0:T(8,128)(2,1)S(1)}, u32[]{:S(2)}, u32[]{:S(2)}) collective-permute-start(bf16[256,1536]{1,0:T(8,128)(2,1)} %get-tuple-element.460), channel_id=1, source_target_pairs={{16,19},{17,16},{18,17},{19,18},{20,23},{21,20},{22,21},{23,22},{2... | collective-permute-start | bytes 2359304 | tf_op jit(solution)/shard_map/ppermute | solution.py:782
  220.2 131.8 %collective-permute-start.33 = (bf16[256,1536]{1,0:T(8,128)(2,1)}, bf16[256,1536]{1,0:T(8,128)(2,1)S(1)}, u32[]{:S(2)}, u32[]{:S(2)}) collective-permute-start(bf16[256,1536]{1,0:T(8,128)(2,1)} %get-tuple-element.461), channel_id=1, source_target_pairs={{16,18},{17,19},{18,16},{19,17},{20,22},{21,23},{22,20},{23,21},{2... | collective-permute-start | bytes 2359304 | tf_op jit(solution)/shard_map/ppermute | solution.py:782
  220.9 131.1 %collective-permute-start.32 = (bf16[256,1536]{1,0:T(8,128)(2,1)}, bf16[256,1536]{1,0:T(8,128)(2,1)S(1)}, u32[]{:S(2)}, u32[]{:S(2)}) collective-permute-start(bf16[256,1536]{1,0:T(8,128)(2,1)} %get-tuple-element.462), channel_id=1, source_target_pairs={{16,17},{17,18},{18,19},{19,16},{20,21},{21,22},{22,23},{23,20},{2... | collective-permute-start | bytes 2359304 | tf_op jit(solution)/shard_map/ppermute | solution.py:782
  375.2 47.5 %collective-permute-start.35 = (bf16[256,1536]{1,0:T(8,128)(2,1)}, bf16[256,1536]{1,0:T(8,128)(2,1)}, u32[]{:S(2)}, u32[]{:S(2)}) collective-permute-start(bf16[256,1536]{1,0:T(8,128)(2,1)} %get-tuple-element.286), channel_id=1, source_target_pairs={{16,0},{17,1},{18,2},{19,3},{20,4},{21,5},{22,6},{23,7},{24,8},{25... | collective-permute-start | bytes 2359304 | tf_op jit(solution)/shard_map/ppermute | solution.py:920
  378.6 83.6 %collective-permute-start.31 = (bf16[256,1536]{1,0:T(8,128)(2,1)}, bf16[256,1536]{1,0:T(8,128)(2,1)}, u32[]{:S(2)}, u32[]{:S(2)}) collective-permute-start(bf16[256,1536]{1,0:T(8,128)(2,1)} %get-tuple-element.464), channel_id=1, source_target_pairs={{0,2},{1,3},{2,0},{3,1},{4,6},{5,7},{6,4},{7,5},{8,10},{9,11},{10,... | collective-permute-start | bytes 2359304 | tf_op jit(solution)/shard_map/ppermute | solution.py:743
  382.6 78.4 %collective-permute-start.30 = (bf16[256,1536]{1,0:T(8,128)(2,1)}, bf16[256,1536]{1,0:T(8,128)(2,1)}, u32[]{:S(2)}, u32[]{:S(2)}) collective-permute-start(bf16[256,1536]{1,0:T(8,128)(2,1)} %get-tuple-element.465), channel_id=1, source_target_pairs={{0,3},{1,0},{2,1},{3,2},{4,7},{5,4},{6,5},{7,6},{8,11},{9,8},{10,9... | collective-permute-start | bytes 2359304 | tf_op jit(solution)/shard_map/ppermute | solution.py:743
  389.5 70.2 %collective-permute-start.29 = (bf16[256,1536]{1,0:T(8,128)(2,1)}, bf16[256,1536]{1,0:T(8,128)(2,1)}, u32[]{:S(2)}, u32[]{:S(2)}) collective-permute-start(bf16[256,1536]{1,0:T(8,128)(2,1)} %get-tuple-element.466), channel_id=1, source_target_pairs={{0,1},{1,2},{2,3},{3,0},{4,5},{5,6},{6,7},{7,4},{8,9},{9,10},{10,1... | collective-permute-start | bytes 2359304 | tf_op jit(solution)/shard_map/ppermute | solution.py:743
  422.6 51.4 %collective-permute-start.36 = (bf16[256,1536]{1,0:T(8,128)(2,1)}, bf16[256,1536]{1,0:T(8,128)(2,1)S(1)}, u32[]{:S(2)}, u32[]{:S(2)}) collective-permute-start(bf16[256,1536]{1,0:T(8,128)(2,1)} %get-tuple-element.302), channel_id=1, source_target_pairs={{16,0},{17,1},{18,2},{19,3},{20,4},{21,5},{22,6},{23,7},{24,8},{25... | collective-permute-start | bytes 2359304 | tf_op jit(solution)/shard_map/ppermute | solution.py:920
  474.0 40.7 %collective-permute-start.37 = (bf16[256,1536]{1,0:T(8,128)(2,1)S(1)}, bf16[256,1536]{1,0:T(8,128)(2,1)S(1)}, u32[]{:S(2)}, u32[]{:S(2)}) collective-permute-start(bf16[256,1536]{1,0:T(8,128)(2,1)S(1)} %copy-done.98), channel_id=1, source_target_pairs={{16,0},{17,1},{18,2},{19,3},{20,4},{21,5},{22,6},{23,7},{24,8},{25... | collective-permute-start | bytes 2359304 | tf_op jit(solution)/shard_map/ppermute | solution.py:920
  514.7 46.3 %collective-permute-start.38 = (bf16[256,1536]{1,0:T(8,128)(2,1)}, bf16[256,1536]{1,0:T(8,128)(2,1)}, u32[]{:S(2)}, u32[]{:S(2)}) collective-permute-start(bf16[256,1536]{1,0:T(8,128)(2,1)} %get-tuple-element.319), channel_id=1, source_target_pairs={{16,0},{17,1},{18,2},{19,3},{20,4},{21,5},{22,6},{23,7},{24,8},{25... | collective-permute-start | bytes 2359304 | tf_op jit(solution)/shard_map/ppermute | solution.py:920
  627.4 71.9 %collective-permute-start.55 = (bf16[8,96,3456]{2,1,0:T(8,128)(2,1)}, bf16[8,96,3456]{2,1,0:T(8,128)(2,1)S(1)}, u32[]{:S(2)}, u32[]{:S(2)}) collective-permute-start(bf16[8,96,3456]{2,1,0:T(8,128)(2,1)} %bitcast.227), channel_id=1, source_target_pairs={{0,4},{4,0},{8,12},{12,8},{1,5},{5,1},{9,13},{13,9},{2,6},{6,2},{1... | collective-permute-start | bytes 15925256 | tf_op jit(solution)/shard_map/ppermute | solution.py:629
  635.3 36.6 %collective-permute-start.40 = (bf16[256,1536]{1,0:T(8,128)(2,1)}, bf16[256,1536]{1,0:T(8,128)(2,1)}, u32[]{:S(2)}, u32[]{:S(2)}) collective-permute-start(bf16[256,1536]{1,0:T(8,128)(2,1)} %get-tuple-element.432), channel_id=1, source_target_pairs={{0,3},{1,0},{2,1},{3,2},{4,7},{5,4},{6,5},{7,6},{8,11},{9,8},{10,9... | collective-permute-start | bytes 2359304 | tf_op jit(solution)/shard_map/ppermute | solution.py:743
  638.9 52.1 %collective-permute-start.39 = (bf16[256,1536]{1,0:T(8,128)(2,1)}, bf16[256,1536]{1,0:T(8,128)(2,1)}, u32[]{:S(2)}, u32[]{:S(2)}) collective-permute-start(bf16[256,1536]{1,0:T(8,128)(2,1)} %get-tuple-element.433), channel_id=1, source_target_pairs={{0,1},{1,2},{2,3},{3,0},{4,5},{5,6},{6,7},{7,4},{8,9},{9,10},{10,1... | collective-permute-start | bytes 2359304 | tf_op jit(solution)/shard_map/ppermute | solution.py:743
  650.8 79.6 %collective-permute-start.42 = (bf16[8,96,3072]{2,1,0:T(8,128)(2,1)}, bf16[8,96,3072]{2,1,0:T(8,128)(2,1)}, u32[]{:S(2)}, u32[]{:S(2)}) collective-permute-start(bf16[8,96,3072]{2,1,0:T(8,128)(2,1)} %bitcast.228), channel_id=1, source_target_pairs={{0,4},{4,0},{8,12},{12,8},{1,5},{5,1},{9,13},{13,9},{2,6},{6,2},{1... | collective-permute-start | bytes 14155784 | tf_op jit(solution)/shard_map/ppermute | solution.py:629
  804.2 56.1 %collective-permute-start.41 = (bf16[256,1536]{1,0:T(8,128)(2,1)S(1)}, bf16[256,1536]{1,0:T(8,128)(2,1)S(1)}, u32[]{:S(2)}, u32[]{:S(2)}) collective-permute-start(bf16[256,1536]{1,0:T(8,128)(2,1)S(1)} %copy-done.66), channel_id=1, source_target_pairs={{0,2},{1,3},{2,0},{3,1},{4,6},{5,7},{6,4},{7,5},{8,10},{9,11},{10,... | collective-permute-start | bytes 2359304 | tf_op jit(solution)/shard_map/ppermute | solution.py:743
  818.7 37.4 %collective-permute-start.54 = (f32[8,3328]{1,0:T(8,128)S(1)}, f32[8,3328]{1,0:T(8,128)S(1)}, u32[]{:S(2)}, u32[]{:S(2)}) collective-permute-start(f32[8,3328]{1,0:T(8,128)S(1)} %add.697), channel_id=1, source_target_pairs={{0,2},{1,3},{2,0},{3,1},{4,6},{5,7},{6,4},{7,5},{8,10},{9,11},{10,... | collective-permute-start | bytes 319496 | tf_op jit(solution)/shard_map/ppermute | solution.py:594
  (144 other events, 1910.4 us)
Sparse Core Ops, SparseCore 0:
  10.2 176.4 all-gather.1
  579.1 151.6 reduce-scatter.1
